TPU v7x, 256 devices: a whole 4x4x8 slice. The times are simulated.
256 devices in a mesh: mesh: 2 (over core), vocab: 32 (over y, z), dp: 4 (over x).
Axes of the slice: x: 4, y: 4, z: 8, core: 2. Of those that a mesh axis runs over, the one named last changes fastest.
Arguments:
- teacher_hidden: bfloat16 [512, 5120], P(('vocab', 'dp')), may hold values from -1024 to 1024
- teacher_head: bfloat16 [5120, 81920], P(None, ('vocab', 'dp')), may hold values from -2 to 2
- student_hidden: bfloat16 [512, 3584], P(('vocab', 'dp')), may hold values from -1024 to 1024
- student_head: bfloat16 [3584, 640, 128], P(None, None, ('vocab', 'dp')), may hold values from -2 to 2
- tiles: int32 [512, 128], replicated, may hold values from 0 to 639, as said below
Outputs:
- hidden_grad: bfloat16 [512, 3584], P(('mesh', 'vocab', 'dp'))
Inputs may be any that keep to these rules, and one draw needn't show every extreme that they name: Each row names 128 distinct tiles, at most 2 of them among tiles k * 5 to (k + 1) * 5 - 1 for any k; in every draw some such block holds 2 tiles of every row, so that it holds 1024 named (row, tile) pairs.
All inputs are finite; a program needn't handle non-finite values.
Results may differ from a plain program's by a relative error of at most 0.0048.
Values may be sent and summed in bfloat16 or wider, within the bound.
No kernel may reach another device: no remote copies, remote signals or barrier semaphores. Data moves between devices by JAX's collectives and lax.ppermute only.
A program may use at most 128 MiB of HBM per device.

v0:
```python
import functools

import jax
import jax.numpy as jnp
import numpy as np
from jax import lax
from jax.experimental import pallas as pl
from jax.experimental.pallas import tpu as pltpu
from jax.sharding import PartitionSpec as P

loss_scale = 1024.0
NX, NY, NZ = 4, 4, 8
LINE = ("vocab", "dp")
WHOLE = ("mesh", "vocab", "dp")
HALF = NX * NY * NZ


def device(m, x, y, z):
    return m * HALF + (y * NZ + z) * NX + x


LINES_Z = [
    [device(m, x, y, z) for z in range(NZ)]
    for m in range(2)
    for x in range(NX)
    for y in range(NY)
]
LINES_X = [
    [[device(m, x, y, z) for x in range(NX)] for y in range(NY) for z in range(NZ)]
    for m in range(2)
]
LINES_Y = [
    [[device(m, x, y, z) for y in range(NY)] for x in range(NX) for z in range(NZ)]
    for m in range(2)
]
PLANES_YZ = [
    [device(0, x, y, z) for y in range(NY) for z in range(NZ)] for x in range(NX)
]
PLANES_XZ = [
    [device(1, x, y, z) for x in range(NX) for z in range(NZ)] for y in range(NY)
]


def exchange(value, groups):
    return lax.all_to_all(value, WHOLE, 0, 0, tiled=True, axis_index_groups=groups)


def spread(value, groups):
    count = len(groups[0])
    rows, width = value.shape
    copies = jnp.broadcast_to(value[None], (count, rows, width)).reshape(count * rows, width)
    return exchange(copies, groups)


def home(x, y, z):
    x1, x0 = x // 2, x % 2
    y1, y0 = y // 2, y % 2
    z2, z1, z0 = z // 4, (z // 2) % 2, z % 2
    return 2 * x0 + y1, 2 * y0 + z2, 4 * z1 + 2 * z0 + x1


def row_orders():
    orders = np.zeros((2, 2 * HALF, 2 * HALF), np.float32)
    for x in range(NX):
        for y in range(NY):
            for z in range(NZ):
                hx, hy, hz = home(x, y, z)
                for b in range(2):
                    orders[0, ((hx * NY + hy) * NZ + hz) * 2 + b, ((x * NY + y) * NZ + z) * 2 + b] = 1
                    orders[1, ((hy * NX + hx) * NZ + hz) * 2 + b, ((y * NX + x) * NZ + z) * 2 + b] = 1
    return orders


def last_hop():
    pairs = []
    for m in range(2):
        for x in range(NX):
            for y in range(NY):
                for z in range(NZ):
                    pairs.append(
                        (device(m, x, y, z), device(x % 2, 2 * (x // 2) + m, y, z))
                    )
    return pairs


def tile_words(tiles_t):
    count, rows = tiles_t.shape

    def kernel(tiles_ref, word_ref):
        block = lax.broadcasted_iota(jnp.int32, (count, rows), 0)

        def step(k, word):
            tile = tiles_ref[pl.ds(k, 1), :]
            own = (tile * 205) >> 10
            bit = 1 << (tile - 5 * own)
            return word + jnp.where(block == own, bit, 0)

        word_ref[...] = lax.fori_loop(0, count, step, jnp.zeros((count, rows), jnp.int32))

    return pl.pallas_call(
        kernel,
        out_shape=jax.ShapeDtypeStruct((count, rows), jnp.int32),
    )(tiles_t)


def logits_and_message(hidden, teacher_head, student_cols, own_word, per_shard):
    rows = hidden.shape[0]
    dt, cols = teacher_head.shape
    ds = student_cols.shape[0]
    depth = 512
    t_steps, s_steps = dt // depth, ds // depth
    lanes = cols // per_shard

    def kernel(word_ref, h_ref, t_ref, s_ref, msg_ref, logit_ref, t_acc, s_acc):
        k = pl.program_id(0)

        @pl.when(k == 0)
        def _():
            t_acc[...] = jnp.zeros_like(t_acc)
            s_acc[...] = jnp.zeros_like(s_acc)

        @pl.when(k < t_steps)
        def _():
            t_acc[...] += jnp.dot(h_ref[...], t_ref[...], preferred_element_type=jnp.float32)

        @pl.when(k >= t_steps)
        def _():
            s_acc[...] += jnp.dot(h_ref[...], s_ref[...], preferred_element_type=jnp.float32)

        @pl.when(k == t_steps + s_steps - 1)
        def _():
            word = word_ref[...]
            t_log = t_acc[...].T
            s_log = s_acc[...].T
            logit_ref[...] = s_log
            t_top = jnp.max(t_log, axis=0, keepdims=True)
            named_before = jnp.zeros((1, rows), jnp.int32)
            t_total = jnp.zeros((1, rows), jnp.float32)
            t_rest = jnp.zeros((1, rows), jnp.float32)
            first = jnp.zeros((lanes, rows), jnp.float32)
            second = jnp.zeros((lanes, rows), jnp.float32)
            for t in range(per_shard):
                e = jnp.exp(t_log[t * lanes : (t + 1) * lanes] - t_top)
                part = jnp.sum(e, axis=0, keepdims=True)
                named = (word >> t) & 1
                t_total += part
                t_rest += jnp.where(named == 0, part, 0.0)
                first = jnp.where((named == 1) & (named_before == 0), e, first)
                second = jnp.where((named == 1) & (named_before == 1), e, second)
                named_before += named
            s_top = jnp.max(s_log, axis=0, keepdims=True)
            place = lax.broadcasted_iota(jnp.int32, (8, rows), 0)
            stats = jnp.where(place == 2, t_top, 0.0)
            stats = jnp.where(place == 3, t_total, stats)
            stats = jnp.where(place == 4, t_rest, stats)
            stats = jnp.where(place == 5, s_top, stats)
            msg_ref[...] = jnp.where(
                (place == 0)[None],
                first[:, None, :],
                jnp.where((place == 1)[None], second[:, None, :], stats[None]),
            )

    return pl.pallas_call(
        kernel,
        grid=(t_steps + s_steps,),
        in_specs=[
            pl.BlockSpec((1, rows), lambda k: (0, 0)),
            pl.BlockSpec((rows, depth), lambda k: (0, k)),
            pl.BlockSpec((depth, cols), lambda k: (jnp.minimum(k, t_steps - 1), 0)),
            pl.BlockSpec((depth, cols), lambda k: (jnp.maximum(k - t_steps, 0), 0)),
        ],
        out_specs=[
            pl.BlockSpec((lanes, 8, rows), lambda k: (0, 0, 0)),
            pl.BlockSpec((cols, rows), lambda k: (0, 0)),
        ],
        out_shape=[
            jax.ShapeDtypeStruct((lanes, 8, rows), jnp.float32),
            jax.ShapeDtypeStruct((cols, rows), jnp.float32),
        ],
        scratch_shapes=[
            pltpu.VMEM((rows, cols), jnp.float32),
            pltpu.VMEM((rows, cols), jnp.float32),
        ],
        compiler_params=pltpu.CompilerParams(vmem_limit_bytes=40 * 1024 * 1024),
    )(own_word, hidden, teacher_head, student_cols)


def expand_words(words, per_shard):
    shards = words.shape[0]
    tile = lax.broadcasted_iota(jnp.int32, (shards * per_shard, 1), 0)
    within = tile - per_shard * ((tile * 205) >> 10)
    wide = spread_blocks(words.astype(jnp.bfloat16), per_shard).astype(jnp.int32)
    named = (wide >> within) & 1
    before = wide & ((1 << within) - 1)
    return named == 1, before == 0


def spread_blocks(value, per_shard):
    shards = value.shape[0]
    tile = lax.broadcasted_iota(jnp.int32, (shards * per_shard, shards), 0)
    start = per_shard * lax.broadcasted_iota(jnp.int32, (shards * per_shard, shards), 1)
    chosen = ((tile >= start) & (tile < start + per_shard)).astype(jnp.float32).astype(jnp.bfloat16)
    return jnp.dot(chosen, value, preferred_element_type=jnp.float32)


def student_sums(words, logit, message, per_shard):
    cols, rows = logit.shape

    def kernel(word_ref, logit_ref, msg_ref, out_ref):
        named, _ = expand_words(word_ref[...], per_shard)
        top = jnp.max(logit_ref[...], axis=0, keepdims=True)
        e = jnp.exp(logit_ref[...] - top)
        total = jnp.sum(e, axis=0, keepdims=True)
        rest = jnp.sum(jnp.where(named, 0.0, e), axis=0, keepdims=True)
        place = lax.broadcasted_iota(jnp.int32, (8, rows), 0)
        stats = jnp.where(place == 6, total, jnp.where(place == 7, rest, 0.0))
        out_ref[...] = jnp.where((place >= 6)[None], stats[None], msg_ref[...])

    return pl.pallas_call(
        kernel,
        out_shape=jax.ShapeDtypeStruct(message.shape, jnp.float32),
        compiler_params=pltpu.CompilerParams(vmem_limit_bytes=40 * 1024 * 1024),
    )(words, logit, message)


def gradient(words, logit, arrived, order, student_cols, per_shard):
    cols, rows = logit.shape
    ds = student_cols.shape[0]
    width = 512

    def kernel(word_ref, logit_ref, msg_ref, order_ref, w_ref, out_ref, kl_ref):
        @pl.when(pl.program_id(0) == 0)
        def _():
            def sums(at):
                top_each = msg_ref[:, at, :]
                top = jnp.max(top_each, axis=0, keepdims=True)
                weight = jnp.exp(top_each - top)
                total = jnp.sum(weight * msg_ref[:, at + 1, :], axis=0, keepdims=True)
                rest = jnp.sum(weight * msg_ref[:, at + 2, :], axis=0, keepdims=True)
                return top, weight, total, rest / total

            _, t_weight, t_total, t_mass = sums(2)
            s_top, _, s_total, s_mass = sums(5)
            scale = t_weight / t_total
            first = (msg_ref[:, 0, :] * scale).astype(jnp.bfloat16)
            second = (msg_ref[:, 1, :] * scale).astype(jnp.bfloat16)
            named, is_first = expand_words(word_ref[...], per_shard)
            teacher = jnp.where(
                is_first, spread_blocks(first, per_shard), spread_blocks(second, per_shard)
            )
            prob = jnp.exp(logit_ref[...] - s_top) / s_total
            kl = (
                jnp.where(named, prob - teacher, prob * (1.0 - t_mass / s_mass)) * loss_scale
            ).astype(jnp.bfloat16)
            kl_ref[...] = lax.dot_general(
                order_ref[...], kl, (((1,), (1,)), ((), ())), preferred_element_type=jnp.float32
            ).astype(jnp.bfloat16)

        out_ref[...] = lax.dot_general(
            kl_ref[...], w_ref[...], (((1,), (1,)), ((), ())), preferred_element_type=jnp.float32
        ).astype(jnp.bfloat16)

    return pl.pallas_call(
        kernel,
        grid=(ds // width,),
        in_specs=[
            pl.BlockSpec(words.shape, lambda k: (0, 0)),
            pl.BlockSpec((cols, rows), lambda k: (0, 0)),
            pl.BlockSpec(arrived.shape, lambda k: (0, 0, 0)),
            pl.BlockSpec((rows, rows), lambda k: (0, 0)),
            pl.BlockSpec((width, cols), lambda k: (k, 0)),
        ],
        out_specs=pl.BlockSpec((rows, width), lambda k: (0, k)),
        out_shape=jax.ShapeDtypeStruct((rows, ds), jnp.bfloat16),
        scratch_shapes=[pltpu.VMEM((rows, cols), jnp.bfloat16)],
        compiler_params=pltpu.CompilerParams(vmem_limit_bytes=40 * 1024 * 1024),
    )(words, logit, arrived, order, student_cols)


def per_device(teacher_hidden, teacher_head, student_hidden, student_head, tiles):
    shards = lax.axis_size(LINE)
    shard_index = lax.axis_index(LINE)
    core = lax.axis_index("mesh")
    ds, tiles_all, lane_count = student_head.shape
    student_cols = student_head.reshape(ds, tiles_all * lane_count)
    per_shard = tiles_all // shards
    picks = tiles.shape[1]

    both = jnp.concatenate((teacher_hidden, student_hidden), axis=1)
    mine = lax.dynamic_slice_in_dim(both, 2 * core, 2, 0)
    gathered = spread(mine, LINES_Z)
    gathered = spread(gathered, LINES_Y[0] + LINES_X[1])
    gathered = spread(gathered, LINES_X[0] + LINES_Y[1])

    by_chip = tiles.reshape(NY, NZ, NX, 2, 2, picks)
    by_chip = lax.dynamic_index_in_dim(by_chip, core, 3, keepdims=False)
    tiles_t = jnp.where(
        core == 0, by_chip.transpose(4, 2, 0, 1, 3), by_chip.transpose(4, 0, 2, 1, 3)
    ).reshape(picks, 2 * shards)
    words = tile_words(tiles_t)
    own_word = lax.dynamic_slice_in_dim(words, shard_index, 1, 0)

    message, logit = logits_and_message(
        gathered, teacher_head, student_cols, own_word, per_shard
    )
    message = student_sums(words, logit, message, per_shard)
    arrived = lax.all_to_all(message, LINE, 0, 0, tiled=True)

    order = lax.dynamic_index_in_dim(
        jnp.asarray(row_orders(), jnp.bfloat16), core, 0, keepdims=False
    )
    partial = gradient(words, logit, arrived, order, student_cols, per_shard)

    rows = partial.shape[0]
    near = exchange(partial, LINES_X[0] + LINES_Y[1])
    near = jnp.sum(near.reshape(NX, rows // NX, ds).astype(jnp.float32), axis=0)
    far = exchange(near.astype(jnp.bfloat16), PLANES_YZ + PLANES_XZ)
    summed = jnp.sum(far.reshape(NY * NZ, 2, ds).astype(jnp.float32), axis=0)
    return lax.ppermute(summed.astype(jnp.bfloat16), WHOLE, last_hop())


def solution(mesh):
    return jax.shard_map(
        per_device,
        mesh=mesh,
        in_specs=(
            P(("vocab", "dp"), None),
            P(None, ("vocab", "dp")),
            P(("vocab", "dp"), None),
            P(None, None, ("vocab", "dp")),
            P(),
        ),
        out_specs=P(("mesh", "vocab", "dp"), None),
        check_vma=False,
    )
```

profile of v0, /device:TPU:1, one launch (start us, length us, event | category | flops | bytes accessed | tf_op | source)
XLA Modules:
  0.0 171.1 jit_solution(4847679533855536110)
XLA Ops:
  0.0 0.9 fusion
  1.0 19.4 %all_to_all.43 = bf16[8,2,8704]{2,1,0:T(2,128)(2,1)S(1)} all-to-all(bf16[8,2,8704]{2,1,0:T(2,128)(2,1)S(1)} %broadcast_in_dim.10), channel_id=1, replica_groups={{0,4,8,12,16,20,24,28},{32,36,40,44,48,52,56,60},{64,68,72,76,80,84,88,..., dimensions={0} | all-to-all | bytes 557056 | tf_op jit(solution)/shard_map/all_to_all | solution.py:45
  20.6 14.2 %all_to_all.44 = bf16[4,16,8704]{2,1,0:T(8,128)(2,1)S(1)} all-to-all(bf16[4,16,8704]{2,1,0:T(8,128)(2,1)S(1)} %broadcast_in_dim.24), channel_id=1, replica_groups={{0,32,64,96},{4,36,68,100},{8,40,72,104},{12,44,76,108},{16,48,80,112},..., dimensions={0} | all-to-all | bytes 2228224 | tf_op jit(solution)/shard_map/all_to_all | solution.py:45
  34.8 2.5 %broadcast_in_dim.26 = bf16[4,64,8704]{2,1,0:T(8,128)(2,1)} broadcast(bf16[64,8704]{1,0:T(8,128)(2,1)S(1)} %bitcast.20), dimensions={1,2} | broadcast | bytes 5570560 | tf_op jit(solution)/shard_map/broadcast_in_dim | solution.py:51
  37.3 4.9 %all-to-all-start.2 = ((bf16[4,64,8704]{2,1,0:T(8,128)(2,1)}), bf16[4,64,8704]{2,1,0:T(8,128)(2,1)}, u32[]{:S(2)}, u32[]{:S(2)}) async-start(bf16[4,64,8704]{2,1,0:T(8,128)(2,1)} %broadcast_in_dim.26), calls=%async_computation.2 | async-start | bytes 8912896 | tf_op jit(solution)/shard_map/all_to_all | solution.py:45
  42.3 0.8 copy.17.tiles_ref
  43.0 6.3 %shard_map.64.word_ref = s32[128,256]{1,0:T(8,128)} custom-call(s32[128,256]{1,0:T(8,128)} %copy.17.tiles_ref), custom_call_target="tpu_custom_call" | custom-call | tf_op jit(solution)/shard_map/pallas_call | solution.py:100
  49.4 0.7 constant_dynamic-slice_fusion.word_ref
  50.1 20.5 %all-to-all-done.2 = bf16[4,64,8704]{2,1,0:T(8,128)(2,1)} async-done(((bf16[4,64,8704]{2,1,0:T(8,128)(2,1)}), bf16[4,64,8704]{2,1,0:T(8,128)(2,1)}, u32[]{:S(2)}, u32[]{:S(2)}) %all-to-all-start.2) | async-done | bytes 4456480 | tf_op jit(solution)/shard_map/all_to_all | solution.py:45
  70.5 2.3 %copy-done.1 = bf16[3584,640,1]{1,0,2:T(8,128)(2,1)S(1)} copy-done((bf16[3584,640,1]{1,0,2:T(8,128)(2,1)S(1)}, bf16[3584,640,1]{1,0,2:T(8,128)(2,1)}, u32[]{:S(2)}) %copy-start.1) | copy-done | bytes 4587544
  72.8 14.1 %shard_map.65 = (f32[128,8,256]{2,1,0:T(8,128)S(1)}, f32[640,256]{1,0:T(8,128)S(1)}) custom-call(s32[1,256]{1,0:T(1,128)S(1)} %constant_dynamic-slice_fusion.word_ref, bf16[256,8704]{1,0:T(8,128)(2,1)} %bitcast.7.h_ref, bf16[5120,640]{1,0:T(8,128)(2,1)} %t_ref.1, bf16[3584,640]{1,0:T(8,128)(2,1)S(1)} %bitcast.17), custom_call_target="tpu_custom_call" | custom-call | tf_op jit(solution)/shard_map/pallas_call | solution.py:163
  87.0 1.5 shard_map.66
  88.5 6.2 %all-to-all-start.3 = ((f32[128,8,256]{2,1,0:T(8,128)}), f32[128,8,256]{2,1,0:T(8,128)S(1)}, u32[]{:S(2)}, u32[]{:S(2)}) async-start(f32[128,8,256]{2,1,0:T(8,128)} %shard_map.66), calls=%async_computation.3 | async-start | bytes 2097152 | tf_op jit(solution)/shard_map/all_to_all | solution.py:307
  94.7 23.2 %all-to-all-done.3.msg_ref = f32[128,8,256]{2,1,0:T(8,128)S(1)} async-done(((f32[128,8,256]{2,1,0:T(8,128)}), f32[128,8,256]{2,1,0:T(8,128)S(1)}, u32[]{:S(2)}, u32[]{:S(2)}) %all-to-all-start.3) | async-done | bytes 1048608 | tf_op jit(solution)/shard_map/all_to_all | solution.py:307
  117.9 2.3 %copy-done.2 = bf16[3584,640,1]{1,0,2:T(8,128)(2,1)S(1)} copy-done((bf16[3584,640,1]{1,0,2:T(8,128)(2,1)S(1)}, bf16[3584,640,1]{1,0,2:T(8,128)(2,1)}, u32[]{:S(2)}) %copy-start.2) | copy-done | bytes 4587544
  120.2 4.2 %shard_map.67 = bf16[256,3584]{1,0:T(8,128)(2,1)S(1)} custom-call(s32[128,256]{1,0:T(8,128)S(1)} %copy-done.3, f32[640,256]{1,0:T(8,128)S(1)} %get-tuple-element.7.logit_ref, f32[128,8,256]{2,1,0:T(8,128)S(1)} %all-to-all-done.3.msg_ref, bf16[256,256]{1,0:T(8,128)(2,1)S(1)} %dynamic-slice_bitcast_fusion.order_ref, bf16[3584,640]{1,0:T(8,128)(2,1)S(1)} %bitcast.18), custom_call_target="tpu_custom_call" | custom-call | tf_op jit(solution)/shard_map/pallas_call | solution.py:263
  124.4 17.0 %all_to_all.45 = bf16[4,64,3584]{2,1,0:T(8,128)(2,1)S(1)} all-to-all(bf16[4,64,3584]{2,1,0:T(8,128)(2,1)S(1)} %bitcast.19), channel_id=1, replica_groups={{0,1,2,3},{4,5,6,7},{8,9,10,11},{12,13,14,15},{16,17,18,19},{20,21,22,2..., dimensions={0} | all-to-all | bytes 3670016 | tf_op jit(solution)/shard_map/all_to_all | solution.py:45
  141.5 0.4 reduce_sum.24
  141.8 0.2 all_to_all.35
  142.0 17.9 %all_to_all.46 = bf16[32,2,3584]{2,1,0:T(2,128)(2,1)S(1)} all-to-all(bf16[32,2,3584]{2,1,0:T(2,128)(2,1)S(1)} %all_to_all.35), channel_id=1, replica_groups={{0,4,8,12,16,20,24,28,32,36,40,44,48,52,56,60,64,68,72,76,80,84,88,92,9..., dimensions={0} | all-to-all | bytes 917504 | tf_op jit(solution)/shard_map/all_to_all | solution.py:45
  159.9 0.4 reduce_sum.25
  160.3 8.8 %collective-permute-start = (bf16[2,3584]{1,0:T(2,128)(2,1)S(1)}, bf16[2,3584]{1,0:T(2,128)(2,1)S(1)}, u32[]{:S(2)}, u32[]{:S(2)}) collective-permute-start(bf16[2,3584]{1,0:T(2,128)(2,1)S(1)} %reduce_sum.25), channel_id=1, source_target_pairs={{0,0},{4,4},{8,8},{12,12},{16,16},{20,20},{24,24},{28,28},{32,32},... | collective-permute-start | bytes 43016 | tf_op jit(solution)/shard_map/ppermute | solution.py:319
  169.1 1.4 collective-permute-done
  170.5 0.6 copy.24
  (13 shorter events, 0.4 us)
Async XLA Ops:
  0.0 42.2 %copy-start = (s32[512,128]{1,0:T(8,128)S(1)}, s32[512,128]{1,0:T(8,128)}, u32[]{:S(2)}) copy-start(s32[512,128]{1,0:T(8,128)} %param.10) | copy-start | bytes 786436
  37.3 33.2 %all-to-all-start.2 = ((bf16[4,64,8704]{2,1,0:T(8,128)(2,1)}), bf16[4,64,8704]{2,1,0:T(8,128)(2,1)}, u32[]{:S(2)}, u32[]{:S(2)}) async-start(bf16[4,64,8704]{2,1,0:T(8,128)(2,1)} %broadcast_in_dim.26), calls=%async_computation.2 | async-start | bytes 8912896 | tf_op jit(solution)/shard_map/all_to_all | solution.py:45
  70.5 2.3 %copy-start.1 = (bf16[3584,640,1]{1,0,2:T(8,128)(2,1)S(1)}, bf16[3584,640,1]{1,0,2:T(8,128)(2,1)}, u32[]{:S(2)}) copy-start(bf16[3584,640,1]{1,0,2:T(8,128)(2,1)} %param.9) | copy-start | bytes 13762564
  72.8 14.1 %copy-start.3 = (s32[128,256]{1,0:T(8,128)S(1)}, s32[128,256]{1,0:T(8,128)}, u32[]{:S(2)}) copy-start(s32[128,256]{1,0:T(8,128)} %shard_map.64.word_ref) | copy-start | bytes 393220
  87.0 7.7 %copy-start.4 = (bf16[2,256,256]{2,1,0:T(8,128)(2,1)S(1)}, bf16[2,256,256]{2,1,0:T(8,128)(2,1)}, u32[]{:S(2)}) copy-start(bf16[2,256,256]{2,1,0:T(8,128)(2,1)} %constant.37.clone) | copy-start | bytes 786436
  88.5 29.4 %all-to-all-start.3 = ((f32[128,8,256]{2,1,0:T(8,128)}), f32[128,8,256]{2,1,0:T(8,128)S(1)}, u32[]{:S(2)}, u32[]{:S(2)}) async-start(f32[128,8,256]{2,1,0:T(8,128)} %shard_map.66), calls=%async_computation.3 | async-start | bytes 2097152 | tf_op jit(solution)/shard_map/all_to_all | solution.py:307
  117.9 2.3 %copy-start.2 = (bf16[3584,640,1]{1,0,2:T(8,128)(2,1)S(1)}, bf16[3584,640,1]{1,0,2:T(8,128)(2,1)}, u32[]{:S(2)}) copy-start(bf16[3584,640,1]{1,0,2:T(8,128)(2,1)} %param.9) | copy-start | bytes 13762564
  160.3 10.2 %collective-permute-start = (bf16[2,3584]{1,0:T(2,128)(2,1)S(1)}, bf16[2,3584]{1,0:T(2,128)(2,1)S(1)}, u32[]{:S(2)}, u32[]{:S(2)}) collective-permute-start(bf16[2,3584]{1,0:T(2,128)(2,1)S(1)} %reduce_sum.25), channel_id=1, source_target_pairs={{0,0},{4,4},{8,8},{12,12},{16,16},{20,20},{24,24},{28,28},{32,32},... | collective-permute-start | bytes 43016 | tf_op jit(solution)/shard_map/ppermute | solution.py:319
where the time goes:
time: 172 us; the launch traced here: 171 us
  blocking collectives  68.6 us (40%)
  waiting for transfers between devices  45 us (26%)
  Pallas kernels  26.2 us (15%)
  starting transfers between devices  19.9 us (12%)
  local copies, waits for them, and re-layouts  9.64 us (6%)
    all_to_all x4, blocking collectives, exchange(): lax.all_to_all(value, WHOLE, 0, 0, tiled=True, axis_index_groups=groups)  68.6 us
    all_to_all x1, waiting for transfers between devices, per_device(): arrived = lax.all_to_all(message, LINE, 0, 0, tiled=True)  23.2 us
    all_to_all x1, waiting for transfers between devices, exchange(): lax.all_to_all(value, WHOLE, 0, 0, tiled=True, axis_index_groups=groups)  20.5 us
    pallas_call x1, Pallas kernels, logits_and_message(): pl.pallas_call(kernel, grid=(t_steps + s_steps,), in_specs=[pl.BlockSpec(...  14.1 us
    ppermute x1, starting transfers between devices, per_device(): return lax.ppermute(summed.astype(jnp.bfloat16), WHOLE, last_hop())  8.78 us
    pallas_call x1, Pallas kernels, tile_words(): pl.pallas_call(kernel, out_shape=jax.ShapeDtypeStruct((count, rows), jnp....  6.34 us
    all_to_all x1, starting transfers between devices, per_device(): arrived = lax.all_to_all(message, LINE, 0, 0, tiled=True)  6.21 us
    unnamed x11, local copies, waits for them, and re-layouts  5.21 us
  transfers between devices with their start and end apart: 3, of which 3 were waited for; matrix products, arithmetic and copies ran while one was open for 1% of the time, Pallas kernels for 4%

commit v1 on v0

v1 whole, which is shorter than its diff:
```python
import functools

import jax
import jax.numpy as jnp
import numpy as np
from jax import lax
from jax.experimental import pallas as pl
from jax.experimental.pallas import tpu as pltpu
from jax.sharding import PartitionSpec as P

loss_scale = 1024.0
NX, NY, NZ = 4, 4, 8
LINE = ("vocab", "dp")
WHOLE = ("mesh", "vocab", "dp")
HALF = NX * NY * NZ


def device(m, x, y, z):
    return m * HALF + (y * NZ + z) * NX + x


LINES_Z = [
    [device(m, x, y, z) for z in range(NZ)]
    for m in range(2)
    for x in range(NX)
    for y in range(NY)
]
LINES_X = [
    [[device(m, x, y, z) for x in range(NX)] for y in range(NY) for z in range(NZ)]
    for m in range(2)
]
LINES_Y = [
    [[device(m, x, y, z) for y in range(NY)] for x in range(NX) for z in range(NZ)]
    for m in range(2)
]
PLANES_YZ = [
    [device(0, x, y, z) for y in range(NY) for z in range(NZ)] for x in range(NX)
]
PLANES_XZ = [
    [device(1, x, y, z) for x in range(NX) for z in range(NZ)] for y in range(NY)
]


def exchange(value, groups):
    return lax.all_to_all(value, WHOLE, 0, 0, tiled=True, axis_index_groups=groups)


def spread(value, groups):
    count = len(groups[0])
    rows, width = value.shape
    copies = jnp.broadcast_to(value[None], (count, rows, width)).reshape(count * rows, width)
    return exchange(copies, groups)


def along(value, by):
    pairs = []
    for x in range(NX):
        for y in range(NY):
            for z in range(NZ):
                pairs.append((device(0, x, y, z), device(0, (x + by) % NX, y, z)))
                pairs.append((device(1, x, y, z), device(1, x, (y + by) % NY, z)))
    return lax.ppermute(value, WHOLE, pairs)


def home(x, y, z):
    x1, x0 = x // 2, x % 2
    y1, y0 = y // 2, y % 2
    z2, z1, z0 = z // 4, (z // 2) % 2, z % 2
    return 2 * x0 + y1, 2 * y0 + z2, 4 * z1 + 2 * z0 + x1


def row_orders():
    orders = np.zeros((2, 2 * HALF, 2 * HALF), np.float32)
    for x in range(NX):
        for y in range(NY):
            for z in range(NZ):
                hx, hy, hz = home(x, y, z)
                for b in range(2):
                    orders[0, ((hx * NY + hy) * NZ + hz) * 2 + b, ((x * NY + y) * NZ + z) * 2 + b] = 1
                    orders[1, ((hy * NX + hx) * NZ + hz) * 2 + b, ((y * NX + x) * NZ + z) * 2 + b] = 1
    return orders


def last_hop():
    pairs = []
    for m in range(2):
        for x in range(NX):
            for y in range(NY):
                for z in range(NZ):
                    pairs.append(
                        (device(m, x, y, z), device(x % 2, 2 * (x // 2) + m, y, z))
                    )
    return pairs


def tile_words(tiles_t):
    count, rows = tiles_t.shape

    def kernel(tiles_ref, word_ref):
        block = lax.broadcasted_iota(jnp.int32, (count, rows), 0)

        def step(k, word):
            tile = tiles_ref[pl.ds(k, 1), :]
            own = (tile * 205) >> 10
            bit = 1 << (tile - 5 * own)
            return word + jnp.where(block == own, bit, 0)

        word_ref[...] = lax.fori_loop(0, count, step, jnp.zeros((count, rows), jnp.int32), unroll=8)

    return pl.pallas_call(
        kernel,
        out_shape=jax.ShapeDtypeStruct((count, rows), jnp.int32),
        cost_estimate=pl.CostEstimate(
            flops=16 * count * count * rows, bytes_accessed=8 * count * rows, transcendentals=0
        ),
    )(tiles_t)


def fetch(source, chunk, buffer, semaphores):
    copies = []
    for k in range(source.shape[0] // chunk):
        rows = pl.ds(k * chunk, chunk)
        copies.append(pltpu.make_async_copy(source.at[rows], buffer.at[rows], semaphores.at[k]))
        copies[-1].start()
    return copies


def logits_and_message(
    slot, own, below, above, left_half, right_half, teacher_head, student_cols, words, own_word,
    per_shard,
):
    piece = own.shape[0]
    rows = 4 * piece
    cols = teacher_head.shape[1]
    lanes = cols // per_shard
    half = left_half.shape[1]
    depth = 512
    t_steps, s_steps = teacher_head.shape[0] // depth, student_cols.shape[0] // depth

    def kernel(
        slot_ref, own_ref, below_ref, above_ref, lh_ref, rh_ref, word_ref, own_word_ref,
        t_hbm, s_hbm, msg_ref, logit_ref, t_ref, s_ref, part_ref, all_ref, t_sem, s_sem,
    ):
        copies = fetch(t_hbm, depth, t_ref, t_sem) + fetch(s_hbm, depth, s_ref, s_sem)

        def across(start, stop):
            if stop <= half:
                return lh_ref[:, start:stop]
            if start >= half:
                return rh_ref[:, start - half : stop - half]
            return jnp.concatenate((lh_ref[:, start:], rh_ref[:, : stop - half]), axis=1)

        for k in range(t_steps + s_steps):
            at = k * depth
            span = slice(at, at + depth)
            left = jnp.concatenate(
                (own_ref[:, span], above_ref[:, span], across(at, at + depth), below_ref[:, span]),
                axis=0,
            )
            copies[k].wait()
            if k < t_steps:
                right, col = t_ref[span, :], slice(0, cols)
            else:
                right, col = s_ref[at - t_steps * depth : at - t_steps * depth + depth, :], slice(cols, 2 * cols)
            term = jnp.dot(left, right, preferred_element_type=jnp.float32)
            if k in (0, t_steps):
                part_ref[:, col] = term
            else:
                part_ref[:, col] += term

        for offset in range(4):
            at = lax.rem(slot_ref[0] + offset, 4)
            all_ref[pl.ds(pl.multiple_of(at * piece, piece), piece), :] = part_ref[
                offset * piece : (offset + 1) * piece, :
            ]

        word = own_word_ref[...]
        t_log = all_ref[:, :cols].T
        s_log = all_ref[:, cols:].T
        logit_ref[...] = s_log
        t_top = jnp.max(t_log, axis=0, keepdims=True)
        named_before = jnp.zeros((1, rows), jnp.int32)
        t_total = jnp.zeros((1, rows), jnp.float32)
        t_rest = jnp.zeros((1, rows), jnp.float32)
        first = jnp.zeros((lanes, rows), jnp.float32)
        second = jnp.zeros((lanes, rows), jnp.float32)
        for t in range(per_shard):
            e = jnp.exp(t_log[t * lanes : (t + 1) * lanes] - t_top)
            part = jnp.sum(e, axis=0, keepdims=True)
            named = (word >> t) & 1
            t_total += part
            t_rest += jnp.where(named == 0, part, 0.0)
            first = jnp.where((named == 1) & (named_before == 0), e, first)
            second = jnp.where((named == 1) & (named_before == 1), e, second)
            named_before += named
        named_s, _ = expand_words(word_ref[...], per_shard)
        s_top = jnp.max(s_log, axis=0, keepdims=True)
        e = jnp.exp(s_log - s_top)
        s_total = jnp.sum(e, axis=0, keepdims=True)
        s_rest = jnp.sum(jnp.where(named_s, 0.0, e), axis=0, keepdims=True)
        line = lax.broadcasted_iota(jnp.int32, (8, rows), 0)
        stats = jnp.zeros((8, rows), jnp.float32)
        for at, value in enumerate((t_top, t_total, t_rest, s_top, s_total, s_rest)):
            stats = jnp.where(line == at + 2, value, stats)
        msg_ref[...] = jnp.where(
            (line == 0)[None],
            first[:, None, :],
            jnp.where((line == 1)[None], second[:, None, :], stats[None]),
        )

    whole = pl.BlockSpec(memory_space=pltpu.VMEM)
    remote = pl.BlockSpec(memory_space=pltpu.HBM)
    return pl.pallas_call(
        kernel,
        in_specs=[pl.BlockSpec(memory_space=pltpu.SMEM)] + [whole] * 7 + [remote] * 2,
        out_specs=[whole, whole],
        out_shape=[
            jax.ShapeDtypeStruct((lanes, 8, rows), jnp.float32),
            jax.ShapeDtypeStruct((cols, rows), jnp.float32),
        ],
        scratch_shapes=[
            pltpu.VMEM(teacher_head.shape, jnp.bfloat16),
            pltpu.VMEM(student_cols.shape, jnp.bfloat16),
            pltpu.VMEM((rows, 2 * cols), jnp.float32),
            pltpu.VMEM((rows, 2 * cols), jnp.float32),
            pltpu.SemaphoreType.DMA((t_steps,)),
            pltpu.SemaphoreType.DMA((s_steps,)),
        ],
        compiler_params=pltpu.CompilerParams(vmem_limit_bytes=48 * 1024 * 1024),
    )(slot, own, below, above, left_half, right_half, words, own_word, teacher_head, student_cols)


def expand_words(words, per_shard):
    shards = words.shape[0]
    tile = lax.broadcasted_iota(jnp.int32, (shards * per_shard, 1), 0)
    within = tile - per_shard * ((tile * 205) >> 10)
    wide = spread_blocks(words.astype(jnp.bfloat16), per_shard).astype(jnp.int32)
    named = (wide >> within) & 1
    before = wide & ((1 << within) - 1)
    return named == 1, before == 0


def spread_blocks(value, per_shard):
    shards = value.shape[0]
    tile = lax.broadcasted_iota(jnp.int32, (shards * per_shard, shards), 0)
    start = per_shard * lax.broadcasted_iota(jnp.int32, (shards * per_shard, shards), 1)
    chosen = ((tile >= start) & (tile < start + per_shard)).astype(jnp.float32).astype(jnp.bfloat16)
    return jnp.dot(chosen, value, preferred_element_type=jnp.float32)


def gradient(words, logit, arrived, order, student_cols, per_shard):
    cols, rows = logit.shape
    ds = student_cols.shape[0]
    width = 512

    def kernel(word_ref, logit_ref, msg_ref, order_ref, w_hbm, out_ref, w_ref, w_sem):
        copies = fetch(w_hbm, width, w_ref, w_sem)

        def sums(at):
            top_each = msg_ref[:, at, :]
            top = jnp.max(top_each, axis=0, keepdims=True)
            weight = jnp.exp(top_each - top)
            total = jnp.sum(weight * msg_ref[:, at + 1, :], axis=0, keepdims=True)
            rest = jnp.sum(weight * msg_ref[:, at + 2, :], axis=0, keepdims=True)
            return top, weight, total, rest / total

        _, t_weight, t_total, t_mass = sums(2)
        s_top, _, s_total, s_mass = sums(5)
        scale = t_weight / t_total
        first = (msg_ref[:, 0, :] * scale).astype(jnp.bfloat16)
        second = (msg_ref[:, 1, :] * scale).astype(jnp.bfloat16)
        named, is_first = expand_words(word_ref[...], per_shard)
        teacher = jnp.where(
            is_first, spread_blocks(first, per_shard), spread_blocks(second, per_shard)
        )
        prob = jnp.exp(logit_ref[...] - s_top) / s_total
        kl = (
            jnp.where(named, prob - teacher, prob * (1.0 - t_mass / s_mass)) * loss_scale
        ).astype(jnp.bfloat16)
        kl = lax.dot_general(
            order_ref[...], kl, (((1,), (1,)), ((), ())), preferred_element_type=jnp.float32
        ).astype(jnp.bfloat16)
        for k in range(ds // width):
            span = slice(k * width, (k + 1) * width)
            copies[k].wait()
            out_ref[:, span] = lax.dot_general(
                kl, w_ref[span, :], (((1,), (1,)), ((), ())), preferred_element_type=jnp.float32
            ).astype(jnp.bfloat16)

    whole = pl.BlockSpec(memory_space=pltpu.VMEM)
    return pl.pallas_call(
        kernel,
        in_specs=[whole] * 4 + [pl.BlockSpec(memory_space=pltpu.HBM)],
        out_specs=whole,
        out_shape=jax.ShapeDtypeStruct((rows, ds), jnp.bfloat16),
        scratch_shapes=[
            pltpu.VMEM(student_cols.shape, jnp.bfloat16),
            pltpu.SemaphoreType.DMA((ds // width,)),
        ],
        compiler_params=pltpu.CompilerParams(vmem_limit_bytes=48 * 1024 * 1024),
    )(words, logit, arrived, order, student_cols)


def per_device(teacher_hidden, teacher_head, student_hidden, student_head, tiles):
    shards = lax.axis_size(LINE)
    shard_index = lax.axis_index(LINE)
    core = lax.axis_index("mesh")
    ds, tiles_all, lane_count = student_head.shape
    student_cols = student_head.reshape(ds, tiles_all * lane_count)
    per_shard = tiles_all // shards
    picks = tiles.shape[1]

    both = jnp.concatenate((teacher_hidden, student_hidden), axis=1)
    mine = lax.dynamic_slice_in_dim(both, 2 * core, 2, 0)
    gathered = spread(mine, LINES_Z)
    gathered = spread(gathered, LINES_Y[0] + LINES_X[1])
    by_chip = tiles.reshape(NY, NZ, NX, 2, 2, picks)
    by_chip = lax.dynamic_index_in_dim(by_chip, core, 3, keepdims=False)
    tiles_t = jnp.where(
        core == 0, by_chip.transpose(4, 2, 0, 1, 3), by_chip.transpose(4, 0, 2, 1, 3)
    ).reshape(picks, 2 * shards)
    words = tile_words(tiles_t)
    below, above = along(gathered, 1), along(gathered, -1)
    below, above, words = lax.optimization_barrier((below, above, words))
    half = gathered.shape[1] // 2
    left_half = along(below[:, :half], 1)
    right_half = along(above[:, half:], -1)
    own_word = lax.dynamic_slice_in_dim(words, shard_index, 1, 0)

    slot = jnp.where(core == 0, lax.axis_index("dp"), lax.axis_index("vocab") // NZ)
    message, logit = logits_and_message(
        slot.reshape(1), gathered, below, above, left_half, right_half, teacher_head,
        student_cols, words, own_word, per_shard,
    )
    arrived = lax.all_to_all(message, LINE, 0, 0, tiled=True)

    order = lax.dynamic_index_in_dim(
        jnp.asarray(row_orders(), jnp.bfloat16), core, 0, keepdims=False
    )
    partial = gradient(words, logit, arrived, order, student_cols, per_shard)

    rows = partial.shape[0]
    near = exchange(partial, LINES_X[0] + LINES_Y[1])
    near = jnp.sum(near.reshape(NX, rows // NX, ds).astype(jnp.float32), axis=0)
    far = exchange(near.astype(jnp.bfloat16), PLANES_YZ + PLANES_XZ)
    summed = jnp.sum(far.reshape(NY * NZ, 2, ds).astype(jnp.float32), axis=0)
    return lax.ppermute(summed.astype(jnp.bfloat16), WHOLE, last_hop())


def solution(mesh):
    return jax.shard_map(
        per_device,
        mesh=mesh,
        in_specs=(
            P(("vocab", "dp"), None),
            P(None, ("vocab", "dp")),
            P(("vocab", "dp"), None),
            P(None, None, ("vocab", "dp")),
            P(),
        ),
        out_specs=P(("mesh", "vocab", "dp"), None),
        check_vma=False,
    )
```

time: 172 us -> 160 us (0.930)
  waiting for transfers between devices: 45 us -> 38.2 us
  Pallas kernels: 26.2 us -> 20 us
  starting transfers between devices: 19.9 us -> 22.9 us
  local copies, waits for them, and re-layouts: 9.64 us -> 7.49 us
    all_to_all x1 -> x0, waiting for transfers between devices: 20.5 us -> none  [exchange(): lax.all_to_all(value, WHOLE, 0, 0, tiled=True, axis_index_groups=groups)]
    ppermute x0 -> x4, waiting for transfers between devices: none -> 14.2 us  [along(): return lax.ppermute(value, WHOLE, pairs)]
    ppermute x0 -> x4, starting transfers between devices: none -> 5.35 us  [along(): return lax.ppermute(value, WHOLE, pairs)]
    all_to_all x1 -> x0, starting transfers between devices: 4.88 us -> none  [exchange(): lax.all_to_all(value, WHOLE, 0, 0, tiled=True, axis_index_groups=groups)]
    pallas_call x3 -> x2, Pallas kernels: 19.8 us -> 15.3 us  [the longest x1 10.2 us: logits_and_message(): pl.pallas_call(kernel, in_specs=[pl.BlockSpec(memory_space=pltpu.SMEM)] +...]
    slice x0 -> x2, local copies, waits for them, and re-layouts: none -> 2.78 us  [the longest x1 1.92 us: per_device(): right_half = along(above[:, half:], -1)]
    all_to_all x1, starting transfers between devices: 6.21 us -> 8.82 us  [per_device(): arrived = lax.all_to_all(message, LINE, 0, 0, tiled=True)]
    broadcast_in_dim x4 -> x3, local copies, waits for them, and re-layouts: 2.78 us -> 0.33 us  [spread(): jnp.broadcast_to(value[None], (count, rows, width))]
  transfers between devices with their start and end apart: 3 -> 6, of which waited for: 3 -> 5; matrix products, arithmetic and copies ran while one was open for 1% -> 2% of each run, Pallas kernels for 4% -> 3%
where the time goes in v1:
time: 160 us; the launch traced here: 159 us
  blocking collectives  69 us (43%)
  waiting for transfers between devices  38.2 us (24%)
  starting transfers between devices  22.9 us (14%)
  Pallas kernels  20 us (12%)
  local copies, waits for them, and re-layouts  7.49 us (5%)
  other arithmetic  1.68 us (1%)
    all_to_all x4, blocking collectives, exchange(): lax.all_to_all(value, WHOLE, 0, 0, tiled=True, axis_index_groups=groups)  69 us
    all_to_all x1, waiting for transfers between devices, per_device(): arrived = lax.all_to_all(message, LINE, 0, 0, tiled=True)  22.5 us
    ppermute x4, waiting for transfers between devices, along(): return lax.ppermute(value, WHOLE, pairs)  14.2 us
    pallas_call x1, Pallas kernels, logits_and_message(): pl.pallas_call(kernel, in_specs=[pl.BlockSpec(memory_space=pltpu.SMEM)] +...  10.2 us
    all_to_all x1, starting transfers between devices, per_device(): arrived = lax.all_to_all(message, LINE, 0, 0, tiled=True)  8.82 us
    ppermute x1, starting transfers between devices, per_device(): return lax.ppermute(summed.astype(jnp.bfloat16), WHOLE, last_hop())  8.77 us
    ppermute x4, starting transfers between devices, along(): return lax.ppermute(value, WHOLE, pairs)  5.35 us
    pallas_call x1, Pallas kernels, gradient(): pl.pallas_call(kernel, in_specs=[whole] * 4 + [pl.BlockSpec(memory_space=...  5.09 us
  transfers between devices with their start and end apart: 6, of which 5 were waited for; matrix products, arithmetic and copies ran while one was open for 2% of the time, Pallas kernels for 3%

profile of v1, /device:TPU:1, one launch (start us, length us, event | category | flops | bytes accessed | tf_op | source)
XLA Modules:
  0.0 159.4 jit_solution(8507488727810873730)
XLA Ops:
  0.0 0.9 fusion
  1.0 19.4 %all_to_all.37 = bf16[8,2,8704]{2,1,0:T(2,128)(2,1)S(1)} all-to-all(bf16[8,2,8704]{2,1,0:T(2,128)(2,1)S(1)} %broadcast_in_dim.6), channel_id=1, replica_groups={{0,4,8,12,16,20,24,28},{32,36,40,44,48,52,56,60},{64,68,72,76,80,84,88,..., dimensions={0} | all-to-all | bytes 557056 | tf_op jit(solution)/shard_map/all_to_all | solution.py:45
  20.6 14.2 %all_to_all.38 = bf16[4,16,8704]{2,1,0:T(8,128)(2,1)S(1)} all-to-all(bf16[4,16,8704]{2,1,0:T(8,128)(2,1)S(1)} %broadcast_in_dim.16), channel_id=1, replica_groups={{0,32,64,96},{4,36,68,100},{8,40,72,104},{12,44,76,108},{16,48,80,112},..., dimensions={0} | all-to-all | bytes 2228224 | tf_op jit(solution)/shard_map/all_to_all | solution.py:45
  34.8 1.0 collective-permute-start
  35.8 1.7 %collective-permute-start.1 = (bf16[64,8704]{1,0:T(8,128)(2,1)S(1)}, bf16[64,8704]{1,0:T(8,128)(2,1)}, u32[]{:S(2)}, u32[]{:S(2)}) collective-permute-start(bf16[64,8704]{1,0:T(8,128)(2,1)S(1)} %bitcast.19), channel_id=1, source_target_pairs={{0,3},{128,224},{4,7},{132,228},{8,11},{136,232},{12,15},{140,236}... | collective-permute-start | bytes 3342344 | tf_op jit(solution)/shard_map/ppermute | solution.py:62
  38.3 4.7 %shard_map.64.word_ref = s32[128,256]{1,0:T(8,128)} custom-call(s32[128,256]{1,0:T(8,128)} %copy.17.tiles_ref), custom_call_target="tpu_custom_call" | custom-call | flops 67108864 | bytes 262144 | tf_op jit(solution)/shard_map/pallas_call | solution.py:110
  43.0 7.7 %collective-permute-done.below_ref = bf16[64,8704]{1,0:T(8,128)(2,1)S(1)} collective-permute-done((bf16[64,8704]{1,0:T(8,128)(2,1)S(1)}, bf16[64,8704]{1,0:T(8,128)(2,1)S(1)}, u32[]{:S(2)}, u32[]{:S(2)}) %collective-permute-start) | collective-permute-done | bytes 1114144 | tf_op jit(solution)/shard_map/ppermute | solution.py:62
  50.7 0.9 slice.6
  51.6 1.2 collective-permute-start.2
  52.8 1.9 %slice.7 = bf16[64,4352]{1,0:T(8,128)(2,1)} slice(bf16[64,8704]{1,0:T(8,128)(2,1)} %collective-permute-done.1.above_ref), slice={[0:64], [4352:8704]} | slice | bytes 1114112 | tf_op jit(solution)/shard_map/slice | solution.py:327
  54.7 1.5 collective-permute-start.3
  56.2 5.5 %collective-permute-done.2.lh_ref = bf16[64,4352]{1,0:T(8,128)(2,1)S(1)} collective-permute-done((bf16[64,4352]{1,0:T(8,128)(2,1)}, bf16[64,4352]{1,0:T(8,128)(2,1)S(1)}, u32[]{:S(2)}, u32[]{:S(2)}) %collective-permute-start.2) | collective-permute-done | bytes 557088 | tf_op jit(solution)/shard_map/ppermute | solution.py:62
  61.7 0.8 copy-done.3
  62.5 1.1 collective-permute-done.3.rh_ref
  63.6 1.1 copy-done.4
  64.6 10.2 %shard_map.65 = (f32[128,8,256]{2,1,0:T(8,128)S(1)}, f32[640,256]{1,0:T(8,128)S(1)}) custom-call(s32[1]{0:T(128)} %bitcast.7.slot_ref, bf16[64,8704]{1,0:T(8,128)(2,1)S(1)} %bitcast.20, bf16[64,8704]{1,0:T(8,128)(2,1)S(1)} %collective-permute-done.below_ref, bf16[64,8704]{1,0:T(8,128)(2,1)} %collective-permute-done.1.above_ref, ...), custom_call_target="tpu_custom_call" | custom-call | tf_op jit(solution)/shard_map/pallas_call | solution.py:213
  74.9 1.0 copy-done.2
  75.8 8.8 %all-to-all-start.2 = ((f32[128,8,256]{2,1,0:T(8,128)}), f32[128,8,256]{2,1,0:T(8,128)S(1)}, u32[]{:S(2)}, u32[]{:S(2)}) async-start(f32[128,8,256]{2,1,0:T(8,128)} %copy-done.2), calls=%async_computation.2 | async-start | bytes 2097152 | tf_op jit(solution)/shard_map/all_to_all | solution.py:335
  84.7 22.5 %all-to-all-done.2.msg_ref = f32[128,8,256]{2,1,0:T(8,128)S(1)} async-done(((f32[128,8,256]{2,1,0:T(8,128)}), f32[128,8,256]{2,1,0:T(8,128)S(1)}, u32[]{:S(2)}, u32[]{:S(2)}) %all-to-all-start.2) | async-done | bytes 1048608 | tf_op jit(solution)/shard_map/all_to_all | solution.py:335
  107.2 5.1 %shard_map.66 = bf16[256,3584]{1,0:T(8,128)(2,1)S(1)} custom-call(s32[128,256]{1,0:T(8,128)S(1)} %copy-done.1, f32[640,256]{1,0:T(8,128)S(1)} %get-tuple-element.13.logit_ref, f32[128,8,256]{2,1,0:T(8,128)S(1)} %all-to-all-done.2.msg_ref, bf16[256,256]{1,0:T(8,128)(2,1)S(1)} %dynamic-slice_bitcast_fusion.order_ref, bf16[3584,640]{1,0:T(8,128)(2,1)} %bitcast.22), custom_call_target="tpu_custom_call" | custom-call | tf_op jit(solution)/shard_map/pallas_call | solution.py:291
  112.3 17.2 %all_to_all.39 = bf16[4,64,3584]{2,1,0:T(8,128)(2,1)S(1)} all-to-all(bf16[4,64,3584]{2,1,0:T(8,128)(2,1)S(1)} %bitcast.17), channel_id=1, replica_groups={{0,1,2,3},{4,5,6,7},{8,9,10,11},{12,13,14,15},{16,17,18,19},{20,21,22,2..., dimensions={0} | all-to-all | bytes 3670016 | tf_op jit(solution)/shard_map/all_to_all | solution.py:45
  130.1 18.2 %all_to_all.40 = bf16[32,2,3584]{2,1,0:T(2,128)(2,1)S(1)} all-to-all(bf16[32,2,3584]{2,1,0:T(2,128)(2,1)S(1)} %all_to_all.30), channel_id=1, replica_groups={{0,4,8,12,16,20,24,28,32,36,40,44,48,52,56,60,64,68,72,76,80,84,88,92,9..., dimensions={0} | all-to-all | bytes 917504 | tf_op jit(solution)/shard_map/all_to_all | solution.py:45
  148.7 8.8 %collective-permute-start.4 = (bf16[2,3584]{1,0:T(2,128)(2,1)S(1)}, bf16[2,3584]{1,0:T(2,128)(2,1)S(1)}, u32[]{:S(2)}, u32[]{:S(2)}) collective-permute-start(bf16[2,3584]{1,0:T(2,128)(2,1)S(1)} %reduce_sum.25), channel_id=1, source_target_pairs={{0,0},{4,4},{8,8},{12,12},{16,16},{20,20},{24,24},{28,28},{32,32},... | collective-permute-start | bytes 43016 | tf_op jit(solution)/shard_map/ppermute | solution.py:347
  157.4 1.4 collective-permute-done.4
  (21 shorter events, 2.7 us)
Async XLA Ops:
  0.0 37.5 %copy-start = (s32[512,128]{1,0:T(8,128)S(1)}, s32[512,128]{1,0:T(8,128)}, u32[]{:S(2)}) copy-start(s32[512,128]{1,0:T(8,128)} %param.10) | copy-start | bytes 786436
  34.8 15.9 %collective-permute-start = (bf16[64,8704]{1,0:T(8,128)(2,1)S(1)}, bf16[64,8704]{1,0:T(8,128)(2,1)S(1)}, u32[]{:S(2)}, u32[]{:S(2)}) collective-permute-start(bf16[64,8704]{1,0:T(8,128)(2,1)S(1)} %bitcast.18), channel_id=1, source_target_pairs={{0,1},{128,160},{4,5},{132,164},{8,9},{136,168},{12,13},{140,172},... | collective-permute-start | bytes 3342344 | tf_op jit(solution)/shard_map/ppermute | solution.py:62
  35.8 14.9 %collective-permute-start.1 = (bf16[64,8704]{1,0:T(8,128)(2,1)S(1)}, bf16[64,8704]{1,0:T(8,128)(2,1)}, u32[]{:S(2)}, u32[]{:S(2)}) collective-permute-start(bf16[64,8704]{1,0:T(8,128)(2,1)S(1)} %bitcast.19), channel_id=1, source_target_pairs={{0,3},{128,224},{4,7},{132,228},{8,11},{136,232},{12,15},{140,236}... | collective-permute-start | bytes 3342344 | tf_op jit(solution)/shard_map/ppermute | solution.py:62
  43.0 13.1 %copy-start.1 = (s32[128,256]{1,0:T(8,128)S(1)}, s32[128,256]{1,0:T(8,128)}, u32[]{:S(2)}) copy-start(s32[128,256]{1,0:T(8,128)} %shard_map.64.word_ref) | copy-start | bytes 393220
  51.6 10.1 %collective-permute-start.2 = (bf16[64,4352]{1,0:T(8,128)(2,1)}, bf16[64,4352]{1,0:T(8,128)(2,1)S(1)}, u32[]{:S(2)}, u32[]{:S(2)}) collective-permute-start(bf16[64,4352]{1,0:T(8,128)(2,1)} %slice.6), channel_id=1, source_target_pairs={{0,1},{128,160},{4,5},{132,164},{8,9},{136,168},{12,13},{140,172},... | collective-permute-start | bytes 1671176 | tf_op jit(solution)/shard_map/ppermute | solution.py:62
  54.7 8.9 %collective-permute-start.3 = (bf16[64,4352]{1,0:T(8,128)(2,1)}, bf16[64,4352]{1,0:T(8,128)(2,1)}, u32[]{:S(2)}, u32[]{:S(2)}) collective-permute-start(bf16[64,4352]{1,0:T(8,128)(2,1)} %slice.7), channel_id=1, source_target_pairs={{0,3},{128,224},{4,7},{132,228},{8,11},{136,232},{12,15},{140,236}... | collective-permute-start | bytes 1671176 | tf_op jit(solution)/shard_map/ppermute | solution.py:62
  61.7 0.8 copy-start.3
  63.6 1.1 copy-start.4
  74.9 1.0 copy-start.2
  75.8 8.8 %copy-start.5 = (bf16[2,256,256]{2,1,0:T(8,128)(2,1)S(1)}, bf16[2,256,256]{2,1,0:T(8,128)(2,1)}, u32[]{:S(2)}) copy-start(bf16[2,256,256]{2,1,0:T(8,128)(2,1)} %constant.52.clone) | copy-start | bytes 786436
  75.8 31.4 %all-to-all-start.2 = ((f32[128,8,256]{2,1,0:T(8,128)}), f32[128,8,256]{2,1,0:T(8,128)S(1)}, u32[]{:S(2)}, u32[]{:S(2)}) async-start(f32[128,8,256]{2,1,0:T(8,128)} %copy-done.2), calls=%async_computation.2 | async-start | bytes 2097152 | tf_op jit(solution)/shard_map/all_to_all | solution.py:335
  148.7 10.2 %collective-permute-start.4 = (bf16[2,3584]{1,0:T(2,128)(2,1)S(1)}, bf16[2,3584]{1,0:T(2,128)(2,1)S(1)}, u32[]{:S(2)}, u32[]{:S(2)}) collective-permute-start(bf16[2,3584]{1,0:T(2,128)(2,1)S(1)} %reduce_sum.25), channel_id=1, source_target_pairs={{0,0},{4,4},{8,8},{12,12},{16,16},{20,20},{24,24},{28,28},{32,32},... | collective-permute-start | bytes 43016 | tf_op jit(solution)/shard_map/ppermute | solution.py:347

commit v2 on v1

--- a/solution.py
+++ b/solution.py
@@ -52,14 +52,25 @@
     return exchange(copies, groups)
 
 
+def step(value, axes, by):
+    sizes = {"x": NX, "y": NY}
+    pairs = []
+    for m in range(2):
+        for x in range(NX):
+            for y in range(NY):
+                for z in range(NZ):
+                    to = {"x": x, "y": y}
+                    to[axes[m]] = (to[axes[m]] + by) % sizes[axes[m]]
+                    pairs.append((device(m, x, y, z), device(m, to["x"], to["y"], z)))
+    return lax.ppermute(value, WHOLE, pairs)
+
+
+def across(value, by):
+    return step(value, ("y", "x"), by)
+
+
 def along(value, by):
-    pairs = []
-    for x in range(NX):
-        for y in range(NY):
-            for z in range(NZ):
-                pairs.append((device(0, x, y, z), device(0, (x + by) % NX, y, z)))
-                pairs.append((device(1, x, y, z), device(1, x, (y + by) % NY, z)))
-    return lax.ppermute(value, WHOLE, pairs)
+    return step(value, ("x", "y"), by)
 
 
 def home(x, y, z):
@@ -125,54 +136,45 @@
     return copies
 
 
-def logits_and_message(
-    slot, own, below, above, left_half, right_half, teacher_head, student_cols, words, own_word,
-    per_shard,
-):
-    piece = own.shape[0]
-    rows = 4 * piece
+def logits_and_message(slots, halves, teacher_head, student_cols, words, own_word, per_shard):
+    count = len(halves)
+    half = halves[0].shape[0]
+    rows = count * half
+    block = half // 2
     cols = teacher_head.shape[1]
     lanes = cols // per_shard
-    half = left_half.shape[1]
     depth = 512
     t_steps, s_steps = teacher_head.shape[0] // depth, student_cols.shape[0] // depth
 
-    def kernel(
-        slot_ref, own_ref, below_ref, above_ref, lh_ref, rh_ref, word_ref, own_word_ref,
-        t_hbm, s_hbm, msg_ref, logit_ref, t_ref, s_ref, part_ref, all_ref, t_sem, s_sem,
-    ):
+    def kernel(slot_ref, *refs):
+        half_refs = refs[:count]
+        (
+            word_ref, own_word_ref, t_hbm, s_hbm, msg_ref, logit_ref,
+            t_ref, s_ref, part_ref, all_ref, t_sem, s_sem,
+        ) = refs[count:]
         copies = fetch(t_hbm, depth, t_ref, t_sem) + fetch(s_hbm, depth, s_ref, s_sem)
 
-        def across(start, stop):
-            if stop <= half:
-                return lh_ref[:, start:stop]
-            if start >= half:
-                return rh_ref[:, start - half : stop - half]
-            return jnp.concatenate((lh_ref[:, start:], rh_ref[:, : stop - half]), axis=1)
-
         for k in range(t_steps + s_steps):
-            at = k * depth
-            span = slice(at, at + depth)
             left = jnp.concatenate(
-                (own_ref[:, span], above_ref[:, span], across(at, at + depth), below_ref[:, span]),
-                axis=0,
+                [ref[:, k * depth : (k + 1) * depth] for ref in half_refs], axis=0
             )
             copies[k].wait()
             if k < t_steps:
-                right, col = t_ref[span, :], slice(0, cols)
+                right, col = t_ref[k * depth : (k + 1) * depth, :], slice(0, cols)
             else:
-                right, col = s_ref[at - t_steps * depth : at - t_steps * depth + depth, :], slice(cols, 2 * cols)
+                n = k - t_steps
+                right, col = s_ref[n * depth : (n + 1) * depth, :], slice(cols, 2 * cols)
             term = jnp.dot(left, right, preferred_element_type=jnp.float32)
             if k in (0, t_steps):
                 part_ref[:, col] = term
             else:
                 part_ref[:, col] += term
 
-        for offset in range(4):
-            at = lax.rem(slot_ref[0] + offset, 4)
-            all_ref[pl.ds(pl.multiple_of(at * piece, piece), piece), :] = part_ref[
-                offset * piece : (offset + 1) * piece, :
-            ]
+        for n in range(16):
+            third = lax.rem(slot_ref[0] + n // 4, 4)
+            second = lax.rem(slot_ref[1] + (0, 3, 1, 2)[n % 4], 4)
+            at = pl.multiple_of((third * 4 + second) * block, block)
+            all_ref[pl.ds(at, block), :] = part_ref[n * block : (n + 1) * block, :]
 
         word = own_word_ref[...]
         t_log = all_ref[:, :cols].T
@@ -212,7 +214,7 @@
     remote = pl.BlockSpec(memory_space=pltpu.HBM)
     return pl.pallas_call(
         kernel,
-        in_specs=[pl.BlockSpec(memory_space=pltpu.SMEM)] + [whole] * 7 + [remote] * 2,
+        in_specs=[pl.BlockSpec(memory_space=pltpu.SMEM)] + [whole] * (count + 2) + [remote] * 2,
         out_specs=[whole, whole],
         out_shape=[
             jax.ShapeDtypeStruct((lanes, 8, rows), jnp.float32),
@@ -227,7 +229,7 @@
             pltpu.SemaphoreType.DMA((s_steps,)),
         ],
         compiler_params=pltpu.CompilerParams(vmem_limit_bytes=48 * 1024 * 1024),
-    )(slot, own, below, above, left_half, right_half, words, own_word, teacher_head, student_cols)
+    )(slots, *halves, words, own_word, teacher_head, student_cols)
 
 
 def expand_words(words, per_shard):
@@ -313,24 +315,30 @@
     both = jnp.concatenate((teacher_hidden, student_hidden), axis=1)
     mine = lax.dynamic_slice_in_dim(both, 2 * core, 2, 0)
     gathered = spread(mine, LINES_Z)
-    gathered = spread(gathered, LINES_Y[0] + LINES_X[1])
     by_chip = tiles.reshape(NY, NZ, NX, 2, 2, picks)
     by_chip = lax.dynamic_index_in_dim(by_chip, core, 3, keepdims=False)
     tiles_t = jnp.where(
         core == 0, by_chip.transpose(4, 2, 0, 1, 3), by_chip.transpose(4, 0, 2, 1, 3)
     ).reshape(picks, 2 * shards)
     words = tile_words(tiles_t)
-    below, above = along(gathered, 1), along(gathered, -1)
-    below, above, words = lax.optimization_barrier((below, above, words))
-    half = gathered.shape[1] // 2
-    left_half = along(below[:, :half], 1)
-    right_half = along(above[:, half:], -1)
+    last, after, opposite = across(gathered, 1), across(gathered, -1), across(gathered, 2)
+    own = (
+        jnp.concatenate((gathered, last), axis=0),
+        jnp.concatenate((after, opposite), axis=0),
+    )
+    below_first = along(own[0], 1)
+    above_first = along(own[1], -1)
+    below_second = along(own[1], 1)
+    above_second = along(own[0], -1)
+    below_first, above_first, words = lax.optimization_barrier((below_first, above_first, words))
+    far = (along(below_first, 1), along(above_first, -1))
+    halves = own + (above_second, above_first) + far + (below_first, below_second)
     own_word = lax.dynamic_slice_in_dim(words, shard_index, 1, 0)
 
-    slot = jnp.where(core == 0, lax.axis_index("dp"), lax.axis_index("vocab") // NZ)
+    x, y = lax.axis_index("dp"), lax.axis_index("vocab") // NZ
+    slots = jnp.stack((jnp.where(core == 0, x, y), jnp.where(core == 0, y, x)))
     message, logit = logits_and_message(
-        slot.reshape(1), gathered, below, above, left_half, right_half, teacher_head,
-        student_cols, words, own_word, per_shard,
+        slots, halves, teacher_head, student_cols, words, own_word, per_shard
     )
     arrived = lax.all_to_all(message, LINE, 0, 0, tiled=True)
 

time: 160 us -> 154 us (0.963)
  blocking collectives: 69 us -> 54 us
  starting transfers between devices: 22.9 us -> 31 us
  local copies, waits for them, and re-layouts: 7.49 us -> 5.34 us
    all_to_all x4 -> x3, blocking collectives: 69 us -> 54 us  [exchange(): lax.all_to_all(value, WHOLE, 0, 0, tiled=True, axis_index_groups=groups)]
    ppermute x4 -> x9, starting transfers between devices: 5.35 us -> 13.4 us  [step(): return lax.ppermute(value, WHOLE, pairs)]
    slice x2 -> x0, local copies, waits for them, and re-layouts: 2.78 us -> none  [the longest x1 1.92 us: per_device(): right_half = along(above[:, half:], -1)]
    ppermute x4 -> x9, waiting for transfers between devices: 14.2 us -> 14.9 us  [step(): return lax.ppermute(value, WHOLE, pairs)]
    unnamed x13 -> x15, local copies, waits for them, and re-layouts: 3.44 us -> 3.4 us
  transfers between devices with their start and end apart: 6 -> 11, of which waited for: 5 -> 8; matrix products, arithmetic and copies ran while one was open for 2% -> 1% of each run, Pallas kernels for 3% -> 3%
where the time goes in v2:
time: 154 us; the launch traced here: 153 us
  blocking collectives  54 us (35%)
  waiting for transfers between devices  39.8 us (26%)
  starting transfers between devices  31 us (20%)
  Pallas kernels  21.3 us (14%)
  local copies, waits for them, and re-layouts  5.34 us (3%)
  other arithmetic  1.75 us (1%)
    all_to_all x3, blocking collectives, exchange(): lax.all_to_all(value, WHOLE, 0, 0, tiled=True, axis_index_groups=groups)  54 us
    all_to_all x1, waiting for transfers between devices, per_device(): arrived = lax.all_to_all(message, LINE, 0, 0, tiled=True)  23.5 us
    ppermute x9, waiting for transfers between devices, step(): return lax.ppermute(value, WHOLE, pairs)  14.9 us
    ppermute x9, starting transfers between devices, step(): return lax.ppermute(value, WHOLE, pairs)  13.4 us
    pallas_call x1, Pallas kernels, logits_and_message(): pl.pallas_call(kernel, in_specs=[pl.BlockSpec(memory_space=pltpu.SMEM)] +...  11.5 us
    all_to_all x1, starting transfers between devices, per_device(): arrived = lax.all_to_all(message, LINE, 0, 0, tiled=True)  8.88 us
    ppermute x1, starting transfers between devices, per_device(): return lax.ppermute(summed.astype(jnp.bfloat16), WHOLE, last_hop())  8.77 us
    pallas_call x1, Pallas kernels, gradient(): pl.pallas_call(kernel, in_specs=[whole] * 4 + [pl.BlockSpec(memory_space=...  5.09 us
  transfers between devices with their start and end apart: 11, of which 8 were waited for; matrix products, arithmetic and copies ran while one was open for 1% of the time, Pallas kernels for 3%

profile of v2, /device:TPU:1, one launch (start us, length us, event | category | flops | bytes accessed | tf_op | source)
XLA Modules:
  0.0 153.4 jit_solution(4728779821321504537)
XLA Ops:
  0.0 0.9 fusion
  1.0 19.4 %all_to_all.32 = bf16[8,2,8704]{2,1,0:T(2,128)(2,1)S(1)} all-to-all(bf16[8,2,8704]{2,1,0:T(2,128)(2,1)S(1)} %broadcast_in_dim.2), channel_id=1, replica_groups={{0,4,8,12,16,20,24,28},{32,36,40,44,48,52,56,60},{64,68,72,76,80,84,88,..., dimensions={0} | all-to-all | bytes 557056 | tf_op jit(solution)/shard_map/all_to_all | solution.py:45
  20.6 2.6 %collective-permute-start.2 = (bf16[16,8704]{1,0:T(8,128)(2,1)S(1)}, bf16[16,8704]{1,0:T(8,128)(2,1)S(1)}, u32[]{:S(2)}, u32[]{:S(2)}) collective-permute-start(bf16[16,8704]{1,0:T(8,128)(2,1)S(1)} %all_to_all.22), channel_id=1, source_target_pairs={{0,96},{4,100},{8,104},{12,108},{16,112},{20,116},{24,120},{28,124... | collective-permute-start | bytes 835592 | tf_op jit(solution)/shard_map/ppermute | solution.py:65
  24.3 5.3 %collective-permute-done.2 = bf16[16,8704]{1,0:T(8,128)(2,1)S(1)} collective-permute-done((bf16[16,8704]{1,0:T(8,128)(2,1)S(1)}, bf16[16,8704]{1,0:T(8,128)(2,1)S(1)}, u32[]{:S(2)}, u32[]{:S(2)}) %collective-permute-start.2) | collective-permute-done | bytes 278560 | tf_op jit(solution)/shard_map/ppermute | solution.py:65
  30.1 3.0 %collective-permute-start.4 = (bf16[32,8704]{1,0:T(8,128)(2,1)S(1)}, bf16[32,8704]{1,0:T(8,128)(2,1)S(1)}, u32[]{:S(2)}, u32[]{:S(2)}) collective-permute-start(bf16[32,8704]{1,0:T(8,128)(2,1)S(1)} %constant_dynamic-update-slice_fusion.2.refs_1_), channel_id=1, source_target_pairs={{0,3},{4,7},{8,11},{12,15},{16,19},{20,23},{24,27},{28,31},{32,35}... | collective-permute-start | bytes 1671176 | tf_op jit(solution)/shard_map/ppermute | solution.py:65
  33.3 1.2 collective-permute-start.1
  34.6 0.8 copy.17.tiles_ref
  35.3 4.7 %shard_map.64.refs_8_.word_ref = s32[128,256]{1,0:T(8,128)} custom-call(s32[128,256]{1,0:T(8,128)} %copy.17.tiles_ref), custom_call_target="tpu_custom_call" | custom-call | flops 67108864 | bytes 262144 | tf_op jit(solution)/shard_map/pallas_call | solution.py:121
  40.1 1.2 collective-permute-start.8
  41.2 1.5 collective-permute-start.5
  43.4 2.7 %collective-permute-start.7 = (bf16[32,8704]{1,0:T(8,128)(2,1)S(1)}, bf16[32,8704]{1,0:T(8,128)(2,1)}, u32[]{:S(2)}, u32[]{:S(2)}) collective-permute-start(bf16[32,8704]{1,0:T(8,128)(2,1)S(1)} %collective-permute-done.4.refs_3_), channel_id=1, source_target_pairs={{0,3},{4,7},{8,11},{12,15},{16,19},{20,23},{24,27},{28,31},{32,35}... | collective-permute-start | bytes 1671176 | tf_op jit(solution)/shard_map/ppermute | solution.py:65
  46.8 3.1 %collective-permute-done.8.refs_7_ = bf16[32,8704]{1,0:T(8,128)(2,1)S(1)} collective-permute-done((bf16[32,8704]{1,0:T(8,128)(2,1)S(1)}, bf16[32,8704]{1,0:T(8,128)(2,1)S(1)}, u32[]{:S(2)}, u32[]{:S(2)}) %collective-permute-start.8) | collective-permute-done | bytes 557088 | tf_op jit(solution)/shard_map/ppermute | solution.py:65
  49.9 0.8 copy-done.3
  50.7 5.3 %collective-permute-done.6.refs_4_ = bf16[32,8704]{1,0:T(8,128)(2,1)} collective-permute-done((bf16[32,8704]{1,0:T(8,128)(2,1)S(1)}, bf16[32,8704]{1,0:T(8,128)(2,1)}, u32[]{:S(2)}, u32[]{:S(2)}) %collective-permute-start.6) | collective-permute-done | bytes 557088 | tf_op jit(solution)/shard_map/ppermute | solution.py:65
  56.0 0.9 copy-done.1
  56.9 1.1 copy-done.4
  58.0 11.5 %shard_map.65 = (f32[128,8,256]{2,1,0:T(8,128)}, f32[640,256]{1,0:T(8,128)S(1)}) custom-call(s32[2]{0:T(128)S(1)} %pad_add_fusion.slot_ref, bf16[32,8704]{1,0:T(8,128)(2,1)S(1)} %constant_dynamic-update-slice_fusion.refs_0_, bf16[32,8704]{1,0:T(8,128)(2,1)S(1)} %constant_dynamic-update-slice_fusion.2.refs_1_, ...), custom_call_target="tpu_custom_call" | custom-call | tf_op jit(solution)/shard_map/pallas_call | solution.py:215
  69.5 8.9 %all-to-all-start.1 = ((f32[128,8,256]{2,1,0:T(8,128)}), f32[128,8,256]{2,1,0:T(8,128)S(1)}, u32[]{:S(2)}, u32[]{:S(2)}) async-start(f32[128,8,256]{2,1,0:T(8,128)} %get-tuple-element.14), calls=%async_computation.1 | async-start | bytes 2097152 | tf_op jit(solution)/shard_map/all_to_all | solution.py:343
  78.5 23.5 %all-to-all-done.1.msg_ref = f32[128,8,256]{2,1,0:T(8,128)S(1)} async-done(((f32[128,8,256]{2,1,0:T(8,128)}), f32[128,8,256]{2,1,0:T(8,128)S(1)}, u32[]{:S(2)}, u32[]{:S(2)}) %all-to-all-start.1) | async-done | bytes 1048608 | tf_op jit(solution)/shard_map/all_to_all | solution.py:343
  101.9 5.1 %shard_map.66 = bf16[256,3584]{1,0:T(8,128)(2,1)S(1)} custom-call(s32[128,256]{1,0:T(8,128)S(1)} %copy-done.2, f32[640,256]{1,0:T(8,128)S(1)} %get-tuple-element.13.logit_ref, f32[128,8,256]{2,1,0:T(8,128)S(1)} %all-to-all-done.1.msg_ref, bf16[256,256]{1,0:T(8,128)(2,1)S(1)} %dynamic-slice_bitcast_fusion.order_ref, bf16[3584,640]{1,0:T(8,128)(2,1)} %bitcast.19), custom_call_target="tpu_custom_call" | custom-call | tf_op jit(solution)/shard_map/pallas_call | solution.py:293
  107.0 17.3 %all_to_all.33 = bf16[4,64,3584]{2,1,0:T(8,128)(2,1)S(1)} all-to-all(bf16[4,64,3584]{2,1,0:T(8,128)(2,1)S(1)} %bitcast.17), channel_id=1, replica_groups={{0,1,2,3},{4,5,6,7},{8,9,10,11},{12,13,14,15},{16,17,18,19},{20,21,22,2..., dimensions={0} | all-to-all | bytes 3670016 | tf_op jit(solution)/shard_map/all_to_all | solution.py:45
  124.9 17.3 %all_to_all.34 = bf16[32,2,3584]{2,1,0:T(2,128)(2,1)S(1)} all-to-all(bf16[32,2,3584]{2,1,0:T(2,128)(2,1)S(1)} %all_to_all.26), channel_id=1, replica_groups={{0,4,8,12,16,20,24,28,32,36,40,44,48,52,56,60,64,68,72,76,80,84,88,92,9..., dimensions={0} | all-to-all | bytes 917504 | tf_op jit(solution)/shard_map/all_to_all | solution.py:45
  142.6 8.8 %collective-permute-start.9 = (bf16[2,3584]{1,0:T(2,128)(2,1)S(1)}, bf16[2,3584]{1,0:T(2,128)(2,1)S(1)}, u32[]{:S(2)}, u32[]{:S(2)}) collective-permute-start(bf16[2,3584]{1,0:T(2,128)(2,1)S(1)} %reduce_sum.25), channel_id=1, source_target_pairs={{0,0},{4,4},{8,8},{12,12},{16,16},{20,20},{24,24},{28,28},{32,32},... | collective-permute-start | bytes 43016 | tf_op jit(solution)/shard_map/ppermute | solution.py:355
  151.4 1.4 collective-permute-done.9
  (32 shorter events, 5.2 us)
Async XLA Ops:
  0.0 34.5 %copy-start = (s32[512,128]{1,0:T(8,128)S(1)}, s32[512,128]{1,0:T(8,128)}, u32[]{:S(2)}) copy-start(s32[512,128]{1,0:T(8,128)} %param.10) | copy-start | bytes 786436
  20.6 9.0 %collective-permute-start.2 = (bf16[16,8704]{1,0:T(8,128)(2,1)S(1)}, bf16[16,8704]{1,0:T(8,128)(2,1)S(1)}, u32[]{:S(2)}, u32[]{:S(2)}) collective-permute-start(bf16[16,8704]{1,0:T(8,128)(2,1)S(1)} %all_to_all.22), channel_id=1, source_target_pairs={{0,96},{4,100},{8,104},{12,108},{16,112},{20,116},{24,120},{28,124... | collective-permute-start | bytes 835592 | tf_op jit(solution)/shard_map/ppermute | solution.py:65
  23.1 7.0 %collective-permute-start.3 = (bf16[16,8704]{1,0:T(8,128)(2,1)S(1)}, bf16[16,8704]{1,0:T(8,128)(2,1)S(1)}, u32[]{:S(2)}, u32[]{:S(2)}) collective-permute-start(bf16[16,8704]{1,0:T(8,128)(2,1)S(1)} %all_to_all.22), channel_id=1, source_target_pairs={{0,64},{4,68},{8,72},{12,76},{16,80},{20,84},{24,88},{28,92},{32,9... | collective-permute-start | bytes 835592 | tf_op jit(solution)/shard_map/ppermute | solution.py:65
  23.7 9.6 %collective-permute-start = (bf16[16,8704]{1,0:T(8,128)(2,1)S(1)}, bf16[16,8704]{1,0:T(8,128)(2,1)S(1)}, u32[]{:S(2)}, u32[]{:S(2)}) collective-permute-start(bf16[16,8704]{1,0:T(8,128)(2,1)S(1)} %all_to_all.22), channel_id=1, source_target_pairs={{0,32},{4,36},{8,40},{12,44},{16,48},{20,52},{24,56},{28,60},{32,6... | collective-permute-start | bytes 835592 | tf_op jit(solution)/shard_map/ppermute | solution.py:65
  30.1 12.6 %collective-permute-start.4 = (bf16[32,8704]{1,0:T(8,128)(2,1)S(1)}, bf16[32,8704]{1,0:T(8,128)(2,1)S(1)}, u32[]{:S(2)}, u32[]{:S(2)}) collective-permute-start(bf16[32,8704]{1,0:T(8,128)(2,1)S(1)} %constant_dynamic-update-slice_fusion.2.refs_1_), channel_id=1, source_target_pairs={{0,3},{4,7},{8,11},{12,15},{16,19},{20,23},{24,27},{28,31},{32,35}... | collective-permute-start | bytes 1671176 | tf_op jit(solution)/shard_map/ppermute | solution.py:65
  33.3 10.0 %collective-permute-start.1 = (bf16[32,8704]{1,0:T(8,128)(2,1)S(1)}, bf16[32,8704]{1,0:T(8,128)(2,1)S(1)}, u32[]{:S(2)}, u32[]{:S(2)}) collective-permute-start(bf16[32,8704]{1,0:T(8,128)(2,1)S(1)} %constant_dynamic-update-slice_fusion.refs_0_), channel_id=1, source_target_pairs={{0,1},{4,5},{8,9},{12,13},{16,17},{20,21},{24,25},{28,29},{32,33},... | collective-permute-start | bytes 1671176 | tf_op jit(solution)/shard_map/ppermute | solution.py:65
  40.1 9.9 %collective-permute-start.8 = (bf16[32,8704]{1,0:T(8,128)(2,1)S(1)}, bf16[32,8704]{1,0:T(8,128)(2,1)S(1)}, u32[]{:S(2)}, u32[]{:S(2)}) collective-permute-start(bf16[32,8704]{1,0:T(8,128)(2,1)S(1)} %constant_dynamic-update-slice_fusion.2.refs_1_), channel_id=1, source_target_pairs={{0,1},{4,5},{8,9},{12,13},{16,17},{20,21},{24,25},{28,29},{32,33},... | collective-permute-start | bytes 1671176 | tf_op jit(solution)/shard_map/ppermute | solution.py:65
  41.2 9.5 %collective-permute-start.5 = (bf16[32,8704]{1,0:T(8,128)(2,1)S(1)}, bf16[32,8704]{1,0:T(8,128)(2,1)}, u32[]{:S(2)}, u32[]{:S(2)}) collective-permute-start(bf16[32,8704]{1,0:T(8,128)(2,1)S(1)} %constant_dynamic-update-slice_fusion.refs_0_), channel_id=1, source_target_pairs={{0,3},{4,7},{8,11},{12,15},{16,19},{20,23},{24,27},{28,31},{32,35}... | collective-permute-start | bytes 1671176 | tf_op jit(solution)/shard_map/ppermute | solution.py:65
  43.4 12.7 %collective-permute-start.6 = (bf16[32,8704]{1,0:T(8,128)(2,1)S(1)}, bf16[32,8704]{1,0:T(8,128)(2,1)}, u32[]{:S(2)}, u32[]{:S(2)}) collective-permute-start(bf16[32,8704]{1,0:T(8,128)(2,1)S(1)} %collective-permute-done.1.refs_6_), channel_id=1, source_target_pairs={{0,1},{4,5},{8,9},{12,13},{16,17},{20,21},{24,25},{28,29},{32,33},... | collective-permute-start | bytes 1671176 | tf_op jit(solution)/shard_map/ppermute | solution.py:65
  43.4 12.7 %collective-permute-start.7 = (bf16[32,8704]{1,0:T(8,128)(2,1)S(1)}, bf16[32,8704]{1,0:T(8,128)(2,1)}, u32[]{:S(2)}, u32[]{:S(2)}) collective-permute-start(bf16[32,8704]{1,0:T(8,128)(2,1)S(1)} %collective-permute-done.4.refs_3_), channel_id=1, source_target_pairs={{0,3},{4,7},{8,11},{12,15},{16,19},{20,23},{24,27},{28,31},{32,35}... | collective-permute-start | bytes 1671176 | tf_op jit(solution)/shard_map/ppermute | solution.py:65
  49.9 0.8 copy-start.3
  56.0 0.9 copy-start.1
  56.9 1.1 copy-start.4
  58.0 20.4 %copy-start.5 = (bf16[2,256,256]{2,1,0:T(8,128)(2,1)S(1)}, bf16[2,256,256]{2,1,0:T(8,128)(2,1)}, u32[]{:S(2)}) copy-start(bf16[2,256,256]{2,1,0:T(8,128)(2,1)} %constant.52.clone) | copy-start | bytes 786436
  58.0 44.0 %copy-start.2 = (s32[128,256]{1,0:T(8,128)S(1)}, s32[128,256]{1,0:T(8,128)}, u32[]{:S(2)}) copy-start(s32[128,256]{1,0:T(8,128)} %shard_map.64.refs_8_.word_ref) | copy-start | bytes 393220
  69.5 32.4 %all-to-all-start.1 = ((f32[128,8,256]{2,1,0:T(8,128)}), f32[128,8,256]{2,1,0:T(8,128)S(1)}, u32[]{:S(2)}, u32[]{:S(2)}) async-start(f32[128,8,256]{2,1,0:T(8,128)} %get-tuple-element.14), calls=%async_computation.1 | async-start | bytes 2097152 | tf_op jit(solution)/shard_map/all_to_all | solution.py:343
  142.6 10.2 %collective-permute-start.9 = (bf16[2,3584]{1,0:T(2,128)(2,1)S(1)}, bf16[2,3584]{1,0:T(2,128)(2,1)S(1)}, u32[]{:S(2)}, u32[]{:S(2)}) collective-permute-start(bf16[2,3584]{1,0:T(2,128)(2,1)S(1)} %reduce_sum.25), channel_id=1, source_target_pairs={{0,0},{4,4},{8,8},{12,12},{16,16},{20,20},{24,24},{28,28},{32,32},... | collective-permute-start | bytes 43016 | tf_op jit(solution)/shard_map/ppermute | solution.py:355

commit v3 on v2

--- a/solution.py
+++ b/solution.py
@@ -150,7 +150,7 @@
         half_refs = refs[:count]
         (
             word_ref, own_word_ref, t_hbm, s_hbm, msg_ref, logit_ref,
-            t_ref, s_ref, part_ref, all_ref, t_sem, s_sem,
+            t_ref, s_ref, part_ref, all_ref, spare_ref, t_sem, s_sem,
         ) = refs[count:]
         copies = fetch(t_hbm, depth, t_ref, t_sem) + fetch(s_hbm, depth, s_ref, s_sem)
 
@@ -203,12 +203,22 @@
         line = lax.broadcasted_iota(jnp.int32, (8, rows), 0)
         stats = jnp.zeros((8, rows), jnp.float32)
         for at, value in enumerate((t_top, t_total, t_rest, s_top, s_total, s_rest)):
-            stats = jnp.where(line == at + 2, value, stats)
-        msg_ref[...] = jnp.where(
-            (line == 0)[None],
-            first[:, None, :],
-            jnp.where((line == 1)[None], second[:, None, :], stats[None]),
-        )
+            stats = jnp.where(line == at, value, stats)
+        for part in range(rows // 128):
+            spare_ref[part, :lanes, :] = first[:, part * 128 : (part + 1) * 128]
+            spare_ref[part, lanes:, :] = second[:, part * 128 : (part + 1) * 128]
+        core = slot_ref[2]
+        for x in range(4):
+            for y in range(4):
+                to = jnp.where(core == 0, x, y)
+                at = 8 * jnp.where(core == 0, y, x)
+                for slot in range(2):
+                    lines = pl.ds(pl.multiple_of(slot * 32 + at, 8), 8)
+                    for part in range(rows // 128):
+                        msg_ref[to, lines, part * 128 : (part + 1) * 128] = spare_ref[
+                            part, pl.ds(slot * lanes + y * 32 + x, 8, stride=4), :
+                        ]
+            msg_ref[x, 64:72, :] = stats
 
     whole = pl.BlockSpec(memory_space=pltpu.VMEM)
     remote = pl.BlockSpec(memory_space=pltpu.HBM)
@@ -217,7 +227,7 @@
         in_specs=[pl.BlockSpec(memory_space=pltpu.SMEM)] + [whole] * (count + 2) + [remote] * 2,
         out_specs=[whole, whole],
         out_shape=[
-            jax.ShapeDtypeStruct((lanes, 8, rows), jnp.float32),
+            jax.ShapeDtypeStruct((4, 72, rows), jnp.float32),
             jax.ShapeDtypeStruct((cols, rows), jnp.float32),
         ],
         scratch_shapes=[
@@ -225,6 +235,7 @@
             pltpu.VMEM(student_cols.shape, jnp.bfloat16),
             pltpu.VMEM((rows, 2 * cols), jnp.float32),
             pltpu.VMEM((rows, 2 * cols), jnp.float32),
+            pltpu.VMEM((rows // 128, 2 * lanes, 128), jnp.float32),
             pltpu.SemaphoreType.DMA((t_steps,)),
             pltpu.SemaphoreType.DMA((s_steps,)),
         ],
@@ -250,12 +261,57 @@
     return jnp.dot(chosen, value, preferred_element_type=jnp.float32)
 
 
-def gradient(words, logit, arrived, order, student_cols, per_shard):
+def regroup(arrived):
+    sources, _, rows = arrived.shape
+
+    def kernel(in_ref, out_ref):
+        stats = [in_ref[j, 64:72, :] for j in range(sources)]
+
+        def common(at):
+            tops = [s[at : at + 1] for s in stats]
+            top = functools.reduce(jnp.maximum, tops)
+            weights = [jnp.exp(t - top) for t in tops]
+            total = sum(w * s[at + 1 : at + 2] for w, s in zip(weights, stats))
+            rest = sum(w * s[at + 2 : at + 3] for w, s in zip(weights, stats))
+            return weights, (top, total, rest)
+
+        weights, teacher = common(0)
+        _, student = common(3)
+        line = lax.broadcasted_iota(jnp.int32, (8, rows), 0)
+        sums = jnp.zeros((8, rows), jnp.float32)
+        for at, value in enumerate(teacher + student):
+            sums = jnp.where(line == at, value, sums)
+        block = jnp.zeros((32, 8, rows), jnp.float32)
+        for j in range(sources):
+            for slot in range(2):
+                e = in_ref[j, slot * 32 : (slot + 1) * 32, :] * weights[j]
+                block = jnp.where((line == 2 * j + slot)[None], e[:, None, :], block)
+        out_ref[:, :8, :] = block
+        out_ref[:, 8:, :] = jnp.broadcast_to(sums[None], (32, 8, rows))
+
+    return pl.pallas_call(
+        kernel,
+        out_shape=jax.ShapeDtypeStruct((32, 16, rows), jnp.float32),
+        compiler_params=pltpu.CompilerParams(vmem_limit_bytes=48 * 1024 * 1024),
+    )(arrived)
+
+
+def spread_sources(value, core, per_shard):
+    sources = value.shape[0]
+    tile = lax.broadcasted_iota(jnp.int32, (sources * per_shard, 1), 0)
+    arrival = lax.broadcasted_iota(jnp.int32, (1, sources), 1)
+    place, chip = arrival >> 5, arrival & 31
+    shard = jnp.where(core == 0, chip * 4 + place, (place * 8 + (chip & 7)) * 4 + (chip >> 3))
+    chosen = (((tile * 205) >> 10) == shard).astype(jnp.float32).astype(jnp.bfloat16)
+    return jnp.dot(chosen, value, preferred_element_type=jnp.float32)
+
+
+def gradient(slots, words, logit, arrived, order, student_cols, per_shard):
     cols, rows = logit.shape
     ds = student_cols.shape[0]
     width = 512
 
-    def kernel(word_ref, logit_ref, msg_ref, order_ref, w_hbm, out_ref, w_ref, w_sem):
+    def kernel(slot_ref, word_ref, logit_ref, msg_ref, order_ref, w_hbm, out_ref, w_ref, w_sem):
         copies = fetch(w_hbm, width, w_ref, w_sem)
 
         def sums(at):
@@ -266,15 +322,17 @@
             rest = jnp.sum(weight * msg_ref[:, at + 2, :], axis=0, keepdims=True)
             return top, weight, total, rest / total
 
-        _, t_weight, t_total, t_mass = sums(2)
-        s_top, _, s_total, s_mass = sums(5)
+        _, t_weight, t_total, t_mass = sums(8)
+        s_top, _, s_total, s_mass = sums(11)
         scale = t_weight / t_total
-        first = (msg_ref[:, 0, :] * scale).astype(jnp.bfloat16)
-        second = (msg_ref[:, 1, :] * scale).astype(jnp.bfloat16)
+
+        def arrived_prob(slot):
+            parts = [msg_ref[:, 2 * j + slot, :] * scale for j in range(4)]
+            prob = jnp.concatenate(parts, axis=0).astype(jnp.bfloat16)
+            return spread_sources(prob, slot_ref[2], per_shard)
+
         named, is_first = expand_words(word_ref[...], per_shard)
-        teacher = jnp.where(
-            is_first, spread_blocks(first, per_shard), spread_blocks(second, per_shard)
-        )
+        teacher = jnp.where(is_first, arrived_prob(0), arrived_prob(1))
         prob = jnp.exp(logit_ref[...] - s_top) / s_total
         kl = (
             jnp.where(named, prob - teacher, prob * (1.0 - t_mass / s_mass)) * loss_scale
@@ -292,7 +350,9 @@
     whole = pl.BlockSpec(memory_space=pltpu.VMEM)
     return pl.pallas_call(
         kernel,
-        in_specs=[whole] * 4 + [pl.BlockSpec(memory_space=pltpu.HBM)],
+        in_specs=[pl.BlockSpec(memory_space=pltpu.SMEM)]
+        + [whole] * 4
+        + [pl.BlockSpec(memory_space=pltpu.HBM)],
         out_specs=whole,
         out_shape=jax.ShapeDtypeStruct((rows, ds), jnp.bfloat16),
         scratch_shapes=[
@@ -300,7 +360,7 @@
             pltpu.SemaphoreType.DMA((ds // width,)),
         ],
         compiler_params=pltpu.CompilerParams(vmem_limit_bytes=48 * 1024 * 1024),
-    )(words, logit, arrived, order, student_cols)
+    )(slots, words, logit, arrived, order, student_cols)
 
 
 def per_device(teacher_hidden, teacher_head, student_hidden, student_head, tiles):
@@ -336,16 +396,17 @@
     own_word = lax.dynamic_slice_in_dim(words, shard_index, 1, 0)
 
     x, y = lax.axis_index("dp"), lax.axis_index("vocab") // NZ
-    slots = jnp.stack((jnp.where(core == 0, x, y), jnp.where(core == 0, y, x)))
+    slots = jnp.stack((jnp.where(core == 0, x, y), jnp.where(core == 0, y, x), core))
     message, logit = logits_and_message(
         slots, halves, teacher_head, student_cols, words, own_word, per_shard
     )
-    arrived = lax.all_to_all(message, LINE, 0, 0, tiled=True)
+    near = exchange(message, LINES_X[0] + LINES_Y[1])
+    arrived = exchange(regroup(near), PLANES_YZ + PLANES_XZ)
 
     order = lax.dynamic_index_in_dim(
         jnp.asarray(row_orders(), jnp.bfloat16), core, 0, keepdims=False
     )
-    partial = gradient(words, logit, arrived, order, student_cols, per_shard)
+    partial = gradient(slots, words, logit, arrived, order, student_cols, per_shard)
 
     rows = partial.shape[0]
     near = exchange(partial, LINES_X[0] + LINES_Y[1])

time: 154 us -> 148 us (0.961)
  waiting for transfers between devices: 39.8 us -> 27.6 us
  blocking collectives: 54 us -> 63.2 us
  starting transfers between devices: 31 us -> 28.1 us
    all_to_all x1, waiting for transfers between devices: 23.5 us -> 11.3 us  [exchange(): lax.all_to_all(value, WHOLE, 0, 0, tiled=True, axis_index_groups=groups)]
    all_to_all x3 -> x4, blocking collectives: 54 us -> 63.2 us  [exchange(): lax.all_to_all(value, WHOLE, 0, 0, tiled=True, axis_index_groups=groups)]
    all_to_all x1, starting transfers between devices: 8.88 us -> 4.63 us  [exchange(): lax.all_to_all(value, WHOLE, 0, 0, tiled=True, axis_index_groups=groups)]
    pallas_call x1 -> x2, Pallas kernels: 5.09 us -> 6.35 us  [the longest x1 5.3 us: gradient(): pl.pallas_call(kernel, in_specs=[pl.BlockSpec(memory_space=pltpu.SMEM)] +...]
where the time goes in v3:
time: 148 us; the launch traced here: 147 us
  blocking collectives  63.2 us (43%)
  starting transfers between devices  28.1 us (19%)
  waiting for transfers between devices  27.6 us (19%)
  Pallas kernels  21.2 us (14%)
  local copies, waits for them, and re-layouts  5.37 us (4%)
  other arithmetic  1.75 us (1%)
    all_to_all x4, blocking collectives, exchange(): lax.all_to_all(value, WHOLE, 0, 0, tiled=True, axis_index_groups=groups)  63.2 us
    ppermute x9, waiting for transfers between devices, step(): return lax.ppermute(value, WHOLE, pairs)  14.9 us
    ppermute x9, starting transfers between devices, step(): return lax.ppermute(value, WHOLE, pairs)  13.4 us
    all_to_all x1, waiting for transfers between devices, exchange(): lax.all_to_all(value, WHOLE, 0, 0, tiled=True, axis_index_groups=groups)  11.3 us
    pallas_call x1, Pallas kernels, logits_and_message(): pl.pallas_call(kernel, in_specs=[pl.BlockSpec(memory_space=pltpu.SMEM)] +...  10.2 us
    ppermute x1, starting transfers between devices, per_device(): return lax.ppermute(summed.astype(jnp.bfloat16), WHOLE, last_hop())  10.1 us
    pallas_call x1, Pallas kernels, gradient(): pl.pallas_call(kernel, in_specs=[pl.BlockSpec(memory_space=pltpu.SMEM)] +...  5.3 us
    pallas_call x1, Pallas kernels, tile_words(): pl.pallas_call(kernel, out_shape=jax.ShapeDtypeStruct((count, rows), jnp....  4.7 us
  transfers between devices with their start and end apart: 11, of which 8 were waited for; matrix products, arithmetic and copies ran while one was open for 1% of the time, Pallas kernels for 3%

profile of v3, /device:TPU:1, one launch (start us, length us, event | category | flops | bytes accessed | tf_op | source)
XLA Modules:
  0.0 147.4 jit_solution(13266137089489860501)
XLA Ops:
  0.0 0.9 fusion
  1.0 19.4 %all_to_all.37 = bf16[8,2,8704]{2,1,0:T(2,128)(2,1)S(1)} all-to-all(bf16[8,2,8704]{2,1,0:T(2,128)(2,1)S(1)} %broadcast_in_dim.2), channel_id=1, replica_groups={{0,4,8,12,16,20,24,28},{32,36,40,44,48,52,56,60},{64,68,72,76,80,84,88,..., dimensions={0} | all-to-all | bytes 557056 | tf_op jit(solution)/shard_map/all_to_all | solution.py:45
  20.6 2.6 %collective-permute-start.2 = (bf16[16,8704]{1,0:T(8,128)(2,1)S(1)}, bf16[16,8704]{1,0:T(8,128)(2,1)S(1)}, u32[]{:S(2)}, u32[]{:S(2)}) collective-permute-start(bf16[16,8704]{1,0:T(8,128)(2,1)S(1)} %all_to_all.25), channel_id=1, source_target_pairs={{0,96},{4,100},{8,104},{12,108},{16,112},{20,116},{24,120},{28,124... | collective-permute-start | bytes 835592 | tf_op jit(solution)/shard_map/ppermute | solution.py:65
  24.3 5.3 %collective-permute-done.2 = bf16[16,8704]{1,0:T(8,128)(2,1)S(1)} collective-permute-done((bf16[16,8704]{1,0:T(8,128)(2,1)S(1)}, bf16[16,8704]{1,0:T(8,128)(2,1)S(1)}, u32[]{:S(2)}, u32[]{:S(2)}) %collective-permute-start.2) | collective-permute-done | bytes 278560 | tf_op jit(solution)/shard_map/ppermute | solution.py:65
  30.1 3.0 %collective-permute-start.4 = (bf16[32,8704]{1,0:T(8,128)(2,1)S(1)}, bf16[32,8704]{1,0:T(8,128)(2,1)S(1)}, u32[]{:S(2)}, u32[]{:S(2)}) collective-permute-start(bf16[32,8704]{1,0:T(8,128)(2,1)S(1)} %constant_dynamic-update-slice_fusion.2.refs_1_), channel_id=1, source_target_pairs={{0,3},{4,7},{8,11},{12,15},{16,19},{20,23},{24,27},{28,31},{32,35}... | collective-permute-start | bytes 1671176 | tf_op jit(solution)/shard_map/ppermute | solution.py:65
  33.3 1.2 collective-permute-start.1
  35.3 4.7 %shard_map.64.refs_8_.word_ref = s32[128,256]{1,0:T(8,128)} custom-call(s32[128,256]{1,0:T(8,128)} %copy.17.tiles_ref), custom_call_target="tpu_custom_call" | custom-call | flops 67108864 | bytes 262144 | tf_op jit(solution)/shard_map/pallas_call | solution.py:121
  40.1 1.2 collective-permute-start.8
  41.2 1.5 %collective-permute-start.5 = (bf16[32,8704]{1,0:T(8,128)(2,1)S(1)}, bf16[32,8704]{1,0:T(8,128)(2,1)}, u32[]{:S(2)}, u32[]{:S(2)}) collective-permute-start(bf16[32,8704]{1,0:T(8,128)(2,1)S(1)} %constant_dynamic-update-slice_fusion.refs_0_), channel_id=1, source_target_pairs={{0,3},{4,7},{8,11},{12,15},{16,19},{20,23},{24,27},{28,31},{32,35}... | collective-permute-start | bytes 1671176 | tf_op jit(solution)/shard_map/ppermute | solution.py:65
  43.4 2.7 %collective-permute-start.7 = (bf16[32,8704]{1,0:T(8,128)(2,1)S(1)}, bf16[32,8704]{1,0:T(8,128)(2,1)}, u32[]{:S(2)}, u32[]{:S(2)}) collective-permute-start(bf16[32,8704]{1,0:T(8,128)(2,1)S(1)} %collective-permute-done.4.refs_3_), channel_id=1, source_target_pairs={{0,3},{4,7},{8,11},{12,15},{16,19},{20,23},{24,27},{28,31},{32,35}... | collective-permute-start | bytes 1671176 | tf_op jit(solution)/shard_map/ppermute | solution.py:65
  46.8 3.1 %collective-permute-done.8.refs_7_ = bf16[32,8704]{1,0:T(8,128)(2,1)S(1)} collective-permute-done((bf16[32,8704]{1,0:T(8,128)(2,1)S(1)}, bf16[32,8704]{1,0:T(8,128)(2,1)S(1)}, u32[]{:S(2)}, u32[]{:S(2)}) %collective-permute-start.8) | collective-permute-done | bytes 557088 | tf_op jit(solution)/shard_map/ppermute | solution.py:65
  50.8 5.2 %collective-permute-done.6.refs_4_ = bf16[32,8704]{1,0:T(8,128)(2,1)} collective-permute-done((bf16[32,8704]{1,0:T(8,128)(2,1)S(1)}, bf16[32,8704]{1,0:T(8,128)(2,1)}, u32[]{:S(2)}, u32[]{:S(2)}) %collective-permute-start.6) | collective-permute-done | bytes 557088 | tf_op jit(solution)/shard_map/ppermute | solution.py:65
  56.0 0.9 copy-done.1
  56.9 1.1 copy-done.4
  58.0 10.2 %shard_map.65 = (f32[4,72,256]{2,1,0:T(8,128)S(1)}, f32[640,256]{1,0:T(8,128)S(1)}) custom-call(s32[3]{0:T(128)S(1)} %pad_add_fusion.slot_ref, bf16[32,8704]{1,0:T(8,128)(2,1)S(1)} %constant_dynamic-update-slice_fusion.refs_0_, bf16[32,8704]{1,0:T(8,128)(2,1)S(1)} %constant_dynamic-update-slice_fusion.2.refs_1_, ...), custom_call_target="tpu_custom_call" | custom-call | tf_op jit(solution)/shard_map/pallas_call | solution.py:225
  68.2 9.5 %all_to_all.38.in_ref = f32[4,72,256]{2,1,0:T(8,128)S(1)} all-to-all(f32[4,72,256]{2,1,0:T(8,128)S(1)} %get-tuple-element.14), channel_id=1, replica_groups={{0,1,2,3},{4,5,6,7},{8,9,10,11},{12,13,14,15},{16,17,18,19},{20,21,22,2..., dimensions={0} | all-to-all | bytes 589824 | tf_op jit(solution)/shard_map/all_to_all | solution.py:45
  77.6 1.0 shard_map.66
  78.6 4.6 %all-to-all-start.2 = ((f32[32,16,256]{2,1,0:T(8,128)}), f32[32,16,256]{2,1,0:T(8,128)S(1)}, u32[]{:S(2)}, u32[]{:S(2)}) async-start(f32[32,16,256]{2,1,0:T(8,128)} %shard_map.66), calls=%async_computation.2 | async-start | bytes 1048576 | tf_op jit(solution)/shard_map/all_to_all | solution.py:45
  83.3 11.3 %all-to-all-done.2.msg_ref = f32[32,16,256]{2,1,0:T(8,128)S(1)} async-done(((f32[32,16,256]{2,1,0:T(8,128)}), f32[32,16,256]{2,1,0:T(8,128)S(1)}, u32[]{:S(2)}, u32[]{:S(2)}) %all-to-all-start.2) | async-done | bytes 524320 | tf_op jit(solution)/shard_map/all_to_all | solution.py:45
  94.7 5.3 %shard_map.67 = bf16[256,3584]{1,0:T(8,128)(2,1)S(1)} custom-call(s32[3]{0:T(128)S(1)} %pad_add_fusion.slot_ref, s32[128,256]{1,0:T(8,128)S(1)} %copy-done.2, f32[640,256]{1,0:T(8,128)S(1)} %get-tuple-element.13.logit_ref, f32[32,16,256]{2,1,0:T(8,128)S(1)} %all-to-all-done.2.msg_ref, bf16[256,256]{1,0:T(8,128)(2,1)S(1)} %dynamic-slice_bitcast_fusion.order_ref, ...), custom_call_target="tpu_custom_call" | custom-call | tf_op jit(solution)/shard_map/pallas_call | solution.py:351
  100.0 16.4 %all_to_all.39 = bf16[4,64,3584]{2,1,0:T(8,128)(2,1)S(1)} all-to-all(bf16[4,64,3584]{2,1,0:T(8,128)(2,1)S(1)} %bitcast.18), channel_id=1, replica_groups={{0,1,2,3},{4,5,6,7},{8,9,10,11},{12,13,14,15},{16,17,18,19},{20,21,22,2..., dimensions={0} | all-to-all | bytes 3670016 | tf_op jit(solution)/shard_map/all_to_all | solution.py:45
  117.0 17.9 %all_to_all.40 = bf16[32,2,3584]{2,1,0:T(2,128)(2,1)S(1)} all-to-all(bf16[32,2,3584]{2,1,0:T(2,128)(2,1)S(1)} %all_to_all.30), channel_id=1, replica_groups={{0,4,8,12,16,20,24,28,32,36,40,44,48,52,56,60,64,68,72,76,80,84,88,92,9..., dimensions={0} | all-to-all | bytes 917504 | tf_op jit(solution)/shard_map/all_to_all | solution.py:45
  135.2 10.1 %collective-permute-start.9 = (bf16[2,3584]{1,0:T(2,128)(2,1)S(1)}, bf16[2,3584]{1,0:T(2,128)(2,1)S(1)}, u32[]{:S(2)}, u32[]{:S(2)}) collective-permute-start(bf16[2,3584]{1,0:T(2,128)(2,1)S(1)} %reduce_sum.25), channel_id=1, source_target_pairs={{0,0},{4,4},{8,8},{12,12},{16,16},{20,20},{24,24},{28,28},{32,32},... | collective-permute-start | bytes 43016 | tf_op jit(solution)/shard_map/ppermute | solution.py:416
  145.4 1.4 collective-permute-done.9
  (34 shorter events, 6.7 us)
Async XLA Ops:
  0.0 34.5 %copy-start = (s32[512,128]{1,0:T(8,128)S(1)}, s32[512,128]{1,0:T(8,128)}, u32[]{:S(2)}) copy-start(s32[512,128]{1,0:T(8,128)} %param.10) | copy-start | bytes 786436
  20.6 9.0 %collective-permute-start.2 = (bf16[16,8704]{1,0:T(8,128)(2,1)S(1)}, bf16[16,8704]{1,0:T(8,128)(2,1)S(1)}, u32[]{:S(2)}, u32[]{:S(2)}) collective-permute-start(bf16[16,8704]{1,0:T(8,128)(2,1)S(1)} %all_to_all.25), channel_id=1, source_target_pairs={{0,96},{4,100},{8,104},{12,108},{16,112},{20,116},{24,120},{28,124... | collective-permute-start | bytes 835592 | tf_op jit(solution)/shard_map/ppermute | solution.py:65
  23.1 7.0 %collective-permute-start.3 = (bf16[16,8704]{1,0:T(8,128)(2,1)S(1)}, bf16[16,8704]{1,0:T(8,128)(2,1)S(1)}, u32[]{:S(2)}, u32[]{:S(2)}) collective-permute-start(bf16[16,8704]{1,0:T(8,128)(2,1)S(1)} %all_to_all.25), channel_id=1, source_target_pairs={{0,64},{4,68},{8,72},{12,76},{16,80},{20,84},{24,88},{28,92},{32,9... | collective-permute-start | bytes 835592 | tf_op jit(solution)/shard_map/ppermute | solution.py:65
  23.7 9.6 %collective-permute-start = (bf16[16,8704]{1,0:T(8,128)(2,1)S(1)}, bf16[16,8704]{1,0:T(8,128)(2,1)S(1)}, u32[]{:S(2)}, u32[]{:S(2)}) collective-permute-start(bf16[16,8704]{1,0:T(8,128)(2,1)S(1)} %all_to_all.25), channel_id=1, source_target_pairs={{0,32},{4,36},{8,40},{12,44},{16,48},{20,52},{24,56},{28,60},{32,6... | collective-permute-start | bytes 835592 | tf_op jit(solution)/shard_map/ppermute | solution.py:65
  30.1 12.6 %collective-permute-start.4 = (bf16[32,8704]{1,0:T(8,128)(2,1)S(1)}, bf16[32,8704]{1,0:T(8,128)(2,1)S(1)}, u32[]{:S(2)}, u32[]{:S(2)}) collective-permute-start(bf16[32,8704]{1,0:T(8,128)(2,1)S(1)} %constant_dynamic-update-slice_fusion.2.refs_1_), channel_id=1, source_target_pairs={{0,3},{4,7},{8,11},{12,15},{16,19},{20,23},{24,27},{28,31},{32,35}... | collective-permute-start | bytes 1671176 | tf_op jit(solution)/shard_map/ppermute | solution.py:65
  33.3 10.0 %collective-permute-start.1 = (bf16[32,8704]{1,0:T(8,128)(2,1)S(1)}, bf16[32,8704]{1,0:T(8,128)(2,1)S(1)}, u32[]{:S(2)}, u32[]{:S(2)}) collective-permute-start(bf16[32,8704]{1,0:T(8,128)(2,1)S(1)} %constant_dynamic-update-slice_fusion.refs_0_), channel_id=1, source_target_pairs={{0,1},{4,5},{8,9},{12,13},{16,17},{20,21},{24,25},{28,29},{32,33},... | collective-permute-start | bytes 1671176 | tf_op jit(solution)/shard_map/ppermute | solution.py:65
  40.1 9.9 %collective-permute-start.8 = (bf16[32,8704]{1,0:T(8,128)(2,1)S(1)}, bf16[32,8704]{1,0:T(8,128)(2,1)S(1)}, u32[]{:S(2)}, u32[]{:S(2)}) collective-permute-start(bf16[32,8704]{1,0:T(8,128)(2,1)S(1)} %constant_dynamic-update-slice_fusion.2.refs_1_), channel_id=1, source_target_pairs={{0,1},{4,5},{8,9},{12,13},{16,17},{20,21},{24,25},{28,29},{32,33},... | collective-permute-start | bytes 1671176 | tf_op jit(solution)/shard_map/ppermute | solution.py:65
  41.2 9.6 %collective-permute-start.5 = (bf16[32,8704]{1,0:T(8,128)(2,1)S(1)}, bf16[32,8704]{1,0:T(8,128)(2,1)}, u32[]{:S(2)}, u32[]{:S(2)}) collective-permute-start(bf16[32,8704]{1,0:T(8,128)(2,1)S(1)} %constant_dynamic-update-slice_fusion.refs_0_), channel_id=1, source_target_pairs={{0,3},{4,7},{8,11},{12,15},{16,19},{20,23},{24,27},{28,31},{32,35}... | collective-permute-start | bytes 1671176 | tf_op jit(solution)/shard_map/ppermute | solution.py:65
  43.4 12.7 %collective-permute-start.6 = (bf16[32,8704]{1,0:T(8,128)(2,1)S(1)}, bf16[32,8704]{1,0:T(8,128)(2,1)}, u32[]{:S(2)}, u32[]{:S(2)}) collective-permute-start(bf16[32,8704]{1,0:T(8,128)(2,1)S(1)} %collective-permute-done.1.refs_6_), channel_id=1, source_target_pairs={{0,1},{4,5},{8,9},{12,13},{16,17},{20,21},{24,25},{28,29},{32,33},... | collective-permute-start | bytes 1671176 | tf_op jit(solution)/shard_map/ppermute | solution.py:65
  43.4 12.7 %collective-permute-start.7 = (bf16[32,8704]{1,0:T(8,128)(2,1)S(1)}, bf16[32,8704]{1,0:T(8,128)(2,1)}, u32[]{:S(2)}, u32[]{:S(2)}) collective-permute-start(bf16[32,8704]{1,0:T(8,128)(2,1)S(1)} %collective-permute-done.4.refs_3_), channel_id=1, source_target_pairs={{0,3},{4,7},{8,11},{12,15},{16,19},{20,23},{24,27},{28,31},{32,35}... | collective-permute-start | bytes 1671176 | tf_op jit(solution)/shard_map/ppermute | solution.py:65
  49.9 0.8 copy-start.3
  56.0 0.9 copy-start.1
  56.9 1.1 copy-start.4
  58.0 25.3 %copy-start.5 = (bf16[2,256,256]{2,1,0:T(8,128)(2,1)S(1)}, bf16[2,256,256]{2,1,0:T(8,128)(2,1)}, u32[]{:S(2)}) copy-start(bf16[2,256,256]{2,1,0:T(8,128)(2,1)} %constant.52.clone) | copy-start | bytes 786436
  58.0 36.7 %copy-start.2 = (s32[128,256]{1,0:T(8,128)S(1)}, s32[128,256]{1,0:T(8,128)}, u32[]{:S(2)}) copy-start(s32[128,256]{1,0:T(8,128)} %shard_map.64.refs_8_.word_ref) | copy-start | bytes 393220
  78.6 16.0 %all-to-all-start.2 = ((f32[32,16,256]{2,1,0:T(8,128)}), f32[32,16,256]{2,1,0:T(8,128)S(1)}, u32[]{:S(2)}, u32[]{:S(2)}) async-start(f32[32,16,256]{2,1,0:T(8,128)} %shard_map.66), calls=%async_computation.2 | async-start | bytes 1048576 | tf_op jit(solution)/shard_map/all_to_all | solution.py:45
  135.2 11.5 %collective-permute-start.9 = (bf16[2,3584]{1,0:T(2,128)(2,1)S(1)}, bf16[2,3584]{1,0:T(2,128)(2,1)S(1)}, u32[]{:S(2)}, u32[]{:S(2)}) collective-permute-start(bf16[2,3584]{1,0:T(2,128)(2,1)S(1)} %reduce_sum.25), channel_id=1, source_target_pairs={{0,0},{4,4},{8,8},{12,12},{16,16},{20,20},{24,24},{28,28},{32,32},... | collective-permute-start | bytes 43016 | tf_op jit(solution)/shard_map/ppermute | solution.py:416

commit v4 on v3

--- a/solution.py
+++ b/solution.py
@@ -136,45 +136,90 @@
     return copies
 
 
-def logits_and_message(slots, halves, teacher_head, student_cols, words, own_word, per_shard):
+DEPTH = 512
+EARLY_LIMIT = 32 * 1024 * 1024
+GRADIENT_LIMIT = 48 * 1024 * 1024
+LATE_LIMIT = 16 * 1024 * 1024
+
+
+def add_logits(half_refs, t_ref, s_ref, out_ref, t_copies=(), s_copies=()):
+    cols = t_ref.shape[1]
+    at = 0
+    for copies, ref, col in ((t_copies, t_ref, slice(0, cols)), (s_copies, s_ref, slice(cols, 2 * cols))):
+        for k in range(ref.shape[0] // DEPTH):
+            left = jnp.concatenate([half[:, at : at + DEPTH] for half in half_refs], axis=0)
+            if copies:
+                copies[k].wait()
+            term = jnp.dot(
+                left, ref[k * DEPTH : (k + 1) * DEPTH, :], preferred_element_type=jnp.float32
+            )
+            if k == 0:
+                out_ref[:, col] = term
+            else:
+                out_ref[:, col] += term
+            at += DEPTH
+
+
+def logit_cost(rows, teacher_head, student_cols):
+    elements = teacher_head.size + student_cols.size
+    return pl.CostEstimate(
+        flops=2 * rows * elements, bytes_accessed=2 * elements, transcendentals=0
+    )
+
+
+def early_logits(halves, teacher_head, student_cols):
+    count = len(halves)
+    rows = count * halves[0].shape[0]
+    cols = teacher_head.shape[1]
+
+    def kernel(*refs):
+        t_hbm, s_hbm, out_ref, t_ref, s_ref, t_sem, s_sem = refs[count:]
+        t_copies = fetch(t_hbm, DEPTH, t_ref, t_sem)
+        s_copies = fetch(s_hbm, DEPTH, s_ref, s_sem)
+        add_logits(refs[:count], t_ref, s_ref, out_ref, t_copies, s_copies)
+
+    whole = pl.BlockSpec(memory_space=pltpu.VMEM)
+    return pl.pallas_call(
+        kernel,
+        in_specs=[whole] * count + [pl.BlockSpec(memory_space=pltpu.HBM)] * 2,
+        out_specs=[whole] * 3,
+        out_shape=[
+            jax.ShapeDtypeStruct((rows, 2 * cols), jnp.float32),
+            jax.ShapeDtypeStruct(teacher_head.shape, teacher_head.dtype),
+            jax.ShapeDtypeStruct(student_cols.shape, student_cols.dtype),
+        ],
+        scratch_shapes=[
+            pltpu.SemaphoreType.DMA((teacher_head.shape[0] // DEPTH,)),
+            pltpu.SemaphoreType.DMA((student_cols.shape[0] // DEPTH,)),
+        ],
+        cost_estimate=logit_cost(rows, teacher_head, student_cols),
+        compiler_params=pltpu.CompilerParams(vmem_limit_bytes=EARLY_LIMIT),
+    )(*halves, teacher_head, student_cols)
+
+
+def logits_and_message(slots, early, halves, teacher_head, student_cols, words, own_word, per_shard):
     count = len(halves)
     half = halves[0].shape[0]
-    rows = count * half
+    rows = 2 * count * half
     block = half // 2
     cols = teacher_head.shape[1]
     lanes = cols // per_shard
-    depth = 512
-    t_steps, s_steps = teacher_head.shape[0] // depth, student_cols.shape[0] // depth
-
-    def kernel(slot_ref, *refs):
-        half_refs = refs[:count]
+
+    def kernel(slot_ref, early_ref, *refs):
         (
-            word_ref, own_word_ref, t_hbm, s_hbm, msg_ref, logit_ref,
-            t_ref, s_ref, part_ref, all_ref, spare_ref, t_sem, s_sem,
+            word_ref, own_word_ref, t_ref, s_ref, msg_ref, logit_ref,
+            late_ref, all_ref, spare_ref,
         ) = refs[count:]
-        copies = fetch(t_hbm, depth, t_ref, t_sem) + fetch(s_hbm, depth, s_ref, s_sem)
-
-        for k in range(t_steps + s_steps):
-            left = jnp.concatenate(
-                [ref[:, k * depth : (k + 1) * depth] for ref in half_refs], axis=0
-            )
-            copies[k].wait()
-            if k < t_steps:
-                right, col = t_ref[k * depth : (k + 1) * depth, :], slice(0, cols)
-            else:
-                n = k - t_steps
-                right, col = s_ref[n * depth : (n + 1) * depth, :], slice(cols, 2 * cols)
-            term = jnp.dot(left, right, preferred_element_type=jnp.float32)
-            if k in (0, t_steps):
-                part_ref[:, col] = term
-            else:
-                part_ref[:, col] += term
-
-        for n in range(16):
-            third = lax.rem(slot_ref[0] + n // 4, 4)
-            second = lax.rem(slot_ref[1] + (0, 3, 1, 2)[n % 4], 4)
-            at = pl.multiple_of((third * 4 + second) * block, block)
-            all_ref[pl.ds(at, block), :] = part_ref[n * block : (n + 1) * block, :]
+        add_logits(refs[:count], t_ref, s_ref, late_ref)
+
+        for source_ref, places in ((early_ref, (0, 1, 3, 6)), (late_ref, (2, 4, 5, 7))):
+            for n, place in enumerate(places):
+                for k in range(2):
+                    third = lax.rem(slot_ref[0] + place // 2, 4)
+                    second = lax.rem(slot_ref[1] + (0, 3, 1, 2)[2 * (place % 2) + k], 4)
+                    at = pl.multiple_of((third * 4 + second) * block, block)
+                    start = n * half + k * block
+                    all_ref[pl.ds(at, block), :] = source_ref[start : start + block, :]
 
         word = own_word_ref[...]
         t_log = all_ref[:, :cols].T
@@ -221,26 +266,22 @@
             msg_ref[x, 64:72, :] = stats
 
     whole = pl.BlockSpec(memory_space=pltpu.VMEM)
-    remote = pl.BlockSpec(memory_space=pltpu.HBM)
     return pl.pallas_call(
         kernel,
-        in_specs=[pl.BlockSpec(memory_space=pltpu.SMEM)] + [whole] * (count + 2) + [remote] * 2,
+        in_specs=[pl.BlockSpec(memory_space=pltpu.SMEM)] + [whole] * (count + 5),
         out_specs=[whole, whole],
         out_shape=[
             jax.ShapeDtypeStruct((4, 72, rows), jnp.float32),
             jax.ShapeDtypeStruct((cols, rows), jnp.float32),
         ],
         scratch_shapes=[
-            pltpu.VMEM(teacher_head.shape, jnp.bfloat16),
-            pltpu.VMEM(student_cols.shape, jnp.bfloat16),
-            pltpu.VMEM((rows, 2 * cols), jnp.float32),
+            pltpu.VMEM((rows // 2, 2 * cols), jnp.float32),
             pltpu.VMEM((rows, 2 * cols), jnp.float32),
             pltpu.VMEM((rows // 128, 2 * lanes, 128), jnp.float32),
-            pltpu.SemaphoreType.DMA((t_steps,)),
-            pltpu.SemaphoreType.DMA((s_steps,)),
         ],
-        compiler_params=pltpu.CompilerParams(vmem_limit_bytes=48 * 1024 * 1024),
-    )(slots, *halves, words, own_word, teacher_head, student_cols)
+        cost_estimate=logit_cost(rows // 2, teacher_head, student_cols),
+        compiler_params=pltpu.CompilerParams(vmem_limit_bytes=LATE_LIMIT),
+    )(slots, early, *halves, words, own_word, teacher_head, student_cols)
 
 
 def expand_words(words, per_shard):
@@ -292,7 +333,7 @@
     return pl.pallas_call(
         kernel,
         out_shape=jax.ShapeDtypeStruct((32, 16, rows), jnp.float32),
-        compiler_params=pltpu.CompilerParams(vmem_limit_bytes=48 * 1024 * 1024),
+        compiler_params=pltpu.CompilerParams(vmem_limit_bytes=LATE_LIMIT),
     )(arrived)
 
 
@@ -310,8 +351,10 @@
     cols, rows = logit.shape
     ds = student_cols.shape[0]
     width = 512
-
-    def kernel(slot_ref, word_ref, logit_ref, msg_ref, order_ref, w_hbm, out_ref, w_ref, w_sem):
+    block = rows // 4
+
+    def kernel(slot_ref, word_ref, logit_ref, msg_ref, order_ref, w_hbm, *refs):
+        out_refs, (kl_ref, near_ref, w_ref, w_sem) = refs[:4], refs[4:]
         copies = fetch(w_hbm, width, w_ref, w_sem)
 
         def sums(at):
@@ -337,15 +380,23 @@
         kl = (
             jnp.where(named, prob - teacher, prob * (1.0 - t_mass / s_mass)) * loss_scale
         ).astype(jnp.bfloat16)
-        kl = lax.dot_general(
+        kl_ref[...] = lax.dot_general(
             order_ref[...], kl, (((1,), (1,)), ((), ())), preferred_element_type=jnp.float32
         ).astype(jnp.bfloat16)
+        for n in range(4):
+            at = pl.multiple_of(lax.rem(slot_ref[0] + n, 4) * block, block)
+            near_ref[n * block : (n + 1) * block, :] = kl_ref[pl.ds(at, block), :]
         for k in range(ds // width):
             span = slice(k * width, (k + 1) * width)
             copies[k].wait()
-            out_ref[:, span] = lax.dot_general(
-                kl, w_ref[span, :], (((1,), (1,)), ((), ())), preferred_element_type=jnp.float32
+            term = lax.dot_general(
+                near_ref[...],
+                w_ref[span, :],
+                (((1,), (1,)), ((), ())),
+                preferred_element_type=jnp.float32,
             ).astype(jnp.bfloat16)
+            for n in range(4):
+                out_refs[n][:, span] = term[n * block : (n + 1) * block, :]
 
     whole = pl.BlockSpec(memory_space=pltpu.VMEM)
     return pl.pallas_call(
@@ -353,13 +404,15 @@
         in_specs=[pl.BlockSpec(memory_space=pltpu.SMEM)]
         + [whole] * 4
         + [pl.BlockSpec(memory_space=pltpu.HBM)],
-        out_specs=whole,
-        out_shape=jax.ShapeDtypeStruct((rows, ds), jnp.bfloat16),
+        out_specs=[whole] * 4,
+        out_shape=[jax.ShapeDtypeStruct((block, ds), jnp.bfloat16)] * 4,
         scratch_shapes=[
+            pltpu.VMEM((rows, cols), jnp.bfloat16),
+            pltpu.VMEM((rows, cols), jnp.bfloat16),
             pltpu.VMEM(student_cols.shape, jnp.bfloat16),
             pltpu.SemaphoreType.DMA((ds // width,)),
         ],
-        compiler_params=pltpu.CompilerParams(vmem_limit_bytes=48 * 1024 * 1024),
+        compiler_params=pltpu.CompilerParams(vmem_limit_bytes=GRADIENT_LIMIT),
     )(slots, words, logit, arrived, order, student_cols)
 
 
@@ -382,6 +435,7 @@
     ).reshape(picks, 2 * shards)
     words = tile_words(tiles_t)
     last, after, opposite = across(gathered, 1), across(gathered, -1), across(gathered, 2)
+    opposite, words = lax.optimization_barrier((opposite, words))
     own = (
         jnp.concatenate((gathered, last), axis=0),
         jnp.concatenate((after, opposite), axis=0),
@@ -390,15 +444,15 @@
     above_first = along(own[1], -1)
     below_second = along(own[1], 1)
     above_second = along(own[0], -1)
-    below_first, above_first, words = lax.optimization_barrier((below_first, above_first, words))
     far = (along(below_first, 1), along(above_first, -1))
-    halves = own + (above_second, above_first) + far + (below_first, below_second)
+    early, teacher_near, student_near = early_logits(own + (above_first, below_first), teacher_head, student_cols)
+    late = (above_second,) + far + (below_second,)
     own_word = lax.dynamic_slice_in_dim(words, shard_index, 1, 0)
 
     x, y = lax.axis_index("dp"), lax.axis_index("vocab") // NZ
     slots = jnp.stack((jnp.where(core == 0, x, y), jnp.where(core == 0, y, x), core))
     message, logit = logits_and_message(
-        slots, halves, teacher_head, student_cols, words, own_word, per_shard
+        slots, early, late, teacher_near, student_near, words, own_word, per_shard
     )
     near = exchange(message, LINES_X[0] + LINES_Y[1])
     arrived = exchange(regroup(near), PLANES_YZ + PLANES_XZ)
@@ -406,11 +460,11 @@
     order = lax.dynamic_index_in_dim(
         jnp.asarray(row_orders(), jnp.bfloat16), core, 0, keepdims=False
     )
-    partial = gradient(slots, words, logit, arrived, order, student_cols, per_shard)
-
-    rows = partial.shape[0]
-    near = exchange(partial, LINES_X[0] + LINES_Y[1])
-    near = jnp.sum(near.reshape(NX, rows // NX, ds).astype(jnp.float32), axis=0)
+    kept, after_chip, opposite_chip, last_chip = gradient(
+        slots, words, logit, arrived, order, student_cols, per_shard
+    )
+    terms = (kept, along(opposite_chip, 2), along(after_chip, 1), along(last_chip, -1))
+    near = sum(term.astype(jnp.float32) for term in terms)
     far = exchange(near.astype(jnp.bfloat16), PLANES_YZ + PLANES_XZ)
     summed = jnp.sum(far.reshape(NY * NZ, 2, ds).astype(jnp.float32), axis=0)
     return lax.ppermute(summed.astype(jnp.bfloat16), WHOLE, last_hop())

time: 148 us -> 138 us (0.932)
  blocking collectives: 63.2 us -> 26.3 us
  waiting for transfers between devices: 27.6 us -> 40.8 us
  starting transfers between devices: 28.1 us -> 40.5 us
    all_to_all x4 -> x2, blocking collectives: 63.2 us -> 26.3 us  [exchange(): lax.all_to_all(value, WHOLE, 0, 0, tiled=True, axis_index_groups=groups)]
    all_to_all x1 -> x2, starting transfers between devices: 4.63 us -> 14.1 us  [exchange(): lax.all_to_all(value, WHOLE, 0, 0, tiled=True, axis_index_groups=groups)]
    ppermute x9 -> x12, waiting for transfers between devices: 14.9 us -> 22.3 us  [step(): return lax.ppermute(value, WHOLE, pairs)]
    pallas_call x0 -> x1, Pallas kernels: none -> 7.41 us  [early_logits(): pl.pallas_call(kernel, in_specs=[whole] * count + [pl.BlockSpec(memory_sp...]
    pallas_call x1, Pallas kernels: 10.2 us -> 4.02 us  [logits_and_message(): pl.pallas_call(kernel, in_specs=[pl.BlockSpec(memory_space=pltpu.SMEM)] +...]
    all_to_all x1 -> x2, waiting for transfers between devices: 11.3 us -> 17.1 us  [exchange(): lax.all_to_all(value, WHOLE, 0, 0, tiled=True, axis_index_groups=groups)]
    ppermute x9 -> x12, starting transfers between devices: 13.4 us -> 16.1 us  [step(): return lax.ppermute(value, WHOLE, pairs)]
    unnamed x15 -> x11, local copies, waits for them, and re-layouts: 3.44 us -> 2.95 us
  transfers between devices with their start and end apart: 11 -> 15, of which waited for: 8 -> 9; matrix products, arithmetic and copies ran while one was open for 1% -> 1% of each run, Pallas kernels for 3% -> 9%
where the time goes in v4:
time: 138 us; the launch traced here: 137 us
  waiting for transfers between devices  40.8 us (30%)
  starting transfers between devices  40.5 us (29%)
  blocking collectives  26.3 us (19%)
  Pallas kernels  22.5 us (16%)
  local copies, waits for them, and re-layouts  5.58 us (4%)
  other arithmetic  1.61 us (1%)
    all_to_all x2, blocking collectives, exchange(): lax.all_to_all(value, WHOLE, 0, 0, tiled=True, axis_index_groups=groups)  26.3 us
    ppermute x12, waiting for transfers between devices, step(): return lax.ppermute(value, WHOLE, pairs)  22.3 us
    all_to_all x2, waiting for transfers between devices, exchange(): lax.all_to_all(value, WHOLE, 0, 0, tiled=True, axis_index_groups=groups)  17.1 us
    ppermute x12, starting transfers between devices, step(): return lax.ppermute(value, WHOLE, pairs)  16.1 us
    all_to_all x2, starting transfers between devices, exchange(): lax.all_to_all(value, WHOLE, 0, 0, tiled=True, axis_index_groups=groups)  14.1 us
    ppermute x1, starting transfers between devices, per_device(): return lax.ppermute(summed.astype(jnp.bfloat16), WHOLE, last_hop())  10.2 us
    pallas_call x1, Pallas kernels, early_logits(): pl.pallas_call(kernel, in_specs=[whole] * count + [pl.BlockSpec(memory_sp...  7.41 us
    pallas_call x1, Pallas kernels, gradient(): pl.pallas_call(kernel, in_specs=[pl.BlockSpec(memory_space=pltpu.SMEM)] +...  5.29 us
  transfers between devices with their start and end apart: 15, of which 9 were waited for; matrix products, arithmetic and copies ran while one was open for 1% of the time, Pallas kernels for 9%

profile of v4, /device:TPU:1, one launch (start us, length us, event | category | flops | bytes accessed | tf_op | source)
XLA Modules:
  0.0 137.4 jit_solution(13093148878548660422)
XLA Ops:
  1.7 9.0 %all-to-all-start = ((bf16[8,2,8704]{2,1,0:T(2,128)(2,1)}), bf16[8,2,8704]{2,1,0:T(2,128)(2,1)S(1)}, u32[]{:S(2)}, u32[]{:S(2)}) async-start(bf16[8,2,8704]{2,1,0:T(2,128)(2,1)} %broadcast_in_dim.2), calls=%async_computation | async-start | bytes 557056 | tf_op jit(solution)/shard_map/all_to_all | solution.py:45
  11.6 4.7 %shard_map.64.refs_4_.word_ref = s32[128,256]{1,0:T(8,128)} custom-call(s32[128,256]{1,0:T(8,128)} %copy.11.tiles_ref), custom_call_target="tpu_custom_call" | custom-call | flops 67108864 | bytes 262144 | tf_op jit(solution)/shard_map/pallas_call | solution.py:121
  16.3 5.3 %all-to-all-done = bf16[8,2,8704]{2,1,0:T(2,128)(2,1)S(1)} async-done(((bf16[8,2,8704]{2,1,0:T(2,128)(2,1)}), bf16[8,2,8704]{2,1,0:T(2,128)(2,1)S(1)}, u32[]{:S(2)}, u32[]{:S(2)}) %all-to-all-start) | async-done | bytes 278560 | tf_op jit(solution)/shard_map/all_to_all | solution.py:45
  21.6 2.8 %collective-permute-start = (bf16[16,8704]{1,0:T(8,128)(2,1)S(1)}, bf16[16,8704]{1,0:T(8,128)(2,1)S(1)}, u32[]{:S(2)}, u32[]{:S(2)}) collective-permute-start(bf16[16,8704]{1,0:T(8,128)(2,1)S(1)} %all_to_all.19), channel_id=1, source_target_pairs={{0,64},{4,68},{8,72},{12,76},{16,80},{20,84},{24,88},{28,92},{32,9... | collective-permute-start | bytes 835592 | tf_op jit(solution)/shard_map/ppermute | solution.py:65
  26.0 2.9 %collective-permute-done = bf16[16,8704]{1,0:T(8,128)(2,1)S(1)} collective-permute-done((bf16[16,8704]{1,0:T(8,128)(2,1)S(1)}, bf16[16,8704]{1,0:T(8,128)(2,1)S(1)}, u32[]{:S(2)}, u32[]{:S(2)}) %collective-permute-start) | collective-permute-done | bytes 278560 | tf_op jit(solution)/shard_map/ppermute | solution.py:65
  28.9 2.8 %collective-permute-done.2 = bf16[16,8704]{1,0:T(8,128)(2,1)S(1)} collective-permute-done((bf16[16,8704]{1,0:T(8,128)(2,1)S(1)}, bf16[16,8704]{1,0:T(8,128)(2,1)S(1)}, u32[]{:S(2)}, u32[]{:S(2)}) %collective-permute-start.2) | collective-permute-done | bytes 278560 | tf_op jit(solution)/shard_map/ppermute | solution.py:65
  31.8 3.1 %collective-permute-start.3 = (bf16[32,8704]{1,0:T(8,128)(2,1)S(1)}, bf16[32,8704]{1,0:T(8,128)(2,1)S(1)}, u32[]{:S(2)}, u32[]{:S(2)}) collective-permute-start(bf16[32,8704]{1,0:T(8,128)(2,1)S(1)} %constant_dynamic-update-slice_fusion.2.refs_1_), channel_id=1, source_target_pairs={{0,3},{4,7},{8,11},{12,15},{16,19},{20,23},{24,27},{28,31},{32,35}... | collective-permute-start | bytes 1671176 | tf_op jit(solution)/shard_map/ppermute | solution.py:65
  35.1 2.7 %collective-permute-start.5 = (bf16[32,8704]{1,0:T(8,128)(2,1)S(1)}, bf16[32,8704]{1,0:T(8,128)(2,1)S(1)}, u32[]{:S(2)}, u32[]{:S(2)}) collective-permute-start(bf16[32,8704]{1,0:T(8,128)(2,1)S(1)} %constant_dynamic-update-slice_fusion.refs_0_), channel_id=1, source_target_pairs={{0,3},{4,7},{8,11},{12,15},{16,19},{20,23},{24,27},{28,31},{32,35}... | collective-permute-start | bytes 1671176 | tf_op jit(solution)/shard_map/ppermute | solution.py:65
  37.8 3.6 %collective-permute-done.3.refs_2_ = bf16[32,8704]{1,0:T(8,128)(2,1)S(1)} collective-permute-done((bf16[32,8704]{1,0:T(8,128)(2,1)S(1)}, bf16[32,8704]{1,0:T(8,128)(2,1)S(1)}, u32[]{:S(2)}, u32[]{:S(2)}) %collective-permute-start.3) | collective-permute-done | bytes 557088 | tf_op jit(solution)/shard_map/ppermute | solution.py:65
  41.4 3.1 %collective-permute-start.7 = (bf16[32,8704]{1,0:T(8,128)(2,1)S(1)}, bf16[32,8704]{1,0:T(8,128)(2,1)}, u32[]{:S(2)}, u32[]{:S(2)}) collective-permute-start(bf16[32,8704]{1,0:T(8,128)(2,1)S(1)} %collective-permute-done.3.refs_2_), channel_id=1, source_target_pairs={{0,3},{4,7},{8,11},{12,15},{16,19},{20,23},{24,27},{28,31},{32,35}... | collective-permute-start | bytes 1671176 | tf_op jit(solution)/shard_map/ppermute | solution.py:65
  45.8 2.3 %copy-done.1 = bf16[3584,640,1]{1,0,2:T(8,128)(2,1)S(1)} copy-done((bf16[3584,640,1]{1,0,2:T(8,128)(2,1)S(1)}, bf16[3584,640,1]{1,0,2:T(8,128)(2,1)}, u32[]{:S(2)}) %copy-start.1) | copy-done | bytes 4587544
  48.1 7.4 %shard_map.65 = (f32[128,1280]{1,0:T(8,128)S(1)}, bf16[5120,640]{1,0:T(8,128)(2,1)S(1)}, bf16[3584,640]{1,0:T(8,128)(2,1)S(1)}) custom-call(bf16[32,8704]{1,0:T(8,128)(2,1)S(1)} %constant_dynamic-update-slice_fusion.refs_0_, bf16[32,8704]{1,0:T(8,128)(2,1)S(1)} %constant_dynamic-update-slice_fusion.2.refs_1_, ...), custom_call_target="tpu_custom_call" | custom-call | flops 1426063360 | bytes 11141120 | tf_op jit(solution)/shard_map/pallas_call | solution.py:182
  55.5 1.4 %collective-permute-done.6.refs_1_ = bf16[32,8704]{1,0:T(8,128)(2,1)} collective-permute-done((bf16[32,8704]{1,0:T(8,128)(2,1)}, bf16[32,8704]{1,0:T(8,128)(2,1)}, u32[]{:S(2)}, u32[]{:S(2)}) %collective-permute-start.6) | collective-permute-done | bytes 557088 | tf_op jit(solution)/shard_map/ppermute | solution.py:65
  56.9 4.0 %shard_map.66 = (f32[4,72,256]{2,1,0:T(8,128)S(1)}, f32[640,256]{1,0:T(8,128)S(1)}) custom-call(s32[3]{0:T(128)S(1)} %pad_add_fusion.slot_ref, f32[128,1280]{1,0:T(8,128)S(1)} %get-tuple-element.18.early_ref, bf16[32,8704]{1,0:T(8,128)(2,1)S(1)} %collective-permute-done.5.refs_0_, bf16[32,8704]{1,0:T(8,128)(2,1)} %collective-permute-done.6.refs_1_, ...), custom_call_target="tpu_custom_call" | custom-call | flops 1426063360 | bytes 11141120 | tf_op jit(solution)/shard_map/pallas_call | solution.py:269
  61.0 8.1 %all_to_all.28.in_ref = f32[4,72,256]{2,1,0:T(8,128)S(1)} all-to-all(f32[4,72,256]{2,1,0:T(8,128)S(1)} %get-tuple-element.22), channel_id=1, replica_groups={{0,1,2,3},{4,5,6,7},{8,9,10,11},{12,13,14,15},{16,17,18,19},{20,21,22,2..., dimensions={0} | all-to-all | bytes 589824 | tf_op jit(solution)/shard_map/all_to_all | solution.py:45
  69.0 1.1 shard_map.67
  70.1 5.1 %all-to-all-start.2 = ((f32[32,16,256]{2,1,0:T(8,128)}), f32[32,16,256]{2,1,0:T(8,128)S(1)}, u32[]{:S(2)}, u32[]{:S(2)}) async-start(f32[32,16,256]{2,1,0:T(8,128)} %shard_map.67), calls=%async_computation.2 | async-start | bytes 1048576 | tf_op jit(solution)/shard_map/all_to_all | solution.py:45
  75.2 11.8 %all-to-all-done.2.msg_ref = f32[32,16,256]{2,1,0:T(8,128)S(1)} async-done(((f32[32,16,256]{2,1,0:T(8,128)}), f32[32,16,256]{2,1,0:T(8,128)S(1)}, u32[]{:S(2)}, u32[]{:S(2)}) %all-to-all-start.2) | async-done | bytes 524320 | tf_op jit(solution)/shard_map/all_to_all | solution.py:45
  87.0 5.3 %shard_map.68 = (bf16[64,3584]{1,0:T(8,128)(2,1)S(1)}, bf16[64,3584]{1,0:T(8,128)(2,1)S(1)}, bf16[64,3584]{1,0:T(8,128)(2,1)S(1)}, bf16[64,3584]{1,0:T(8,128)(2,1)S(1)}) custom-call(s32[3]{0:T(128)S(1)} %pad_add_fusion.slot_ref, s32[128,256]{1,0:T(8,128)S(1)} %copy-done.2, f32[640,256]{1,0:T(8,128)S(1)} %get-tuple-element.21.logit_ref, ...), custom_call_target="tpu_custom_call" | custom-call | tf_op jit(solution)/shard_map/pallas_call | solution.py:402
  92.4 2.7 %collective-permute-start.11 = (bf16[64,3584]{1,0:T(8,128)(2,1)S(1)}, bf16[64,3584]{1,0:T(8,128)(2,1)S(1)}, u32[]{:S(2)}, u32[]{:S(2)}) collective-permute-start(bf16[64,3584]{1,0:T(8,128)(2,1)S(1)} %get-tuple-element.26), channel_id=1, source_target_pairs={{0,3},{4,7},{8,11},{12,15},{16,19},{20,23},{24,27},{28,31},{32,35}... | collective-permute-start | bytes 1376264 | tf_op jit(solution)/shard_map/ppermute | solution.py:65
  95.1 11.1 %collective-permute-done.10 = bf16[64,3584]{1,0:T(8,128)(2,1)S(1)} collective-permute-done((bf16[64,3584]{1,0:T(8,128)(2,1)S(1)}, bf16[64,3584]{1,0:T(8,128)(2,1)S(1)}, u32[]{:S(2)}, u32[]{:S(2)}) %collective-permute-start.10) | collective-permute-done | bytes 458784 | tf_op jit(solution)/shard_map/ppermute | solution.py:65
  106.6 18.3 %all_to_all.29 = bf16[32,2,3584]{2,1,0:T(2,128)(2,1)S(1)} all-to-all(bf16[32,2,3584]{2,1,0:T(2,128)(2,1)S(1)} %all_to_all.22), channel_id=1, replica_groups={{0,4,8,12,16,20,24,28,32,36,40,44,48,52,56,60,64,68,72,76,80,84,88,92,9..., dimensions={0} | all-to-all | bytes 917504 | tf_op jit(solution)/shard_map/all_to_all | solution.py:45
  125.2 10.2 %collective-permute-start.12 = (bf16[2,3584]{1,0:T(2,128)(2,1)S(1)}, bf16[2,3584]{1,0:T(2,128)(2,1)S(1)}, u32[]{:S(2)}, u32[]{:S(2)}) collective-permute-start(bf16[2,3584]{1,0:T(2,128)(2,1)S(1)} %reduce_sum.12), channel_id=1, source_target_pairs={{0,0},{4,4},{8,8},{12,12},{16,16},{20,20},{24,24},{28,28},{32,32},... | collective-permute-start | bytes 43016 | tf_op jit(solution)/shard_map/ppermute | solution.py:470
  135.4 1.4 %collective-permute-done.12 = bf16[2,3584]{1,0:T(2,128)(2,1)S(1)} collective-permute-done((bf16[2,3584]{1,0:T(2,128)(2,1)S(1)}, bf16[2,3584]{1,0:T(2,128)(2,1)S(1)}, u32[]{:S(2)}, u32[]{:S(2)}) %collective-permute-start.12) | collective-permute-done | bytes 14368 | tf_op jit(solution)/shard_map/ppermute | solution.py:470
  (37 shorter events, 7.2 us)
Async XLA Ops:
  0.0 10.7 %copy-start = (s32[512,128]{1,0:T(8,128)S(1)}, s32[512,128]{1,0:T(8,128)}, u32[]{:S(2)}) copy-start(s32[512,128]{1,0:T(8,128)} %param.10) | copy-start | bytes 786436
  1.7 19.8 %all-to-all-start = ((bf16[8,2,8704]{2,1,0:T(2,128)(2,1)}), bf16[8,2,8704]{2,1,0:T(2,128)(2,1)S(1)}, u32[]{:S(2)}, u32[]{:S(2)}) async-start(bf16[8,2,8704]{2,1,0:T(2,128)(2,1)} %broadcast_in_dim.2), calls=%async_computation | async-start | bytes 557056 | tf_op jit(solution)/shard_map/all_to_all | solution.py:45
  21.6 7.3 %collective-permute-start = (bf16[16,8704]{1,0:T(8,128)(2,1)S(1)}, bf16[16,8704]{1,0:T(8,128)(2,1)S(1)}, u32[]{:S(2)}, u32[]{:S(2)}) collective-permute-start(bf16[16,8704]{1,0:T(8,128)(2,1)S(1)} %all_to_all.19), channel_id=1, source_target_pairs={{0,64},{4,68},{8,72},{12,76},{16,80},{20,84},{24,88},{28,92},{32,9... | collective-permute-start | bytes 835592 | tf_op jit(solution)/shard_map/ppermute | solution.py:65
  24.5 7.3 %collective-permute-start.2 = (bf16[16,8704]{1,0:T(8,128)(2,1)S(1)}, bf16[16,8704]{1,0:T(8,128)(2,1)S(1)}, u32[]{:S(2)}, u32[]{:S(2)}) collective-permute-start(bf16[16,8704]{1,0:T(8,128)(2,1)S(1)} %all_to_all.19), channel_id=1, source_target_pairs={{0,96},{4,100},{8,104},{12,108},{16,112},{20,116},{24,120},{28,124... | collective-permute-start | bytes 835592 | tf_op jit(solution)/shard_map/ppermute | solution.py:65
  25.4 9.6 %collective-permute-start.1 = (bf16[16,8704]{1,0:T(8,128)(2,1)S(1)}, bf16[16,8704]{1,0:T(8,128)(2,1)S(1)}, u32[]{:S(2)}, u32[]{:S(2)}) collective-permute-start(bf16[16,8704]{1,0:T(8,128)(2,1)S(1)} %all_to_all.19), channel_id=1, source_target_pairs={{0,32},{4,36},{8,40},{12,44},{16,48},{20,52},{24,56},{28,60},{32,6... | collective-permute-start | bytes 835592 | tf_op jit(solution)/shard_map/ppermute | solution.py:65
  31.8 9.6 %collective-permute-start.3 = (bf16[32,8704]{1,0:T(8,128)(2,1)S(1)}, bf16[32,8704]{1,0:T(8,128)(2,1)S(1)}, u32[]{:S(2)}, u32[]{:S(2)}) collective-permute-start(bf16[32,8704]{1,0:T(8,128)(2,1)S(1)} %constant_dynamic-update-slice_fusion.2.refs_1_), channel_id=1, source_target_pairs={{0,3},{4,7},{8,11},{12,15},{16,19},{20,23},{24,27},{28,31},{32,35}... | collective-permute-start | bytes 1671176 | tf_op jit(solution)/shard_map/ppermute | solution.py:65
  34.9 10.1 %collective-permute-start.4 = (bf16[32,8704]{1,0:T(8,128)(2,1)S(1)}, bf16[32,8704]{1,0:T(8,128)(2,1)}, u32[]{:S(2)}, u32[]{:S(2)}) collective-permute-start(bf16[32,8704]{1,0:T(8,128)(2,1)S(1)} %constant_dynamic-update-slice_fusion.refs_0_), channel_id=1, source_target_pairs={{0,1},{4,5},{8,9},{12,13},{16,17},{20,21},{24,25},{28,29},{32,33},... | collective-permute-start | bytes 1671176 | tf_op jit(solution)/shard_map/ppermute | solution.py:65
  35.0 20.5 %collective-permute-start.8 = (bf16[32,8704]{1,0:T(8,128)(2,1)S(1)}, bf16[32,8704]{1,0:T(8,128)(2,1)S(1)}, u32[]{:S(2)}, u32[]{:S(2)}) collective-permute-start(bf16[32,8704]{1,0:T(8,128)(2,1)S(1)} %constant_dynamic-update-slice_fusion.2.refs_1_), channel_id=1, source_target_pairs={{0,1},{4,5},{8,9},{12,13},{16,17},{20,21},{24,25},{28,29},{32,33},... | collective-permute-start | bytes 1671176 | tf_op jit(solution)/shard_map/ppermute | solution.py:65
  35.1 20.4 %collective-permute-start.5 = (bf16[32,8704]{1,0:T(8,128)(2,1)S(1)}, bf16[32,8704]{1,0:T(8,128)(2,1)S(1)}, u32[]{:S(2)}, u32[]{:S(2)}) collective-permute-start(bf16[32,8704]{1,0:T(8,128)(2,1)S(1)} %constant_dynamic-update-slice_fusion.refs_0_), channel_id=1, source_target_pairs={{0,3},{4,7},{8,11},{12,15},{16,19},{20,23},{24,27},{28,31},{32,35}... | collective-permute-start | bytes 1671176 | tf_op jit(solution)/shard_map/ppermute | solution.py:65
  41.4 14.1 %collective-permute-start.7 = (bf16[32,8704]{1,0:T(8,128)(2,1)S(1)}, bf16[32,8704]{1,0:T(8,128)(2,1)}, u32[]{:S(2)}, u32[]{:S(2)}) collective-permute-start(bf16[32,8704]{1,0:T(8,128)(2,1)S(1)} %collective-permute-done.3.refs_2_), channel_id=1, source_target_pairs={{0,3},{4,7},{8,11},{12,15},{16,19},{20,23},{24,27},{28,31},{32,35}... | collective-permute-start | bytes 1671176 | tf_op jit(solution)/shard_map/ppermute | solution.py:65
  45.0 11.9 %collective-permute-start.6 = (bf16[32,8704]{1,0:T(8,128)(2,1)}, bf16[32,8704]{1,0:T(8,128)(2,1)}, u32[]{:S(2)}, u32[]{:S(2)}) collective-permute-start(bf16[32,8704]{1,0:T(8,128)(2,1)} %collective-permute-done.4.refs_3_), channel_id=1, source_target_pairs={{0,1},{4,5},{8,9},{12,13},{16,17},{20,21},{24,25},{28,29},{32,33},... | collective-permute-start | bytes 1671176 | tf_op jit(solution)/shard_map/ppermute | solution.py:65
  45.8 2.3 %copy-start.1 = (bf16[3584,640,1]{1,0,2:T(8,128)(2,1)S(1)}, bf16[3584,640,1]{1,0,2:T(8,128)(2,1)}, u32[]{:S(2)}) copy-start(bf16[3584,640,1]{1,0,2:T(8,128)(2,1)} %param.9) | copy-start | bytes 13762564
  48.1 8.9 %copy-start.2 = (s32[128,256]{1,0:T(8,128)S(1)}, s32[128,256]{1,0:T(8,128)}, u32[]{:S(2)}) copy-start(s32[128,256]{1,0:T(8,128)} %shard_map.64.refs_4_.word_ref) | copy-start | bytes 393220
  56.9 18.3 %copy-start.3 = (bf16[2,256,256]{2,1,0:T(8,128)(2,1)S(1)}, bf16[2,256,256]{2,1,0:T(8,128)(2,1)}, u32[]{:S(2)}) copy-start(bf16[2,256,256]{2,1,0:T(8,128)(2,1)} %constant.51.clone) | copy-start | bytes 786436
  70.1 16.9 %all-to-all-start.2 = ((f32[32,16,256]{2,1,0:T(8,128)}), f32[32,16,256]{2,1,0:T(8,128)S(1)}, u32[]{:S(2)}, u32[]{:S(2)}) async-start(f32[32,16,256]{2,1,0:T(8,128)} %shard_map.67), calls=%async_computation.2 | async-start | bytes 1048576 | tf_op jit(solution)/shard_map/all_to_all | solution.py:45
  92.3 13.8 %collective-permute-start.10 = (bf16[64,3584]{1,0:T(8,128)(2,1)S(1)}, bf16[64,3584]{1,0:T(8,128)(2,1)S(1)}, u32[]{:S(2)}, u32[]{:S(2)}) collective-permute-start(bf16[64,3584]{1,0:T(8,128)(2,1)S(1)} %get-tuple-element.25), channel_id=1, source_target_pairs={{0,1},{4,5},{8,9},{12,13},{16,17},{20,21},{24,25},{28,29},{32,33},... | collective-permute-start | bytes 1376264 | tf_op jit(solution)/shard_map/ppermute | solution.py:65
  92.4 13.7 %collective-permute-start.11 = (bf16[64,3584]{1,0:T(8,128)(2,1)S(1)}, bf16[64,3584]{1,0:T(8,128)(2,1)S(1)}, u32[]{:S(2)}, u32[]{:S(2)}) collective-permute-start(bf16[64,3584]{1,0:T(8,128)(2,1)S(1)} %get-tuple-element.26), channel_id=1, source_target_pairs={{0,3},{4,7},{8,11},{12,15},{16,19},{20,23},{24,27},{28,31},{32,35}... | collective-permute-start | bytes 1376264 | tf_op jit(solution)/shard_map/ppermute | solution.py:65
  95.1 11.1 %collective-permute-start.9 = (bf16[64,3584]{1,0:T(8,128)(2,1)S(1)}, bf16[64,3584]{1,0:T(8,128)(2,1)S(1)}, u32[]{:S(2)}, u32[]{:S(2)}) collective-permute-start(bf16[64,3584]{1,0:T(8,128)(2,1)S(1)} %get-tuple-element.24), channel_id=1, source_target_pairs={{0,2},{4,6},{8,10},{12,14},{16,18},{20,22},{24,26},{28,30},{32,34}... | collective-permute-start | bytes 1376264 | tf_op jit(solution)/shard_map/ppermute | solution.py:65
  125.2 11.6 %collective-permute-start.12 = (bf16[2,3584]{1,0:T(2,128)(2,1)S(1)}, bf16[2,3584]{1,0:T(2,128)(2,1)S(1)}, u32[]{:S(2)}, u32[]{:S(2)}) collective-permute-start(bf16[2,3584]{1,0:T(2,128)(2,1)S(1)} %reduce_sum.12), channel_id=1, source_target_pairs={{0,0},{4,4},{8,8},{12,12},{16,16},{20,20},{24,24},{28,28},{32,32},... | collective-permute-start | bytes 43016 | tf_op jit(solution)/shard_map/ppermute | solution.py:470

commit v5 on v4

--- a/solution.py
+++ b/solution.py
@@ -200,14 +200,14 @@
 def logits_and_message(slots, early, halves, teacher_head, student_cols, words, own_word, per_shard):
     count = len(halves)
     half = halves[0].shape[0]
-    rows = 2 * count * half
+    rows = early.shape[0] + count * half
     block = half // 2
     cols = teacher_head.shape[1]
     lanes = cols // per_shard
 
     def kernel(slot_ref, early_ref, *refs):
         (
-            word_ref, own_word_ref, t_ref, s_ref, msg_ref, logit_ref,
+            word_ref, own_word_ref, t_ref, s_ref, *msg_refs, logit_ref,
             late_ref, all_ref, spare_ref,
         ) = refs[count:]
         add_logits(refs[:count], t_ref, s_ref, late_ref)
@@ -252,34 +252,31 @@
         for part in range(rows // 128):
             spare_ref[part, :lanes, :] = first[:, part * 128 : (part + 1) * 128]
             spare_ref[part, lanes:, :] = second[:, part * 128 : (part + 1) * 128]
-        core = slot_ref[2]
-        for x in range(4):
-            for y in range(4):
-                to = jnp.where(core == 0, x, y)
-                at = 8 * jnp.where(core == 0, y, x)
+        for n in range(4):
+            to = lax.rem(slot_ref[0] + n, 4)
+            for r in range(4):
+                x = jnp.where(slot_ref[2] == 0, to, r)
+                y = jnp.where(slot_ref[2] == 0, r, to)
                 for slot in range(2):
-                    lines = pl.ds(pl.multiple_of(slot * 32 + at, 8), 8)
                     for part in range(rows // 128):
-                        msg_ref[to, lines, part * 128 : (part + 1) * 128] = spare_ref[
-                            part, pl.ds(slot * lanes + y * 32 + x, 8, stride=4), :
-                        ]
-            msg_ref[x, 64:72, :] = stats
+                        msg_refs[n][
+                            slot * 32 + 8 * r : slot * 32 + 8 * r + 8, part * 128 : (part + 1) * 128
+                        ] = spare_ref[part, pl.ds(slot * lanes + y * 32 + x, 8, stride=4), :]
+            msg_refs[n][64:72, :] = stats
 
     whole = pl.BlockSpec(memory_space=pltpu.VMEM)
     return pl.pallas_call(
         kernel,
         in_specs=[pl.BlockSpec(memory_space=pltpu.SMEM)] + [whole] * (count + 5),
-        out_specs=[whole, whole],
-        out_shape=[
-            jax.ShapeDtypeStruct((4, 72, rows), jnp.float32),
-            jax.ShapeDtypeStruct((cols, rows), jnp.float32),
-        ],
+        out_specs=[whole] * 5,
+        out_shape=[jax.ShapeDtypeStruct((72, rows), jnp.float32)] * 4
+        + [jax.ShapeDtypeStruct((cols, rows), jnp.float32)],
         scratch_shapes=[
-            pltpu.VMEM((rows // 2, 2 * cols), jnp.float32),
+            pltpu.VMEM((count * half, 2 * cols), jnp.float32),
             pltpu.VMEM((rows, 2 * cols), jnp.float32),
             pltpu.VMEM((rows // 128, 2 * lanes, 128), jnp.float32),
         ],
-        cost_estimate=logit_cost(rows // 2, teacher_head, student_cols),
+        cost_estimate=logit_cost(count * half, teacher_head, student_cols),
         compiler_params=pltpu.CompilerParams(vmem_limit_bytes=LATE_LIMIT),
     )(slots, early, *halves, words, own_word, teacher_head, student_cols)
 
@@ -303,10 +300,12 @@
 
 
 def regroup(arrived):
-    sources, _, rows = arrived.shape
-
-    def kernel(in_ref, out_ref):
-        stats = [in_ref[j, 64:72, :] for j in range(sources)]
+    sources = len(arrived)
+    rows = arrived[0].shape[1]
+
+    def kernel(*refs):
+        in_refs, out_ref = refs[:sources], refs[sources]
+        stats = [ref[64:72, :] for ref in in_refs]
 
         def common(at):
             tops = [s[at : at + 1] for s in stats]
@@ -325,7 +324,7 @@
         block = jnp.zeros((32, 8, rows), jnp.float32)
         for j in range(sources):
             for slot in range(2):
-                e = in_ref[j, slot * 32 : (slot + 1) * 32, :] * weights[j]
+                e = in_refs[j][slot * 32 : (slot + 1) * 32, :] * weights[j]
                 block = jnp.where((line == 2 * j + slot)[None], e[:, None, :], block)
         out_ref[:, :8, :] = block
         out_ref[:, 8:, :] = jnp.broadcast_to(sums[None], (32, 8, rows))
@@ -334,15 +333,15 @@
         kernel,
         out_shape=jax.ShapeDtypeStruct((32, 16, rows), jnp.float32),
         compiler_params=pltpu.CompilerParams(vmem_limit_bytes=LATE_LIMIT),
-    )(arrived)
-
-
-def spread_sources(value, core, per_shard):
+    )(*arrived)
+
+
+def spread_sources(value, slot_ref, per_shard):
     sources = value.shape[0]
     tile = lax.broadcasted_iota(jnp.int32, (sources * per_shard, 1), 0)
     arrival = lax.broadcasted_iota(jnp.int32, (1, sources), 1)
-    place, chip = arrival >> 5, arrival & 31
-    shard = jnp.where(core == 0, chip * 4 + place, (place * 8 + (chip & 7)) * 4 + (chip >> 3))
+    place, chip = (slot_ref[0] + 4 - (arrival >> 5)) & 3, arrival & 31
+    shard = jnp.where(slot_ref[2] == 0, chip * 4 + place, (place * 8 + (chip & 7)) * 4 + (chip >> 3))
     chosen = (((tile * 205) >> 10) == shard).astype(jnp.float32).astype(jnp.bfloat16)
     return jnp.dot(chosen, value, preferred_element_type=jnp.float32)
 
@@ -372,11 +371,11 @@
         def arrived_prob(slot):
             parts = [msg_ref[:, 2 * j + slot, :] * scale for j in range(4)]
             prob = jnp.concatenate(parts, axis=0).astype(jnp.bfloat16)
-            return spread_sources(prob, slot_ref[2], per_shard)
+            return spread_sources(prob, slot_ref, per_shard)
 
         named, is_first = expand_words(word_ref[...], per_shard)
         teacher = jnp.where(is_first, arrived_prob(0), arrived_prob(1))
-        prob = jnp.exp(logit_ref[...] - s_top) / s_total
+        prob = jnp.exp(logit_ref[...] - s_top) * (1.0 / s_total)
         kl = (
             jnp.where(named, prob - teacher, prob * (1.0 - t_mass / s_mass)) * loss_scale
         ).astype(jnp.bfloat16)
@@ -445,16 +444,20 @@
     below_second = along(own[1], 1)
     above_second = along(own[0], -1)
     far = (along(below_first, 1), along(above_first, -1))
-    early, teacher_near, student_near = early_logits(own + (above_first, below_first), teacher_head, student_cols)
+    early, teacher_near, student_near = early_logits(
+        own + (above_first, below_first), teacher_head, student_cols
+    )
     late = (above_second,) + far + (below_second,)
     own_word = lax.dynamic_slice_in_dim(words, shard_index, 1, 0)
 
     x, y = lax.axis_index("dp"), lax.axis_index("vocab") // NZ
     slots = jnp.stack((jnp.where(core == 0, x, y), jnp.where(core == 0, y, x), core))
-    message, logit = logits_and_message(
+    *message, logit = logits_and_message(
         slots, early, late, teacher_near, student_near, words, own_word, per_shard
     )
-    near = exchange(message, LINES_X[0] + LINES_Y[1])
+    near = (
+        message[0], along(message[1], 1), along(message[2], 2), along(message[3], -1),
+    )
     arrived = exchange(regroup(near), PLANES_YZ + PLANES_XZ)
 
     order = lax.dynamic_index_in_dim(

time: 138 us -> 134 us (0.971)
  blocking collectives: 26.3 us -> 18 us
  waiting for transfers between devices: 40.8 us -> 43.9 us
    all_to_all x2 -> x1, blocking collectives: 26.3 us -> 18 us  [exchange(): lax.all_to_all(value, WHOLE, 0, 0, tiled=True, axis_index_groups=groups)]
    ppermute x12 -> x15, waiting for transfers between devices: 22.3 us -> 25.7 us  [step(): return lax.ppermute(value, WHOLE, pairs)]
    ppermute x12 -> x15, starting transfers between devices: 16.1 us -> 19 us  [step(): return lax.ppermute(value, WHOLE, pairs)]
    ppermute x1, starting transfers between devices: 10.2 us -> 8.66 us  [per_device(): return lax.ppermute(summed.astype(jnp.bfloat16), WHOLE, last_hop())]
  transfers between devices with their start and end apart: 15 -> 18, of which waited for: 9 -> 12; matrix products, arithmetic and copies ran while one was open for 1% -> 1% of each run, Pallas kernels for 9% -> 9%
where the time goes in v5:
time: 134 us; the launch traced here: 133 us
  waiting for transfers between devices  43.9 us (33%)
  starting transfers between devices  41.6 us (31%)
  Pallas kernels  22.5 us (17%)
  blocking collectives  18 us (13%)
  local copies, waits for them, and re-layouts  5.59 us (4%)
  other arithmetic  1.61 us (1%)
    ppermute x15, waiting for transfers between devices, step(): return lax.ppermute(value, WHOLE, pairs)  25.7 us
    ppermute x15, starting transfers between devices, step(): return lax.ppermute(value, WHOLE, pairs)  19 us
    all_to_all x1, blocking collectives, exchange(): lax.all_to_all(value, WHOLE, 0, 0, tiled=True, axis_index_groups=groups)  18 us
    all_to_all x2, waiting for transfers between devices, exchange(): lax.all_to_all(value, WHOLE, 0, 0, tiled=True, axis_index_groups=groups)  16.8 us
    all_to_all x2, starting transfers between devices, exchange(): lax.all_to_all(value, WHOLE, 0, 0, tiled=True, axis_index_groups=groups)  14 us
    ppermute x1, starting transfers between devices, per_device(): return lax.ppermute(summed.astype(jnp.bfloat16), WHOLE, last_hop())  8.66 us
    pallas_call x1, Pallas kernels, early_logits(): pl.pallas_call(kernel, in_specs=[whole] * count + [pl.BlockSpec(memory_sp...  7.41 us
    pallas_call x1, Pallas kernels, gradient(): pl.pallas_call(kernel, in_specs=[pl.BlockSpec(memory_space=pltpu.SMEM)] +...  5.26 us
  transfers between devices with their start and end apart: 18, of which 12 were waited for; matrix products, arithmetic and copies ran while one was open for 1% of the time, Pallas kernels for 9%

profile of v5, /device:TPU:1, one launch (start us, length us, event | category | flops | bytes accessed | tf_op | source)
XLA Modules:
  0.0 133.4 jit_solution(5376129053091093046)
XLA Ops:
  1.7 9.0 %all-to-all-start = ((bf16[8,2,8704]{2,1,0:T(2,128)(2,1)}), bf16[8,2,8704]{2,1,0:T(2,128)(2,1)S(1)}, u32[]{:S(2)}, u32[]{:S(2)}) async-start(bf16[8,2,8704]{2,1,0:T(2,128)(2,1)} %broadcast_in_dim.2), calls=%async_computation | async-start | bytes 557056 | tf_op jit(solution)/shard_map/all_to_all | solution.py:45
  11.6 4.7 %shard_map.64.refs_4_.word_ref = s32[128,256]{1,0:T(8,128)} custom-call(s32[128,256]{1,0:T(8,128)} %copy.11.tiles_ref), custom_call_target="tpu_custom_call" | custom-call | flops 67108864 | bytes 262144 | tf_op jit(solution)/shard_map/pallas_call | solution.py:121
  16.3 5.3 %all-to-all-done = bf16[8,2,8704]{2,1,0:T(2,128)(2,1)S(1)} async-done(((bf16[8,2,8704]{2,1,0:T(2,128)(2,1)}), bf16[8,2,8704]{2,1,0:T(2,128)(2,1)S(1)}, u32[]{:S(2)}, u32[]{:S(2)}) %all-to-all-start) | async-done | bytes 278560 | tf_op jit(solution)/shard_map/all_to_all | solution.py:45
  21.7 2.8 %collective-permute-start = (bf16[16,8704]{1,0:T(8,128)(2,1)S(1)}, bf16[16,8704]{1,0:T(8,128)(2,1)S(1)}, u32[]{:S(2)}, u32[]{:S(2)}) collective-permute-start(bf16[16,8704]{1,0:T(8,128)(2,1)S(1)} %all_to_all.16), channel_id=1, source_target_pairs={{0,64},{4,68},{8,72},{12,76},{16,80},{20,84},{24,88},{28,92},{32,9... | collective-permute-start | bytes 835592 | tf_op jit(solution)/shard_map/ppermute | solution.py:65
  26.1 2.9 %collective-permute-done = bf16[16,8704]{1,0:T(8,128)(2,1)S(1)} collective-permute-done((bf16[16,8704]{1,0:T(8,128)(2,1)S(1)}, bf16[16,8704]{1,0:T(8,128)(2,1)S(1)}, u32[]{:S(2)}, u32[]{:S(2)}) %collective-permute-start) | collective-permute-done | bytes 278560 | tf_op jit(solution)/shard_map/ppermute | solution.py:65
  28.9 2.8 %collective-permute-done.2 = bf16[16,8704]{1,0:T(8,128)(2,1)S(1)} collective-permute-done((bf16[16,8704]{1,0:T(8,128)(2,1)S(1)}, bf16[16,8704]{1,0:T(8,128)(2,1)S(1)}, u32[]{:S(2)}, u32[]{:S(2)}) %collective-permute-start.2) | collective-permute-done | bytes 278560 | tf_op jit(solution)/shard_map/ppermute | solution.py:65
  31.8 3.1 %collective-permute-start.3 = (bf16[32,8704]{1,0:T(8,128)(2,1)S(1)}, bf16[32,8704]{1,0:T(8,128)(2,1)S(1)}, u32[]{:S(2)}, u32[]{:S(2)}) collective-permute-start(bf16[32,8704]{1,0:T(8,128)(2,1)S(1)} %constant_dynamic-update-slice_fusion.2.refs_1_), channel_id=1, source_target_pairs={{0,3},{4,7},{8,11},{12,15},{16,19},{20,23},{24,27},{28,31},{32,35}... | collective-permute-start | bytes 1671176 | tf_op jit(solution)/shard_map/ppermute | solution.py:65
  35.1 2.7 %collective-permute-start.5 = (bf16[32,8704]{1,0:T(8,128)(2,1)S(1)}, bf16[32,8704]{1,0:T(8,128)(2,1)S(1)}, u32[]{:S(2)}, u32[]{:S(2)}) collective-permute-start(bf16[32,8704]{1,0:T(8,128)(2,1)S(1)} %constant_dynamic-update-slice_fusion.refs_0_), channel_id=1, source_target_pairs={{0,3},{4,7},{8,11},{12,15},{16,19},{20,23},{24,27},{28,31},{32,35}... | collective-permute-start | bytes 1671176 | tf_op jit(solution)/shard_map/ppermute | solution.py:65
  37.8 3.6 %collective-permute-done.3.refs_2_ = bf16[32,8704]{1,0:T(8,128)(2,1)S(1)} collective-permute-done((bf16[32,8704]{1,0:T(8,128)(2,1)S(1)}, bf16[32,8704]{1,0:T(8,128)(2,1)S(1)}, u32[]{:S(2)}, u32[]{:S(2)}) %collective-permute-start.3) | collective-permute-done | bytes 557088 | tf_op jit(solution)/shard_map/ppermute | solution.py:65
  41.4 3.1 %collective-permute-start.7 = (bf16[32,8704]{1,0:T(8,128)(2,1)S(1)}, bf16[32,8704]{1,0:T(8,128)(2,1)}, u32[]{:S(2)}, u32[]{:S(2)}) collective-permute-start(bf16[32,8704]{1,0:T(8,128)(2,1)S(1)} %collective-permute-done.3.refs_2_), channel_id=1, source_target_pairs={{0,3},{4,7},{8,11},{12,15},{16,19},{20,23},{24,27},{28,31},{32,35}... | collective-permute-start | bytes 1671176 | tf_op jit(solution)/shard_map/ppermute | solution.py:65
  45.8 2.3 %copy-done.1 = bf16[3584,640,1]{1,0,2:T(8,128)(2,1)S(1)} copy-done((bf16[3584,640,1]{1,0,2:T(8,128)(2,1)S(1)}, bf16[3584,640,1]{1,0,2:T(8,128)(2,1)}, u32[]{:S(2)}) %copy-start.1) | copy-done | bytes 4587544
  48.1 7.4 %shard_map.65 = (f32[128,1280]{1,0:T(8,128)S(1)}, bf16[5120,640]{1,0:T(8,128)(2,1)S(1)}, bf16[3584,640]{1,0:T(8,128)(2,1)S(1)}) custom-call(bf16[32,8704]{1,0:T(8,128)(2,1)S(1)} %constant_dynamic-update-slice_fusion.refs_0_, bf16[32,8704]{1,0:T(8,128)(2,1)S(1)} %constant_dynamic-update-slice_fusion.2.refs_1_, ...), custom_call_target="tpu_custom_call" | custom-call | flops 1426063360 | bytes 11141120 | tf_op jit(solution)/shard_map/pallas_call | solution.py:182
  55.5 1.4 %collective-permute-done.6.refs_1_ = bf16[32,8704]{1,0:T(8,128)(2,1)} collective-permute-done((bf16[32,8704]{1,0:T(8,128)(2,1)}, bf16[32,8704]{1,0:T(8,128)(2,1)}, u32[]{:S(2)}, u32[]{:S(2)}) %collective-permute-start.6) | collective-permute-done | bytes 557088 | tf_op jit(solution)/shard_map/ppermute | solution.py:65
  57.0 4.0 %shard_map.66 = (f32[72,256]{1,0:T(8,128)S(1)}, f32[72,256]{1,0:T(8,128)S(1)}, f32[72,256]{1,0:T(8,128)S(1)}, f32[72,256]{1,0:T(8,128)S(1)}, f32[640,256]{1,0:T(8,128)S(1)}) custom-call(s32[3]{0:T(128)S(1)} %pad_add_fusion.slot_ref, f32[128,1280]{1,0:T(8,128)S(1)} %get-tuple-element.21.early_ref, bf16[32,8704]{1,0:T(8,128)(2,1)S(1)} %collective-permute-done.5.refs_0_, ...), custom_call_target="tpu_custom_call" | custom-call | flops 1426063360 | bytes 11141120 | tf_op jit(solution)/shard_map/pallas_call | solution.py:268
  63.0 2.8 %collective-permute-done.10.refs_2_ = f32[72,256]{1,0:T(8,128)S(1)} collective-permute-done((f32[72,256]{1,0:T(8,128)S(1)}, f32[72,256]{1,0:T(8,128)S(1)}, u32[]{:S(2)}, u32[]{:S(2)}) %collective-permute-start.10) | collective-permute-done | bytes 73760 | tf_op jit(solution)/shard_map/ppermute | solution.py:65
  67.9 5.0 %all-to-all-start.1 = ((f32[32,16,256]{2,1,0:T(8,128)}), f32[32,16,256]{2,1,0:T(8,128)S(1)}, u32[]{:S(2)}, u32[]{:S(2)}) async-start(f32[32,16,256]{2,1,0:T(8,128)} %shard_map.67), calls=%async_computation.1 | async-start | bytes 1048576 | tf_op jit(solution)/shard_map/all_to_all | solution.py:45
  73.0 11.6 %all-to-all-done.1.msg_ref = f32[32,16,256]{2,1,0:T(8,128)S(1)} async-done(((f32[32,16,256]{2,1,0:T(8,128)}), f32[32,16,256]{2,1,0:T(8,128)S(1)}, u32[]{:S(2)}, u32[]{:S(2)}) %all-to-all-start.1) | async-done | bytes 524320 | tf_op jit(solution)/shard_map/all_to_all | solution.py:45
  84.6 5.3 %shard_map.68 = (bf16[64,3584]{1,0:T(8,128)(2,1)S(1)}, bf16[64,3584]{1,0:T(8,128)(2,1)S(1)}, bf16[64,3584]{1,0:T(8,128)(2,1)S(1)}, bf16[64,3584]{1,0:T(8,128)(2,1)S(1)}) custom-call(s32[3]{0:T(128)S(1)} %pad_add_fusion.slot_ref, s32[128,256]{1,0:T(8,128)S(1)} %copy-done.2, f32[640,256]{1,0:T(8,128)S(1)} %get-tuple-element.24.logit_ref, ...), custom_call_target="tpu_custom_call" | custom-call | tf_op jit(solution)/shard_map/pallas_call | solution.py:401
  91.1 2.4 %collective-permute-start.14 = (bf16[64,3584]{1,0:T(8,128)(2,1)S(1)}, bf16[64,3584]{1,0:T(8,128)(2,1)S(1)}, u32[]{:S(2)}, u32[]{:S(2)}) collective-permute-start(bf16[64,3584]{1,0:T(8,128)(2,1)S(1)} %get-tuple-element.32), channel_id=1, source_target_pairs={{0,3},{4,7},{8,11},{12,15},{16,19},{20,23},{24,27},{28,31},{32,35}... | collective-permute-start | bytes 1376264 | tf_op jit(solution)/shard_map/ppermute | solution.py:65
  93.4 5.4 %collective-permute-done.12 = bf16[64,3584]{1,0:T(8,128)(2,1)S(1)} collective-permute-done((bf16[64,3584]{1,0:T(8,128)(2,1)S(1)}, bf16[64,3584]{1,0:T(8,128)(2,1)S(1)}, u32[]{:S(2)}, u32[]{:S(2)}) %collective-permute-start.12) | collective-permute-done | bytes 458784 | tf_op jit(solution)/shard_map/ppermute | solution.py:65
  98.9 5.1 %collective-permute-done.13 = bf16[64,3584]{1,0:T(8,128)(2,1)S(1)} collective-permute-done((bf16[64,3584]{1,0:T(8,128)(2,1)S(1)}, bf16[64,3584]{1,0:T(8,128)(2,1)S(1)}, u32[]{:S(2)}, u32[]{:S(2)}) %collective-permute-start.13) | collective-permute-done | bytes 458784 | tf_op jit(solution)/shard_map/ppermute | solution.py:65
  104.4 18.0 %all_to_all.23 = bf16[32,2,3584]{2,1,0:T(2,128)(2,1)S(1)} all-to-all(bf16[32,2,3584]{2,1,0:T(2,128)(2,1)S(1)} %all_to_all.18), channel_id=1, replica_groups={{0,4,8,12,16,20,24,28,32,36,40,44,48,52,56,60,64,68,72,76,80,84,88,92,9..., dimensions={0} | all-to-all | bytes 917504 | tf_op jit(solution)/shard_map/all_to_all | solution.py:45
  122.8 8.7 %collective-permute-start.15 = (bf16[2,3584]{1,0:T(2,128)(2,1)S(1)}, bf16[2,3584]{1,0:T(2,128)(2,1)S(1)}, u32[]{:S(2)}, u32[]{:S(2)}) collective-permute-start(bf16[2,3584]{1,0:T(2,128)(2,1)S(1)} %reduce_sum.12), channel_id=1, source_target_pairs={{0,0},{4,4},{8,8},{12,12},{16,16},{20,20},{24,24},{28,28},{32,32},... | collective-permute-start | bytes 43016 | tf_op jit(solution)/shard_map/ppermute | solution.py:473
  131.4 1.4 %collective-permute-done.15 = bf16[2,3584]{1,0:T(2,128)(2,1)S(1)} collective-permute-done((bf16[2,3584]{1,0:T(2,128)(2,1)S(1)}, bf16[2,3584]{1,0:T(2,128)(2,1)S(1)}, u32[]{:S(2)}, u32[]{:S(2)}) %collective-permute-start.15) | collective-permute-done | bytes 14368 | tf_op jit(solution)/shard_map/ppermute | solution.py:473
  (42 shorter events, 12.5 us)
Async XLA Ops:
  0.0 10.8 %copy-start = (s32[512,128]{1,0:T(8,128)S(1)}, s32[512,128]{1,0:T(8,128)}, u32[]{:S(2)}) copy-start(s32[512,128]{1,0:T(8,128)} %param.10) | copy-start | bytes 786436
  1.7 19.8 %all-to-all-start = ((bf16[8,2,8704]{2,1,0:T(2,128)(2,1)}), bf16[8,2,8704]{2,1,0:T(2,128)(2,1)S(1)}, u32[]{:S(2)}, u32[]{:S(2)}) async-start(bf16[8,2,8704]{2,1,0:T(2,128)(2,1)} %broadcast_in_dim.2), calls=%async_computation | async-start | bytes 557056 | tf_op jit(solution)/shard_map/all_to_all | solution.py:45
  21.7 7.3 %collective-permute-start = (bf16[16,8704]{1,0:T(8,128)(2,1)S(1)}, bf16[16,8704]{1,0:T(8,128)(2,1)S(1)}, u32[]{:S(2)}, u32[]{:S(2)}) collective-permute-start(bf16[16,8704]{1,0:T(8,128)(2,1)S(1)} %all_to_all.16), channel_id=1, source_target_pairs={{0,64},{4,68},{8,72},{12,76},{16,80},{20,84},{24,88},{28,92},{32,9... | collective-permute-start | bytes 835592 | tf_op jit(solution)/shard_map/ppermute | solution.py:65
  24.5 7.3 %collective-permute-start.2 = (bf16[16,8704]{1,0:T(8,128)(2,1)S(1)}, bf16[16,8704]{1,0:T(8,128)(2,1)S(1)}, u32[]{:S(2)}, u32[]{:S(2)}) collective-permute-start(bf16[16,8704]{1,0:T(8,128)(2,1)S(1)} %all_to_all.16), channel_id=1, source_target_pairs={{0,96},{4,100},{8,104},{12,108},{16,112},{20,116},{24,120},{28,124... | collective-permute-start | bytes 835592 | tf_op jit(solution)/shard_map/ppermute | solution.py:65
  25.4 9.6 %collective-permute-start.1 = (bf16[16,8704]{1,0:T(8,128)(2,1)S(1)}, bf16[16,8704]{1,0:T(8,128)(2,1)S(1)}, u32[]{:S(2)}, u32[]{:S(2)}) collective-permute-start(bf16[16,8704]{1,0:T(8,128)(2,1)S(1)} %all_to_all.16), channel_id=1, source_target_pairs={{0,32},{4,36},{8,40},{12,44},{16,48},{20,52},{24,56},{28,60},{32,6... | collective-permute-start | bytes 835592 | tf_op jit(solution)/shard_map/ppermute | solution.py:65
  31.8 9.6 %collective-permute-start.3 = (bf16[32,8704]{1,0:T(8,128)(2,1)S(1)}, bf16[32,8704]{1,0:T(8,128)(2,1)S(1)}, u32[]{:S(2)}, u32[]{:S(2)}) collective-permute-start(bf16[32,8704]{1,0:T(8,128)(2,1)S(1)} %constant_dynamic-update-slice_fusion.2.refs_1_), channel_id=1, source_target_pairs={{0,3},{4,7},{8,11},{12,15},{16,19},{20,23},{24,27},{28,31},{32,35}... | collective-permute-start | bytes 1671176 | tf_op jit(solution)/shard_map/ppermute | solution.py:65
  34.9 10.1 %collective-permute-start.4 = (bf16[32,8704]{1,0:T(8,128)(2,1)S(1)}, bf16[32,8704]{1,0:T(8,128)(2,1)}, u32[]{:S(2)}, u32[]{:S(2)}) collective-permute-start(bf16[32,8704]{1,0:T(8,128)(2,1)S(1)} %constant_dynamic-update-slice_fusion.refs_0_), channel_id=1, source_target_pairs={{0,1},{4,5},{8,9},{12,13},{16,17},{20,21},{24,25},{28,29},{32,33},... | collective-permute-start | bytes 1671176 | tf_op jit(solution)/shard_map/ppermute | solution.py:65
  35.0 20.5 %collective-permute-start.8 = (bf16[32,8704]{1,0:T(8,128)(2,1)S(1)}, bf16[32,8704]{1,0:T(8,128)(2,1)S(1)}, u32[]{:S(2)}, u32[]{:S(2)}) collective-permute-start(bf16[32,8704]{1,0:T(8,128)(2,1)S(1)} %constant_dynamic-update-slice_fusion.2.refs_1_), channel_id=1, source_target_pairs={{0,1},{4,5},{8,9},{12,13},{16,17},{20,21},{24,25},{28,29},{32,33},... | collective-permute-start | bytes 1671176 | tf_op jit(solution)/shard_map/ppermute | solution.py:65
  35.1 20.4 %collective-permute-start.5 = (bf16[32,8704]{1,0:T(8,128)(2,1)S(1)}, bf16[32,8704]{1,0:T(8,128)(2,1)S(1)}, u32[]{:S(2)}, u32[]{:S(2)}) collective-permute-start(bf16[32,8704]{1,0:T(8,128)(2,1)S(1)} %constant_dynamic-update-slice_fusion.refs_0_), channel_id=1, source_target_pairs={{0,3},{4,7},{8,11},{12,15},{16,19},{20,23},{24,27},{28,31},{32,35}... | collective-permute-start | bytes 1671176 | tf_op jit(solution)/shard_map/ppermute | solution.py:65
  41.4 14.1 %collective-permute-start.7 = (bf16[32,8704]{1,0:T(8,128)(2,1)S(1)}, bf16[32,8704]{1,0:T(8,128)(2,1)}, u32[]{:S(2)}, u32[]{:S(2)}) collective-permute-start(bf16[32,8704]{1,0:T(8,128)(2,1)S(1)} %collective-permute-done.3.refs_2_), channel_id=1, source_target_pairs={{0,3},{4,7},{8,11},{12,15},{16,19},{20,23},{24,27},{28,31},{32,35}... | collective-permute-start | bytes 1671176 | tf_op jit(solution)/shard_map/ppermute | solution.py:65
  45.0 11.9 %collective-permute-start.6 = (bf16[32,8704]{1,0:T(8,128)(2,1)}, bf16[32,8704]{1,0:T(8,128)(2,1)}, u32[]{:S(2)}, u32[]{:S(2)}) collective-permute-start(bf16[32,8704]{1,0:T(8,128)(2,1)} %collective-permute-done.4.refs_3_), channel_id=1, source_target_pairs={{0,1},{4,5},{8,9},{12,13},{16,17},{20,21},{24,25},{28,29},{32,33},... | collective-permute-start | bytes 1671176 | tf_op jit(solution)/shard_map/ppermute | solution.py:65
  45.8 2.3 %copy-start.1 = (bf16[3584,640,1]{1,0,2:T(8,128)(2,1)S(1)}, bf16[3584,640,1]{1,0,2:T(8,128)(2,1)}, u32[]{:S(2)}) copy-start(bf16[3584,640,1]{1,0,2:T(8,128)(2,1)} %param.9) | copy-start | bytes 13762564
  48.1 8.9 %copy-start.2 = (s32[128,256]{1,0:T(8,128)S(1)}, s32[128,256]{1,0:T(8,128)}, u32[]{:S(2)}) copy-start(s32[128,256]{1,0:T(8,128)} %shard_map.64.refs_4_.word_ref) | copy-start | bytes 393220
  57.0 16.0 %copy-start.3 = (bf16[2,256,256]{2,1,0:T(8,128)(2,1)S(1)}, bf16[2,256,256]{2,1,0:T(8,128)(2,1)}, u32[]{:S(2)}) copy-start(bf16[2,256,256]{2,1,0:T(8,128)(2,1)} %constant.51.clone) | copy-start | bytes 786436
  61.0 4.8 %collective-permute-start.10 = (f32[72,256]{1,0:T(8,128)S(1)}, f32[72,256]{1,0:T(8,128)S(1)}, u32[]{:S(2)}, u32[]{:S(2)}) collective-permute-start(f32[72,256]{1,0:T(8,128)S(1)} %get-tuple-element.27), channel_id=1, source_target_pairs={{0,2},{4,6},{8,10},{12,14},{16,18},{20,22},{24,26},{28,30},{32,34}... | collective-permute-start | bytes 221192 | tf_op jit(solution)/shard_map/ppermute | solution.py:65
  61.1 4.7 %collective-permute-start.11 = (f32[72,256]{1,0:T(8,128)S(1)}, f32[72,256]{1,0:T(8,128)S(1)}, u32[]{:S(2)}, u32[]{:S(2)}) collective-permute-start(f32[72,256]{1,0:T(8,128)S(1)} %get-tuple-element.28), channel_id=1, source_target_pairs={{0,3},{4,7},{8,11},{12,15},{16,19},{20,23},{24,27},{28,31},{32,35}... | collective-permute-start | bytes 221192 | tf_op jit(solution)/shard_map/ppermute | solution.py:65
  62.5 4.4 %collective-permute-start.9 = (f32[72,256]{1,0:T(8,128)S(1)}, f32[72,256]{1,0:T(8,128)S(1)}, u32[]{:S(2)}, u32[]{:S(2)}) collective-permute-start(f32[72,256]{1,0:T(8,128)S(1)} %get-tuple-element.26), channel_id=1, source_target_pairs={{0,1},{4,5},{8,9},{12,13},{16,17},{20,21},{24,25},{28,29},{32,33},... | collective-permute-start | bytes 221192 | tf_op jit(solution)/shard_map/ppermute | solution.py:65
  67.9 16.6 %all-to-all-start.1 = ((f32[32,16,256]{2,1,0:T(8,128)}), f32[32,16,256]{2,1,0:T(8,128)S(1)}, u32[]{:S(2)}, u32[]{:S(2)}) async-start(f32[32,16,256]{2,1,0:T(8,128)} %shard_map.67), calls=%async_computation.1 | async-start | bytes 1048576 | tf_op jit(solution)/shard_map/all_to_all | solution.py:45
  89.8 9.0 %collective-permute-start.12 = (bf16[64,3584]{1,0:T(8,128)(2,1)S(1)}, bf16[64,3584]{1,0:T(8,128)(2,1)S(1)}, u32[]{:S(2)}, u32[]{:S(2)}) collective-permute-start(bf16[64,3584]{1,0:T(8,128)(2,1)S(1)} %get-tuple-element.30), channel_id=1, source_target_pairs={{0,2},{4,6},{8,10},{12,14},{16,18},{20,22},{24,26},{28,30},{32,34}... | collective-permute-start | bytes 1376264 | tf_op jit(solution)/shard_map/ppermute | solution.py:65
  90.8 13.2 %collective-permute-start.13 = (bf16[64,3584]{1,0:T(8,128)(2,1)S(1)}, bf16[64,3584]{1,0:T(8,128)(2,1)S(1)}, u32[]{:S(2)}, u32[]{:S(2)}) collective-permute-start(bf16[64,3584]{1,0:T(8,128)(2,1)S(1)} %get-tuple-element.31), channel_id=1, source_target_pairs={{0,1},{4,5},{8,9},{12,13},{16,17},{20,21},{24,25},{28,29},{32,33},... | collective-permute-start | bytes 1376264 | tf_op jit(solution)/shard_map/ppermute | solution.py:65
  91.1 12.9 %collective-permute-start.14 = (bf16[64,3584]{1,0:T(8,128)(2,1)S(1)}, bf16[64,3584]{1,0:T(8,128)(2,1)S(1)}, u32[]{:S(2)}, u32[]{:S(2)}) collective-permute-start(bf16[64,3584]{1,0:T(8,128)(2,1)S(1)} %get-tuple-element.32), channel_id=1, source_target_pairs={{0,3},{4,7},{8,11},{12,15},{16,19},{20,23},{24,27},{28,31},{32,35}... | collective-permute-start | bytes 1376264 | tf_op jit(solution)/shard_map/ppermute | solution.py:65
  122.8 10.1 %collective-permute-start.15 = (bf16[2,3584]{1,0:T(2,128)(2,1)S(1)}, bf16[2,3584]{1,0:T(2,128)(2,1)S(1)}, u32[]{:S(2)}, u32[]{:S(2)}) collective-permute-start(bf16[2,3584]{1,0:T(2,128)(2,1)S(1)} %reduce_sum.12), channel_id=1, source_target_pairs={{0,0},{4,4},{8,8},{12,12},{16,16},{20,20},{24,24},{28,28},{32,32},... | collective-permute-start | bytes 43016 | tf_op jit(solution)/shard_map/ppermute | solution.py:473

commit v6 on v5

--- a/solution.py
+++ b/solution.py
@@ -137,31 +137,31 @@
 
 
 DEPTH = 512
-EARLY_LIMIT = 32 * 1024 * 1024
+EARLY_LIMIT = 40 * 1024 * 1024
 GRADIENT_LIMIT = 48 * 1024 * 1024
 LATE_LIMIT = 16 * 1024 * 1024
 
 
-def add_logits(half_refs, t_ref, s_ref, out_ref, t_copies=(), s_copies=()):
-    cols = t_ref.shape[1]
+def add_logits(half_refs, heads, out_ref, copies=None):
     at = 0
-    for copies, ref, col in ((t_copies, t_ref, slice(0, cols)), (s_copies, s_ref, slice(cols, 2 * cols))):
-        for k in range(ref.shape[0] // DEPTH):
-            left = jnp.concatenate([half[:, at : at + DEPTH] for half in half_refs], axis=0)
-            if copies:
-                copies[k].wait()
-            term = jnp.dot(
-                left, ref[k * DEPTH : (k + 1) * DEPTH, :], preferred_element_type=jnp.float32
-            )
-            if k == 0:
-                out_ref[:, col] = term
-            else:
-                out_ref[:, col] += term
-            at += DEPTH
-
-
-def logit_cost(rows, teacher_head, student_cols):
-    elements = teacher_head.size + student_cols.size
+    for col, refs in heads:
+        start = at
+        for ref in refs:
+            for k in range(ref.shape[0] // DEPTH):
+                left = jnp.concatenate([half[:, at : at + DEPTH] for half in half_refs], axis=0)
+                if copies is not None:
+                    copies[at // DEPTH].wait()
+                term = jnp.dot(
+                    left, ref[k * DEPTH : (k + 1) * DEPTH, :], preferred_element_type=jnp.float32
+                )
+                if at == start:
+                    out_ref[:, col] = term
+                else:
+                    out_ref[:, col] += term
+                at += DEPTH
+
+
+def logit_cost(rows, elements):
     return pl.CostEstimate(
         flops=2 * rows * elements, bytes_accessed=2 * elements, transcendentals=0
     )
@@ -172,45 +172,56 @@
     rows = count * halves[0].shape[0]
     cols = teacher_head.shape[1]
 
+    half = teacher_head.shape[0] // 2
+
     def kernel(*refs):
-        t_hbm, s_hbm, out_ref, t_ref, s_ref, t_sem, s_sem = refs[count:]
-        t_copies = fetch(t_hbm, DEPTH, t_ref, t_sem)
-        s_copies = fetch(s_hbm, DEPTH, s_ref, s_sem)
-        add_logits(refs[:count], t_ref, s_ref, out_ref, t_copies, s_copies)
+        t_hbm, s_hbm, out_ref, t_low, t_high, s_ref, low_sem, high_sem, s_sem = refs[count:]
+        copies = (
+            fetch(t_hbm.at[pl.ds(0, half)], DEPTH, t_low, low_sem)
+            + fetch(t_hbm.at[pl.ds(half, half)], DEPTH, t_high, high_sem)
+            + fetch(s_hbm, DEPTH, s_ref, s_sem)
+        )
+        heads = ((slice(0, cols), (t_low, t_high)), (slice(cols, 2 * cols), (s_ref,)))
+        add_logits(refs[:count], heads, out_ref, copies)
 
     whole = pl.BlockSpec(memory_space=pltpu.VMEM)
+    low = jax.ShapeDtypeStruct((half, cols), teacher_head.dtype)
     return pl.pallas_call(
         kernel,
         in_specs=[whole] * count + [pl.BlockSpec(memory_space=pltpu.HBM)] * 2,
-        out_specs=[whole] * 3,
+        out_specs=[whole] * 4,
         out_shape=[
             jax.ShapeDtypeStruct((rows, 2 * cols), jnp.float32),
-            jax.ShapeDtypeStruct(teacher_head.shape, teacher_head.dtype),
+            low,
+            low,
             jax.ShapeDtypeStruct(student_cols.shape, student_cols.dtype),
         ],
         scratch_shapes=[
-            pltpu.SemaphoreType.DMA((teacher_head.shape[0] // DEPTH,)),
+            pltpu.SemaphoreType.DMA((half // DEPTH,)),
+            pltpu.SemaphoreType.DMA((half // DEPTH,)),
             pltpu.SemaphoreType.DMA((student_cols.shape[0] // DEPTH,)),
         ],
-        cost_estimate=logit_cost(rows, teacher_head, student_cols),
+        cost_estimate=logit_cost(rows, teacher_head.size + student_cols.size),
         compiler_params=pltpu.CompilerParams(vmem_limit_bytes=EARLY_LIMIT),
     )(*halves, teacher_head, student_cols)
 
 
-def logits_and_message(slots, early, halves, teacher_head, student_cols, words, own_word, per_shard):
+def logits_and_message(slots, early, halves, heads, words, own_word, per_shard):
     count = len(halves)
     half = halves[0].shape[0]
     rows = early.shape[0] + count * half
     block = half // 2
-    cols = teacher_head.shape[1]
+    cols = heads[0].shape[1]
     lanes = cols // per_shard
+    elements = sum(head.size for head in heads)
 
     def kernel(slot_ref, early_ref, *refs):
         (
-            word_ref, own_word_ref, t_ref, s_ref, *msg_refs, logit_ref,
+            word_ref, own_word_ref, t_low, t_high, s_ref, *msg_refs, logit_ref,
             late_ref, all_ref, spare_ref,
         ) = refs[count:]
-        add_logits(refs[:count], t_ref, s_ref, late_ref)
+        near = ((slice(0, cols), (t_low, t_high)), (slice(cols, 2 * cols), (s_ref,)))
+        add_logits(refs[:count], near, late_ref)
 
         for source_ref, places in ((early_ref, (0, 1, 3, 6)), (late_ref, (2, 4, 5, 7))):
             for n, place in enumerate(places):
@@ -267,7 +278,7 @@
     whole = pl.BlockSpec(memory_space=pltpu.VMEM)
     return pl.pallas_call(
         kernel,
-        in_specs=[pl.BlockSpec(memory_space=pltpu.SMEM)] + [whole] * (count + 5),
+        in_specs=[pl.BlockSpec(memory_space=pltpu.SMEM)] + [whole] * (count + 6),
         out_specs=[whole] * 5,
         out_shape=[jax.ShapeDtypeStruct((72, rows), jnp.float32)] * 4
         + [jax.ShapeDtypeStruct((cols, rows), jnp.float32)],
@@ -276,9 +287,9 @@
             pltpu.VMEM((rows, 2 * cols), jnp.float32),
             pltpu.VMEM((rows // 128, 2 * lanes, 128), jnp.float32),
         ],
-        cost_estimate=logit_cost(count * half, teacher_head, student_cols),
+        cost_estimate=logit_cost(count * half, elements),
         compiler_params=pltpu.CompilerParams(vmem_limit_bytes=LATE_LIMIT),
-    )(slots, early, *halves, words, own_word, teacher_head, student_cols)
+    )(slots, early, *halves, words, own_word, *heads)
 
 
 def expand_words(words, per_shard):
@@ -444,7 +455,7 @@
     below_second = along(own[1], 1)
     above_second = along(own[0], -1)
     far = (along(below_first, 1), along(above_first, -1))
-    early, teacher_near, student_near = early_logits(
+    early, *near_heads = early_logits(
         own + (above_first, below_first), teacher_head, student_cols
     )
     late = (above_second,) + far + (below_second,)
@@ -453,7 +464,7 @@
     x, y = lax.axis_index("dp"), lax.axis_index("vocab") // NZ
     slots = jnp.stack((jnp.where(core == 0, x, y), jnp.where(core == 0, y, x), core))
     *message, logit = logits_and_message(
-        slots, early, late, teacher_near, student_near, words, own_word, per_shard
+        slots, early, late, near_heads, words, own_word, per_shard
     )
     near = (
         message[0], along(message[1], 1), along(message[2], 2), along(message[3], -1),

time: 134 us -> 134 us (level)
  local copies, waits for them, and re-layouts: 5.59 us -> 3.31 us
  waiting for transfers between devices: 43.9 us -> 45.8 us
    unnamed x11 -> x9, local copies, waits for them, and re-layouts: 2.95 us -> 0.65 us
    ppermute x15, waiting for transfers between devices: 25.7 us -> 27.4 us  [step(): return lax.ppermute(value, WHOLE, pairs)]
  transfers between devices with their start and end apart: 18 -> 18, of which waited for: 12 -> 12; matrix products, arithmetic and copies ran while one was open for 1% -> 1% of each run, Pallas kernels for 9% -> 10%
where the time goes in v6:
time: 134 us; the launch traced here: 133 us
  waiting for transfers between devices  45.8 us (34%)
  starting transfers between devices  40.3 us (30%)
  Pallas kernels  23.8 us (18%)
  blocking collectives  18.5 us (14%)
  local copies, waits for them, and re-layouts  3.31 us (2%)
  other arithmetic  1.61 us (1%)
    ppermute x15, waiting for transfers between devices, step(): return lax.ppermute(value, WHOLE, pairs)  27.4 us
    all_to_all x1, blocking collectives, exchange(): lax.all_to_all(value, WHOLE, 0, 0, tiled=True, axis_index_groups=groups)  18.5 us
    ppermute x15, starting transfers between devices, step(): return lax.ppermute(value, WHOLE, pairs)  18.1 us
    all_to_all x2, waiting for transfers between devices, exchange(): lax.all_to_all(value, WHOLE, 0, 0, tiled=True, axis_index_groups=groups)  17.1 us
    all_to_all x2, starting transfers between devices, exchange(): lax.all_to_all(value, WHOLE, 0, 0, tiled=True, axis_index_groups=groups)  14.1 us
    pallas_call x1, Pallas kernels, early_logits(): pl.pallas_call(kernel, in_specs=[whole] * count + [pl.BlockSpec(memory_sp...  8.69 us
    ppermute x1, starting transfers between devices, per_device(): return lax.ppermute(summed.astype(jnp.bfloat16), WHOLE, last_hop())  8.1 us
    pallas_call x1, Pallas kernels, gradient(): pl.pallas_call(kernel, in_specs=[pl.BlockSpec(memory_space=pltpu.SMEM)] +...  5.26 us
  transfers between devices with their start and end apart: 18, of which 12 were waited for; matrix products, arithmetic and copies ran while one was open for 1% of the time, Pallas kernels for 10%

profile of v6, /device:TPU:1, one launch (start us, length us, event | category | flops | bytes accessed | tf_op | source)
XLA Modules:
  0.0 133.5 jit_solution(3773140963293398720)
XLA Ops:
  1.7 9.0 %all-to-all-start = ((bf16[8,2,8704]{2,1,0:T(2,128)(2,1)}), bf16[8,2,8704]{2,1,0:T(2,128)(2,1)S(1)}, u32[]{:S(2)}, u32[]{:S(2)}) async-start(bf16[8,2,8704]{2,1,0:T(2,128)(2,1)} %broadcast_in_dim.2), calls=%async_computation | async-start | bytes 557056 | tf_op jit(solution)/shard_map/all_to_all | solution.py:45
  11.6 4.7 %shard_map.64.refs_4_.word_ref = s32[128,256]{1,0:T(8,128)} custom-call(s32[128,256]{1,0:T(8,128)} %copy.11.tiles_ref), custom_call_target="tpu_custom_call" | custom-call | flops 67108864 | bytes 262144 | tf_op jit(solution)/shard_map/pallas_call | solution.py:121
  16.3 5.3 %all-to-all-done = bf16[8,2,8704]{2,1,0:T(2,128)(2,1)S(1)} async-done(((bf16[8,2,8704]{2,1,0:T(2,128)(2,1)}), bf16[8,2,8704]{2,1,0:T(2,128)(2,1)S(1)}, u32[]{:S(2)}, u32[]{:S(2)}) %all-to-all-start) | async-done | bytes 278560 | tf_op jit(solution)/shard_map/all_to_all | solution.py:45
  21.7 2.8 %collective-permute-start = (bf16[16,8704]{1,0:T(8,128)(2,1)S(1)}, bf16[16,8704]{1,0:T(8,128)(2,1)S(1)}, u32[]{:S(2)}, u32[]{:S(2)}) collective-permute-start(bf16[16,8704]{1,0:T(8,128)(2,1)S(1)} %all_to_all.16), channel_id=1, source_target_pairs={{0,64},{4,68},{8,72},{12,76},{16,80},{20,84},{24,88},{28,92},{32,9... | collective-permute-start | bytes 835592 | tf_op jit(solution)/shard_map/ppermute | solution.py:65
  26.1 2.9 %collective-permute-done = bf16[16,8704]{1,0:T(8,128)(2,1)S(1)} collective-permute-done((bf16[16,8704]{1,0:T(8,128)(2,1)S(1)}, bf16[16,8704]{1,0:T(8,128)(2,1)S(1)}, u32[]{:S(2)}, u32[]{:S(2)}) %collective-permute-start) | collective-permute-done | bytes 278560 | tf_op jit(solution)/shard_map/ppermute | solution.py:65
  28.9 2.8 %collective-permute-done.2 = bf16[16,8704]{1,0:T(8,128)(2,1)S(1)} collective-permute-done((bf16[16,8704]{1,0:T(8,128)(2,1)S(1)}, bf16[16,8704]{1,0:T(8,128)(2,1)S(1)}, u32[]{:S(2)}, u32[]{:S(2)}) %collective-permute-start.2) | collective-permute-done | bytes 278560 | tf_op jit(solution)/shard_map/ppermute | solution.py:65
  31.8 3.1 %collective-permute-start.3 = (bf16[32,8704]{1,0:T(8,128)(2,1)S(1)}, bf16[32,8704]{1,0:T(8,128)(2,1)S(1)}, u32[]{:S(2)}, u32[]{:S(2)}) collective-permute-start(bf16[32,8704]{1,0:T(8,128)(2,1)S(1)} %constant_dynamic-update-slice_fusion.2.refs_1_), channel_id=1, source_target_pairs={{0,3},{4,7},{8,11},{12,15},{16,19},{20,23},{24,27},{28,31},{32,35}... | collective-permute-start | bytes 1671176 | tf_op jit(solution)/shard_map/ppermute | solution.py:65
  35.1 2.7 %collective-permute-start.5 = (bf16[32,8704]{1,0:T(8,128)(2,1)S(1)}, bf16[32,8704]{1,0:T(8,128)(2,1)S(1)}, u32[]{:S(2)}, u32[]{:S(2)}) collective-permute-start(bf16[32,8704]{1,0:T(8,128)(2,1)S(1)} %constant_dynamic-update-slice_fusion.refs_0_), channel_id=1, source_target_pairs={{0,3},{4,7},{8,11},{12,15},{16,19},{20,23},{24,27},{28,31},{32,35}... | collective-permute-start | bytes 1671176 | tf_op jit(solution)/shard_map/ppermute | solution.py:65
  37.8 3.6 %collective-permute-done.3.refs_2_ = bf16[32,8704]{1,0:T(8,128)(2,1)S(1)} collective-permute-done((bf16[32,8704]{1,0:T(8,128)(2,1)S(1)}, bf16[32,8704]{1,0:T(8,128)(2,1)S(1)}, u32[]{:S(2)}, u32[]{:S(2)}) %collective-permute-start.3) | collective-permute-done | bytes 557088 | tf_op jit(solution)/shard_map/ppermute | solution.py:65
  41.4 3.1 %collective-permute-start.7 = (bf16[32,8704]{1,0:T(8,128)(2,1)S(1)}, bf16[32,8704]{1,0:T(8,128)(2,1)}, u32[]{:S(2)}, u32[]{:S(2)}) collective-permute-start(bf16[32,8704]{1,0:T(8,128)(2,1)S(1)} %collective-permute-done.3.refs_2_), channel_id=1, source_target_pairs={{0,3},{4,7},{8,11},{12,15},{16,19},{20,23},{24,27},{28,31},{32,35}... | collective-permute-start | bytes 1671176 | tf_op jit(solution)/shard_map/ppermute | solution.py:65
  45.8 8.7 %shard_map.65 = (f32[128,1280]{1,0:T(8,128)S(1)}, bf16[2560,640]{1,0:T(8,128)(2,1)S(1)}, bf16[2560,640]{1,0:T(8,128)(2,1)S(1)}, bf16[3584,640]{1,0:T(8,128)(2,1)S(1)}) custom-call(bf16[32,8704]{1,0:T(8,128)(2,1)S(1)} %constant_dynamic-update-slice_fusion.refs_0_, bf16[32,8704]{1,0:T(8,128)(2,1)S(1)} %constant_dynamic-update-slice_fusion.2.refs_1_, ...), custom_call_target="tpu_custom_call" | custom-call | flops 1426063360 | bytes 11141120 | tf_op jit(solution)/shard_map/pallas_call | solution.py:189
  54.5 2.4 %collective-permute-done.6.refs_1_ = bf16[32,8704]{1,0:T(8,128)(2,1)} collective-permute-done((bf16[32,8704]{1,0:T(8,128)(2,1)}, bf16[32,8704]{1,0:T(8,128)(2,1)}, u32[]{:S(2)}, u32[]{:S(2)}) %collective-permute-start.6) | collective-permute-done | bytes 557088 | tf_op jit(solution)/shard_map/ppermute | solution.py:65
  57.0 4.0 %shard_map.66 = (f32[72,256]{1,0:T(8,128)S(1)}, f32[72,256]{1,0:T(8,128)S(1)}, f32[72,256]{1,0:T(8,128)S(1)}, f32[72,256]{1,0:T(8,128)S(1)}, f32[640,256]{1,0:T(8,128)S(1)}) custom-call(s32[3]{0:T(128)S(1)} %pad_add_fusion.slot_ref, f32[128,1280]{1,0:T(8,128)S(1)} %get-tuple-element.22.early_ref, bf16[32,8704]{1,0:T(8,128)(2,1)S(1)} %collective-permute-done.5.refs_0_, ...), custom_call_target="tpu_custom_call" | custom-call | flops 1426063360 | bytes 11141120 | tf_op jit(solution)/shard_map/pallas_call | solution.py:279
  61.3 1.2 collective-permute-start.11
  62.8 3.1 %collective-permute-done.10.refs_2_ = f32[72,256]{1,0:T(8,128)S(1)} collective-permute-done((f32[72,256]{1,0:T(8,128)S(1)}, f32[72,256]{1,0:T(8,128)S(1)}, u32[]{:S(2)}, u32[]{:S(2)}) %collective-permute-start.10) | collective-permute-done | bytes 73760 | tf_op jit(solution)/shard_map/ppermute | solution.py:65
  67.9 5.1 %all-to-all-start.1 = ((f32[32,16,256]{2,1,0:T(8,128)}), f32[32,16,256]{2,1,0:T(8,128)S(1)}, u32[]{:S(2)}, u32[]{:S(2)}) async-start(f32[32,16,256]{2,1,0:T(8,128)} %shard_map.67), calls=%async_computation.1 | async-start | bytes 1048576 | tf_op jit(solution)/shard_map/all_to_all | solution.py:45
  73.1 11.8 %all-to-all-done.1.msg_ref = f32[32,16,256]{2,1,0:T(8,128)S(1)} async-done(((f32[32,16,256]{2,1,0:T(8,128)}), f32[32,16,256]{2,1,0:T(8,128)S(1)}, u32[]{:S(2)}, u32[]{:S(2)}) %all-to-all-start.1) | async-done | bytes 524320 | tf_op jit(solution)/shard_map/all_to_all | solution.py:45
  84.9 5.3 %shard_map.68 = (bf16[64,3584]{1,0:T(8,128)(2,1)S(1)}, bf16[64,3584]{1,0:T(8,128)(2,1)S(1)}, bf16[64,3584]{1,0:T(8,128)(2,1)S(1)}, bf16[64,3584]{1,0:T(8,128)(2,1)S(1)}) custom-call(s32[3]{0:T(128)S(1)} %pad_add_fusion.slot_ref, s32[128,256]{1,0:T(8,128)S(1)} %copy-done.1, f32[640,256]{1,0:T(8,128)S(1)} %get-tuple-element.26.logit_ref, ...), custom_call_target="tpu_custom_call" | custom-call | tf_op jit(solution)/shard_map/pallas_call | solution.py:412
  91.2 1.8 %collective-permute-start.14 = (bf16[64,3584]{1,0:T(8,128)(2,1)S(1)}, bf16[64,3584]{1,0:T(8,128)(2,1)S(1)}, u32[]{:S(2)}, u32[]{:S(2)}) collective-permute-start(bf16[64,3584]{1,0:T(8,128)(2,1)S(1)} %get-tuple-element.34), channel_id=1, source_target_pairs={{0,3},{4,7},{8,11},{12,15},{16,19},{20,23},{24,27},{28,31},{32,35}... | collective-permute-start | bytes 1376264 | tf_op jit(solution)/shard_map/ppermute | solution.py:65
  93.0 6.1 %collective-permute-done.12 = bf16[64,3584]{1,0:T(8,128)(2,1)S(1)} collective-permute-done((bf16[64,3584]{1,0:T(8,128)(2,1)S(1)}, bf16[64,3584]{1,0:T(8,128)(2,1)S(1)}, u32[]{:S(2)}, u32[]{:S(2)}) %collective-permute-start.12) | collective-permute-done | bytes 458784 | tf_op jit(solution)/shard_map/ppermute | solution.py:65
  99.2 4.9 %collective-permute-done.13 = bf16[64,3584]{1,0:T(8,128)(2,1)S(1)} collective-permute-done((bf16[64,3584]{1,0:T(8,128)(2,1)S(1)}, bf16[64,3584]{1,0:T(8,128)(2,1)S(1)}, u32[]{:S(2)}, u32[]{:S(2)}) %collective-permute-start.13) | collective-permute-done | bytes 458784 | tf_op jit(solution)/shard_map/ppermute | solution.py:65
  104.5 18.5 %all_to_all.23 = bf16[32,2,3584]{2,1,0:T(2,128)(2,1)S(1)} all-to-all(bf16[32,2,3584]{2,1,0:T(2,128)(2,1)S(1)} %all_to_all.18), channel_id=1, replica_groups={{0,4,8,12,16,20,24,28,32,36,40,44,48,52,56,60,64,68,72,76,80,84,88,92,9..., dimensions={0} | all-to-all | bytes 917504 | tf_op jit(solution)/shard_map/all_to_all | solution.py:45
  123.4 8.1 %collective-permute-start.15 = (bf16[2,3584]{1,0:T(2,128)(2,1)S(1)}, bf16[2,3584]{1,0:T(2,128)(2,1)S(1)}, u32[]{:S(2)}, u32[]{:S(2)}) collective-permute-start(bf16[2,3584]{1,0:T(2,128)(2,1)S(1)} %reduce_sum.12), channel_id=1, source_target_pairs={{0,0},{4,4},{8,8},{12,12},{16,16},{20,20},{24,24},{28,28},{32,32},... | collective-permute-start | bytes 43016 | tf_op jit(solution)/shard_map/ppermute | solution.py:484
  131.5 1.4 %collective-permute-done.15 = bf16[2,3584]{1,0:T(2,128)(2,1)S(1)} collective-permute-done((bf16[2,3584]{1,0:T(2,128)(2,1)S(1)}, bf16[2,3584]{1,0:T(2,128)(2,1)S(1)}, u32[]{:S(2)}, u32[]{:S(2)}) %collective-permute-start.15) | collective-permute-done | bytes 14368 | tf_op jit(solution)/shard_map/ppermute | solution.py:484
  (40 shorter events, 10.8 us)
Async XLA Ops:
  0.0 10.8 %copy-start = (s32[512,128]{1,0:T(8,128)S(1)}, s32[512,128]{1,0:T(8,128)}, u32[]{:S(2)}) copy-start(s32[512,128]{1,0:T(8,128)} %param.10) | copy-start | bytes 786436
  1.7 19.8 %all-to-all-start = ((bf16[8,2,8704]{2,1,0:T(2,128)(2,1)}), bf16[8,2,8704]{2,1,0:T(2,128)(2,1)S(1)}, u32[]{:S(2)}, u32[]{:S(2)}) async-start(bf16[8,2,8704]{2,1,0:T(2,128)(2,1)} %broadcast_in_dim.2), calls=%async_computation | async-start | bytes 557056 | tf_op jit(solution)/shard_map/all_to_all | solution.py:45
  21.7 7.3 %collective-permute-start = (bf16[16,8704]{1,0:T(8,128)(2,1)S(1)}, bf16[16,8704]{1,0:T(8,128)(2,1)S(1)}, u32[]{:S(2)}, u32[]{:S(2)}) collective-permute-start(bf16[16,8704]{1,0:T(8,128)(2,1)S(1)} %all_to_all.16), channel_id=1, source_target_pairs={{0,64},{4,68},{8,72},{12,76},{16,80},{20,84},{24,88},{28,92},{32,9... | collective-permute-start | bytes 835592 | tf_op jit(solution)/shard_map/ppermute | solution.py:65
  24.5 7.3 %collective-permute-start.2 = (bf16[16,8704]{1,0:T(8,128)(2,1)S(1)}, bf16[16,8704]{1,0:T(8,128)(2,1)S(1)}, u32[]{:S(2)}, u32[]{:S(2)}) collective-permute-start(bf16[16,8704]{1,0:T(8,128)(2,1)S(1)} %all_to_all.16), channel_id=1, source_target_pairs={{0,96},{4,100},{8,104},{12,108},{16,112},{20,116},{24,120},{28,124... | collective-permute-start | bytes 835592 | tf_op jit(solution)/shard_map/ppermute | solution.py:65
  25.4 9.6 %collective-permute-start.1 = (bf16[16,8704]{1,0:T(8,128)(2,1)S(1)}, bf16[16,8704]{1,0:T(8,128)(2,1)S(1)}, u32[]{:S(2)}, u32[]{:S(2)}) collective-permute-start(bf16[16,8704]{1,0:T(8,128)(2,1)S(1)} %all_to_all.16), channel_id=1, source_target_pairs={{0,32},{4,36},{8,40},{12,44},{16,48},{20,52},{24,56},{28,60},{32,6... | collective-permute-start | bytes 835592 | tf_op jit(solution)/shard_map/ppermute | solution.py:65
  31.8 9.6 %collective-permute-start.3 = (bf16[32,8704]{1,0:T(8,128)(2,1)S(1)}, bf16[32,8704]{1,0:T(8,128)(2,1)S(1)}, u32[]{:S(2)}, u32[]{:S(2)}) collective-permute-start(bf16[32,8704]{1,0:T(8,128)(2,1)S(1)} %constant_dynamic-update-slice_fusion.2.refs_1_), channel_id=1, source_target_pairs={{0,3},{4,7},{8,11},{12,15},{16,19},{20,23},{24,27},{28,31},{32,35}... | collective-permute-start | bytes 1671176 | tf_op jit(solution)/shard_map/ppermute | solution.py:65
  34.9 10.1 %collective-permute-start.4 = (bf16[32,8704]{1,0:T(8,128)(2,1)S(1)}, bf16[32,8704]{1,0:T(8,128)(2,1)}, u32[]{:S(2)}, u32[]{:S(2)}) collective-permute-start(bf16[32,8704]{1,0:T(8,128)(2,1)S(1)} %constant_dynamic-update-slice_fusion.refs_0_), channel_id=1, source_target_pairs={{0,1},{4,5},{8,9},{12,13},{16,17},{20,21},{24,25},{28,29},{32,33},... | collective-permute-start | bytes 1671176 | tf_op jit(solution)/shard_map/ppermute | solution.py:65
  35.0 19.5 %collective-permute-start.8 = (bf16[32,8704]{1,0:T(8,128)(2,1)S(1)}, bf16[32,8704]{1,0:T(8,128)(2,1)S(1)}, u32[]{:S(2)}, u32[]{:S(2)}) collective-permute-start(bf16[32,8704]{1,0:T(8,128)(2,1)S(1)} %constant_dynamic-update-slice_fusion.2.refs_1_), channel_id=1, source_target_pairs={{0,1},{4,5},{8,9},{12,13},{16,17},{20,21},{24,25},{28,29},{32,33},... | collective-permute-start | bytes 1671176 | tf_op jit(solution)/shard_map/ppermute | solution.py:65
  35.1 19.4 %collective-permute-start.5 = (bf16[32,8704]{1,0:T(8,128)(2,1)S(1)}, bf16[32,8704]{1,0:T(8,128)(2,1)S(1)}, u32[]{:S(2)}, u32[]{:S(2)}) collective-permute-start(bf16[32,8704]{1,0:T(8,128)(2,1)S(1)} %constant_dynamic-update-slice_fusion.refs_0_), channel_id=1, source_target_pairs={{0,3},{4,7},{8,11},{12,15},{16,19},{20,23},{24,27},{28,31},{32,35}... | collective-permute-start | bytes 1671176 | tf_op jit(solution)/shard_map/ppermute | solution.py:65
  41.4 13.1 %collective-permute-start.7 = (bf16[32,8704]{1,0:T(8,128)(2,1)S(1)}, bf16[32,8704]{1,0:T(8,128)(2,1)}, u32[]{:S(2)}, u32[]{:S(2)}) collective-permute-start(bf16[32,8704]{1,0:T(8,128)(2,1)S(1)} %collective-permute-done.3.refs_2_), channel_id=1, source_target_pairs={{0,3},{4,7},{8,11},{12,15},{16,19},{20,23},{24,27},{28,31},{32,35}... | collective-permute-start | bytes 1671176 | tf_op jit(solution)/shard_map/ppermute | solution.py:65
  45.0 11.9 %collective-permute-start.6 = (bf16[32,8704]{1,0:T(8,128)(2,1)}, bf16[32,8704]{1,0:T(8,128)(2,1)}, u32[]{:S(2)}, u32[]{:S(2)}) collective-permute-start(bf16[32,8704]{1,0:T(8,128)(2,1)} %collective-permute-done.4.refs_3_), channel_id=1, source_target_pairs={{0,1},{4,5},{8,9},{12,13},{16,17},{20,21},{24,25},{28,29},{32,33},... | collective-permute-start | bytes 1671176 | tf_op jit(solution)/shard_map/ppermute | solution.py:65
  45.8 11.2 %copy-start.1 = (s32[128,256]{1,0:T(8,128)S(1)}, s32[128,256]{1,0:T(8,128)}, u32[]{:S(2)}) copy-start(s32[128,256]{1,0:T(8,128)} %shard_map.64.refs_4_.word_ref) | copy-start | bytes 393220
  57.0 16.1 %copy-start.2 = (bf16[2,256,256]{2,1,0:T(8,128)(2,1)S(1)}, bf16[2,256,256]{2,1,0:T(8,128)(2,1)}, u32[]{:S(2)}) copy-start(bf16[2,256,256]{2,1,0:T(8,128)(2,1)} %constant.51.clone) | copy-start | bytes 786436
  61.0 5.0 %collective-permute-start.10 = (f32[72,256]{1,0:T(8,128)S(1)}, f32[72,256]{1,0:T(8,128)S(1)}, u32[]{:S(2)}, u32[]{:S(2)}) collective-permute-start(f32[72,256]{1,0:T(8,128)S(1)} %get-tuple-element.29), channel_id=1, source_target_pairs={{0,2},{4,6},{8,10},{12,14},{16,18},{20,22},{24,26},{28,30},{32,34}... | collective-permute-start | bytes 221192 | tf_op jit(solution)/shard_map/ppermute | solution.py:65
  61.3 4.7 %collective-permute-start.11 = (f32[72,256]{1,0:T(8,128)S(1)}, f32[72,256]{1,0:T(8,128)S(1)}, u32[]{:S(2)}, u32[]{:S(2)}) collective-permute-start(f32[72,256]{1,0:T(8,128)S(1)} %get-tuple-element.30), channel_id=1, source_target_pairs={{0,3},{4,7},{8,11},{12,15},{16,19},{20,23},{24,27},{28,31},{32,35}... | collective-permute-start | bytes 221192 | tf_op jit(solution)/shard_map/ppermute | solution.py:65
  62.5 4.4 %collective-permute-start.9 = (f32[72,256]{1,0:T(8,128)S(1)}, f32[72,256]{1,0:T(8,128)S(1)}, u32[]{:S(2)}, u32[]{:S(2)}) collective-permute-start(f32[72,256]{1,0:T(8,128)S(1)} %get-tuple-element.28), channel_id=1, source_target_pairs={{0,1},{4,5},{8,9},{12,13},{16,17},{20,21},{24,25},{28,29},{32,33},... | collective-permute-start | bytes 221192 | tf_op jit(solution)/shard_map/ppermute | solution.py:65
  67.9 17.0 %all-to-all-start.1 = ((f32[32,16,256]{2,1,0:T(8,128)}), f32[32,16,256]{2,1,0:T(8,128)S(1)}, u32[]{:S(2)}, u32[]{:S(2)}) async-start(f32[32,16,256]{2,1,0:T(8,128)} %shard_map.67), calls=%async_computation.1 | async-start | bytes 1048576 | tf_op jit(solution)/shard_map/all_to_all | solution.py:45
  90.2 9.0 %collective-permute-start.12 = (bf16[64,3584]{1,0:T(8,128)(2,1)S(1)}, bf16[64,3584]{1,0:T(8,128)(2,1)S(1)}, u32[]{:S(2)}, u32[]{:S(2)}) collective-permute-start(bf16[64,3584]{1,0:T(8,128)(2,1)S(1)} %get-tuple-element.32), channel_id=1, source_target_pairs={{0,2},{4,6},{8,10},{12,14},{16,18},{20,22},{24,26},{28,30},{32,34}... | collective-permute-start | bytes 1376264 | tf_op jit(solution)/shard_map/ppermute | solution.py:65
  90.4 13.8 %collective-permute-start.13 = (bf16[64,3584]{1,0:T(8,128)(2,1)S(1)}, bf16[64,3584]{1,0:T(8,128)(2,1)S(1)}, u32[]{:S(2)}, u32[]{:S(2)}) collective-permute-start(bf16[64,3584]{1,0:T(8,128)(2,1)S(1)} %get-tuple-element.33), channel_id=1, source_target_pairs={{0,1},{4,5},{8,9},{12,13},{16,17},{20,21},{24,25},{28,29},{32,33},... | collective-permute-start | bytes 1376264 | tf_op jit(solution)/shard_map/ppermute | solution.py:65
  91.2 12.9 %collective-permute-start.14 = (bf16[64,3584]{1,0:T(8,128)(2,1)S(1)}, bf16[64,3584]{1,0:T(8,128)(2,1)S(1)}, u32[]{:S(2)}, u32[]{:S(2)}) collective-permute-start(bf16[64,3584]{1,0:T(8,128)(2,1)S(1)} %get-tuple-element.34), channel_id=1, source_target_pairs={{0,3},{4,7},{8,11},{12,15},{16,19},{20,23},{24,27},{28,31},{32,35}... | collective-permute-start | bytes 1376264 | tf_op jit(solution)/shard_map/ppermute | solution.py:65
  123.4 9.5 %collective-permute-start.15 = (bf16[2,3584]{1,0:T(2,128)(2,1)S(1)}, bf16[2,3584]{1,0:T(2,128)(2,1)S(1)}, u32[]{:S(2)}, u32[]{:S(2)}) collective-permute-start(bf16[2,3584]{1,0:T(2,128)(2,1)S(1)} %reduce_sum.12), channel_id=1, source_target_pairs={{0,0},{4,4},{8,8},{12,12},{16,16},{20,20},{24,24},{28,28},{32,32},... | collective-permute-start | bytes 43016 | tf_op jit(solution)/shard_map/ppermute | solution.py:484

commit v7 on v6

--- a/solution.py
+++ b/solution.py
@@ -450,10 +450,13 @@
         jnp.concatenate((gathered, last), axis=0),
         jnp.concatenate((after, opposite), axis=0),
     )
-    below_first = along(own[0], 1)
+    below_first, above_second = along(own[0], 1), along(own[0], -1)
+    below_first, above_second, second = lax.optimization_barrier(
+        (below_first, above_second, own[1])
+    )
+    own = (own[0], second)
     above_first = along(own[1], -1)
     below_second = along(own[1], 1)
-    above_second = along(own[0], -1)
     far = (along(below_first, 1), along(above_first, -1))
     early, *near_heads = early_logits(
         own + (above_first, below_first), teacher_head, student_cols

time: 134 us -> 148 us (1.10)
  starting transfers between devices: 40.3 us -> 49.8 us
  waiting for transfers between devices: 45.8 us -> 52.6 us
  blocking collectives: 18.5 us -> 15.9 us
    ppermute x1, starting transfers between devices: 8.1 us -> 17.1 us  [per_device(): return lax.ppermute(summed.astype(jnp.bfloat16), WHOLE, last_hop())]
    ppermute x15, waiting for transfers between devices: 27.4 us -> 34.6 us  [step(): return lax.ppermute(value, WHOLE, pairs)]
    all_to_all x1, blocking collectives: 18.5 us -> 15.9 us  [exchange(): lax.all_to_all(value, WHOLE, 0, 0, tiled=True, axis_index_groups=groups)]
  transfers between devices with their start and end apart: 18 -> 18, of which waited for: 12 -> 10; matrix products, arithmetic and copies ran while one was open for 1% -> 1% of each run, Pallas kernels for 10% -> 9%
where the time goes in v7:
time: 148 us; the launch traced here: 147 us
  waiting for transfers between devices  52.6 us (36%)
  starting transfers between devices  49.8 us (34%)
  Pallas kernels  23.8 us (16%)
  blocking collectives  15.9 us (11%)
  local copies, waits for them, and re-layouts  3.27 us (2%)
  other arithmetic  1.64 us (1%)
    ppermute x15, waiting for transfers between devices, step(): return lax.ppermute(value, WHOLE, pairs)  34.6 us
    ppermute x15, starting transfers between devices, step(): return lax.ppermute(value, WHOLE, pairs)  18.7 us
    ppermute x1, starting transfers between devices, per_device(): return lax.ppermute(summed.astype(jnp.bfloat16), WHOLE, last_hop())  17.1 us
    all_to_all x2, waiting for transfers between devices, exchange(): lax.all_to_all(value, WHOLE, 0, 0, tiled=True, axis_index_groups=groups)  16.6 us
    all_to_all x1, blocking collectives, exchange(): lax.all_to_all(value, WHOLE, 0, 0, tiled=True, axis_index_groups=groups)  15.9 us
    all_to_all x2, starting transfers between devices, exchange(): lax.all_to_all(value, WHOLE, 0, 0, tiled=True, axis_index_groups=groups)  13.9 us
    pallas_call x1, Pallas kernels, early_logits(): pl.pallas_call(kernel, in_specs=[whole] * count + [pl.BlockSpec(memory_sp...  8.69 us
    pallas_call x1, Pallas kernels, gradient(): pl.pallas_call(kernel, in_specs=[pl.BlockSpec(memory_space=pltpu.SMEM)] +...  5.26 us
  transfers between devices with their start and end apart: 18, of which 10 were waited for; matrix products, arithmetic and copies ran while one was open for 1% of the time, Pallas kernels for 9%

profile of v7, /device:TPU:1, one launch (start us, length us, event | category | flops | bytes accessed | tf_op | source)
XLA Modules:
  0.0 147.1 jit_solution(3353413810979686573)
XLA Ops:
  1.7 9.0 %all-to-all-start = ((bf16[8,2,8704]{2,1,0:T(2,128)(2,1)}), bf16[8,2,8704]{2,1,0:T(2,128)(2,1)S(1)}, u32[]{:S(2)}, u32[]{:S(2)}) async-start(bf16[8,2,8704]{2,1,0:T(2,128)(2,1)} %broadcast_in_dim.2), calls=%async_computation | async-start | bytes 557056 | tf_op jit(solution)/shard_map/all_to_all | solution.py:45
  11.6 4.7 %shard_map.64.refs_4_.word_ref = s32[128,256]{1,0:T(8,128)} custom-call(s32[128,256]{1,0:T(8,128)} %copy.11.tiles_ref), custom_call_target="tpu_custom_call" | custom-call | flops 67108864 | bytes 262144 | tf_op jit(solution)/shard_map/pallas_call | solution.py:121
  16.3 5.3 %all-to-all-done = bf16[8,2,8704]{2,1,0:T(2,128)(2,1)S(1)} async-done(((bf16[8,2,8704]{2,1,0:T(2,128)(2,1)}), bf16[8,2,8704]{2,1,0:T(2,128)(2,1)S(1)}, u32[]{:S(2)}, u32[]{:S(2)}) %all-to-all-start) | async-done | bytes 278560 | tf_op jit(solution)/shard_map/all_to_all | solution.py:45
  21.7 2.8 %collective-permute-start = (bf16[16,8704]{1,0:T(8,128)(2,1)S(1)}, bf16[16,8704]{1,0:T(8,128)(2,1)S(1)}, u32[]{:S(2)}, u32[]{:S(2)}) collective-permute-start(bf16[16,8704]{1,0:T(8,128)(2,1)S(1)} %all_to_all.16), channel_id=1, source_target_pairs={{0,64},{4,68},{8,72},{12,76},{16,80},{20,84},{24,88},{28,92},{32,9... | collective-permute-start | bytes 835592 | tf_op jit(solution)/shard_map/ppermute | solution.py:65
  26.0 6.0 %collective-permute-done.1 = bf16[16,8704]{1,0:T(8,128)(2,1)S(1)} collective-permute-done((bf16[16,8704]{1,0:T(8,128)(2,1)S(1)}, bf16[16,8704]{1,0:T(8,128)(2,1)S(1)}, u32[]{:S(2)}, u32[]{:S(2)}) %collective-permute-start.1) | collective-permute-done | bytes 278560 | tf_op jit(solution)/shard_map/ppermute | solution.py:65
  32.0 1.4 collective-permute-start.2
  33.4 1.8 %collective-permute-start.3 = (bf16[32,8704]{1,0:T(8,128)(2,1)S(1)}, bf16[32,8704]{1,0:T(8,128)(2,1)S(1)}, u32[]{:S(2)}, u32[]{:S(2)}) collective-permute-start(bf16[32,8704]{1,0:T(8,128)(2,1)S(1)} %constant_dynamic-update-slice_fusion.refs_0_), channel_id=1, source_target_pairs={{0,3},{4,7},{8,11},{12,15},{16,19},{20,23},{24,27},{28,31},{32,35}... | collective-permute-start | bytes 1671176 | tf_op jit(solution)/shard_map/ppermute | solution.py:65
  35.2 7.1 %collective-permute-done.2.refs_3_ = bf16[32,8704]{1,0:T(8,128)(2,1)S(1)} collective-permute-done((bf16[32,8704]{1,0:T(8,128)(2,1)S(1)}, bf16[32,8704]{1,0:T(8,128)(2,1)S(1)}, u32[]{:S(2)}, u32[]{:S(2)}) %collective-permute-start.2) | collective-permute-done | bytes 557088 | tf_op jit(solution)/shard_map/ppermute | solution.py:65
  42.3 2.8 %collective-permute-start.5 = (bf16[32,8704]{1,0:T(8,128)(2,1)S(1)}, bf16[32,8704]{1,0:T(8,128)(2,1)}, u32[]{:S(2)}, u32[]{:S(2)}) collective-permute-start(bf16[32,8704]{1,0:T(8,128)(2,1)S(1)} %pad_maximum_fusion.refs_1_), channel_id=1, source_target_pairs={{0,3},{4,7},{8,11},{12,15},{16,19},{20,23},{24,27},{28,31},{32,35}... | collective-permute-start | bytes 1671176 | tf_op jit(solution)/shard_map/ppermute | solution.py:65
  45.1 6.5 %collective-permute-done.5.refs_2_ = bf16[32,8704]{1,0:T(8,128)(2,1)} collective-permute-done((bf16[32,8704]{1,0:T(8,128)(2,1)S(1)}, bf16[32,8704]{1,0:T(8,128)(2,1)}, u32[]{:S(2)}, u32[]{:S(2)}) %collective-permute-start.5) | collective-permute-done | bytes 557088 | tf_op jit(solution)/shard_map/ppermute | solution.py:65
  51.5 3.2 %collective-permute-start.7 = (bf16[32,8704]{1,0:T(8,128)(2,1)}, bf16[32,8704]{1,0:T(8,128)(2,1)}, u32[]{:S(2)}, u32[]{:S(2)}) collective-permute-start(bf16[32,8704]{1,0:T(8,128)(2,1)} %collective-permute-done.5.refs_2_), channel_id=1, source_target_pairs={{0,3},{4,7},{8,11},{12,15},{16,19},{20,23},{24,27},{28,31},{32,35}... | collective-permute-start | bytes 1671176 | tf_op jit(solution)/shard_map/ppermute | solution.py:65
  55.6 8.7 %shard_map.65 = (f32[128,1280]{1,0:T(8,128)S(1)}, bf16[2560,640]{1,0:T(8,128)(2,1)S(1)}, bf16[2560,640]{1,0:T(8,128)(2,1)S(1)}, bf16[3584,640]{1,0:T(8,128)(2,1)S(1)}) custom-call(bf16[32,8704]{1,0:T(8,128)(2,1)S(1)} %constant_dynamic-update-slice_fusion.refs_0_, bf16[32,8704]{1,0:T(8,128)(2,1)S(1)} %pad_maximum_fusion.refs_1_, ...), custom_call_target="tpu_custom_call" | custom-call | flops 1426063360 | bytes 11141120 | tf_op jit(solution)/shard_map/pallas_call | solution.py:189
  64.3 4.0 %shard_map.66 = (f32[72,256]{1,0:T(8,128)S(1)}, f32[72,256]{1,0:T(8,128)S(1)}, f32[72,256]{1,0:T(8,128)S(1)}, f32[72,256]{1,0:T(8,128)S(1)}, f32[640,256]{1,0:T(8,128)S(1)}) custom-call(s32[3]{0:T(128)S(1)} %pad_add_fusion.slot_ref, f32[128,1280]{1,0:T(8,128)S(1)} %get-tuple-element.27.early_ref, bf16[32,8704]{1,0:T(8,128)(2,1)S(1)} %collective-permute-done.3.refs_0_, ...), custom_call_target="tpu_custom_call" | custom-call | flops 1426063360 | bytes 11141120 | tf_op jit(solution)/shard_map/pallas_call | solution.py:279
  70.2 3.2 %collective-permute-done.10.refs_2_ = f32[72,256]{1,0:T(8,128)S(1)} collective-permute-done((f32[72,256]{1,0:T(8,128)S(1)}, f32[72,256]{1,0:T(8,128)S(1)}, u32[]{:S(2)}, u32[]{:S(2)}) %collective-permute-start.10) | collective-permute-done | bytes 73760 | tf_op jit(solution)/shard_map/ppermute | solution.py:65
  74.1 1.0 shard_map.67
  75.2 4.9 %all-to-all-start.1 = ((f32[32,16,256]{2,1,0:T(8,128)}), f32[32,16,256]{2,1,0:T(8,128)S(1)}, u32[]{:S(2)}, u32[]{:S(2)}) async-start(f32[32,16,256]{2,1,0:T(8,128)} %shard_map.67), calls=%async_computation.1 | async-start | bytes 1048576 | tf_op jit(solution)/shard_map/all_to_all | solution.py:45
  80.1 11.3 %all-to-all-done.1.msg_ref = f32[32,16,256]{2,1,0:T(8,128)S(1)} async-done(((f32[32,16,256]{2,1,0:T(8,128)}), f32[32,16,256]{2,1,0:T(8,128)S(1)}, u32[]{:S(2)}, u32[]{:S(2)}) %all-to-all-start.1) | async-done | bytes 524320 | tf_op jit(solution)/shard_map/all_to_all | solution.py:45
  91.4 5.3 %shard_map.68 = (bf16[64,3584]{1,0:T(8,128)(2,1)S(1)}, bf16[64,3584]{1,0:T(8,128)(2,1)S(1)}, bf16[64,3584]{1,0:T(8,128)(2,1)S(1)}, bf16[64,3584]{1,0:T(8,128)(2,1)S(1)}) custom-call(s32[3]{0:T(128)S(1)} %pad_add_fusion.slot_ref, s32[128,256]{1,0:T(8,128)S(1)} %copy-done.1, f32[640,256]{1,0:T(8,128)S(1)} %get-tuple-element.32.logit_ref, ...), custom_call_target="tpu_custom_call" | custom-call | tf_op jit(solution)/shard_map/pallas_call | solution.py:412
  98.4 1.8 %collective-permute-start.14 = (bf16[64,3584]{1,0:T(8,128)(2,1)S(1)}, bf16[64,3584]{1,0:T(8,128)(2,1)S(1)}, u32[]{:S(2)}, u32[]{:S(2)}) collective-permute-start(bf16[64,3584]{1,0:T(8,128)(2,1)S(1)} %get-tuple-element.40), channel_id=1, source_target_pairs={{0,3},{4,7},{8,11},{12,15},{16,19},{20,23},{24,27},{28,31},{32,35}... | collective-permute-start | bytes 1376264 | tf_op jit(solution)/shard_map/ppermute | solution.py:65
  100.2 6.3 %collective-permute-done.12 = bf16[64,3584]{1,0:T(8,128)(2,1)S(1)} collective-permute-done((bf16[64,3584]{1,0:T(8,128)(2,1)S(1)}, bf16[64,3584]{1,0:T(8,128)(2,1)S(1)}, u32[]{:S(2)}, u32[]{:S(2)}) %collective-permute-start.12) | collective-permute-done | bytes 458784 | tf_op jit(solution)/shard_map/ppermute | solution.py:65
  106.4 4.8 %collective-permute-done.13 = bf16[64,3584]{1,0:T(8,128)(2,1)S(1)} collective-permute-done((bf16[64,3584]{1,0:T(8,128)(2,1)S(1)}, bf16[64,3584]{1,0:T(8,128)(2,1)S(1)}, u32[]{:S(2)}, u32[]{:S(2)}) %collective-permute-start.13) | collective-permute-done | bytes 458784 | tf_op jit(solution)/shard_map/ppermute | solution.py:65
  111.7 15.9 %all_to_all.23 = bf16[32,2,3584]{2,1,0:T(2,128)(2,1)S(1)} all-to-all(bf16[32,2,3584]{2,1,0:T(2,128)(2,1)S(1)} %all_to_all.18), channel_id=1, replica_groups={{0,4,8,12,16,20,24,28,32,36,40,44,48,52,56,60,64,68,72,76,80,84,88,92,9..., dimensions={0} | all-to-all | bytes 917504 | tf_op jit(solution)/shard_map/all_to_all | solution.py:45
  127.9 17.1 %collective-permute-start.15 = (bf16[2,3584]{1,0:T(2,128)(2,1)S(1)}, bf16[2,3584]{1,0:T(2,128)(2,1)S(1)}, u32[]{:S(2)}, u32[]{:S(2)}) collective-permute-start(bf16[2,3584]{1,0:T(2,128)(2,1)S(1)} %reduce_sum.12), channel_id=1, source_target_pairs={{0,0},{4,4},{8,8},{12,12},{16,16},{20,20},{24,24},{28,28},{32,32},... | collective-permute-start | bytes 43016 | tf_op jit(solution)/shard_map/ppermute | solution.py:487
  145.1 1.4 collective-permute-done.15
  (39 shorter events, 10.6 us)
Async XLA Ops:
  0.0 10.8 %copy-start = (s32[512,128]{1,0:T(8,128)S(1)}, s32[512,128]{1,0:T(8,128)}, u32[]{:S(2)}) copy-start(s32[512,128]{1,0:T(8,128)} %param.10) | copy-start | bytes 786436
  1.7 19.8 %all-to-all-start = ((bf16[8,2,8704]{2,1,0:T(2,128)(2,1)}), bf16[8,2,8704]{2,1,0:T(2,128)(2,1)S(1)}, u32[]{:S(2)}, u32[]{:S(2)}) async-start(bf16[8,2,8704]{2,1,0:T(2,128)(2,1)} %broadcast_in_dim.2), calls=%async_computation | async-start | bytes 557056 | tf_op jit(solution)/shard_map/all_to_all | solution.py:45
  21.7 13.5 %collective-permute-start = (bf16[16,8704]{1,0:T(8,128)(2,1)S(1)}, bf16[16,8704]{1,0:T(8,128)(2,1)S(1)}, u32[]{:S(2)}, u32[]{:S(2)}) collective-permute-start(bf16[16,8704]{1,0:T(8,128)(2,1)S(1)} %all_to_all.16), channel_id=1, source_target_pairs={{0,64},{4,68},{8,72},{12,76},{16,80},{20,84},{24,88},{28,92},{32,9... | collective-permute-start | bytes 835592 | tf_op jit(solution)/shard_map/ppermute | solution.py:65
  24.5 10.7 %collective-permute-start.4 = (bf16[16,8704]{1,0:T(8,128)(2,1)S(1)}, bf16[16,8704]{1,0:T(8,128)(2,1)S(1)}, u32[]{:S(2)}, u32[]{:S(2)}) collective-permute-start(bf16[16,8704]{1,0:T(8,128)(2,1)S(1)} %all_to_all.16), channel_id=1, source_target_pairs={{0,96},{4,100},{8,104},{12,108},{16,112},{20,116},{24,120},{28,124... | collective-permute-start | bytes 835592 | tf_op jit(solution)/shard_map/ppermute | solution.py:65
  25.4 6.6 %collective-permute-start.1 = (bf16[16,8704]{1,0:T(8,128)(2,1)S(1)}, bf16[16,8704]{1,0:T(8,128)(2,1)S(1)}, u32[]{:S(2)}, u32[]{:S(2)}) collective-permute-start(bf16[16,8704]{1,0:T(8,128)(2,1)S(1)} %all_to_all.16), channel_id=1, source_target_pairs={{0,32},{4,36},{8,40},{12,44},{16,48},{20,52},{24,56},{28,60},{32,6... | collective-permute-start | bytes 835592 | tf_op jit(solution)/shard_map/ppermute | solution.py:65
  32.0 10.3 %collective-permute-start.2 = (bf16[32,8704]{1,0:T(8,128)(2,1)S(1)}, bf16[32,8704]{1,0:T(8,128)(2,1)S(1)}, u32[]{:S(2)}, u32[]{:S(2)}) collective-permute-start(bf16[32,8704]{1,0:T(8,128)(2,1)S(1)} %constant_dynamic-update-slice_fusion.refs_0_), channel_id=1, source_target_pairs={{0,1},{4,5},{8,9},{12,13},{16,17},{20,21},{24,25},{28,29},{32,33},... | collective-permute-start | bytes 1671176 | tf_op jit(solution)/shard_map/ppermute | solution.py:65
  33.4 9.0 %collective-permute-start.3 = (bf16[32,8704]{1,0:T(8,128)(2,1)S(1)}, bf16[32,8704]{1,0:T(8,128)(2,1)S(1)}, u32[]{:S(2)}, u32[]{:S(2)}) collective-permute-start(bf16[32,8704]{1,0:T(8,128)(2,1)S(1)} %constant_dynamic-update-slice_fusion.refs_0_), channel_id=1, source_target_pairs={{0,3},{4,7},{8,11},{12,15},{16,19},{20,23},{24,27},{28,31},{32,35}... | collective-permute-start | bytes 1671176 | tf_op jit(solution)/shard_map/ppermute | solution.py:65
  42.3 9.2 %collective-permute-start.5 = (bf16[32,8704]{1,0:T(8,128)(2,1)S(1)}, bf16[32,8704]{1,0:T(8,128)(2,1)}, u32[]{:S(2)}, u32[]{:S(2)}) collective-permute-start(bf16[32,8704]{1,0:T(8,128)(2,1)S(1)} %pad_maximum_fusion.refs_1_), channel_id=1, source_target_pairs={{0,3},{4,7},{8,11},{12,15},{16,19},{20,23},{24,27},{28,31},{32,35}... | collective-permute-start | bytes 1671176 | tf_op jit(solution)/shard_map/ppermute | solution.py:65
  45.1 19.2 %collective-permute-start.8 = (bf16[32,8704]{1,0:T(8,128)(2,1)S(1)}, bf16[32,8704]{1,0:T(8,128)(2,1)S(1)}, u32[]{:S(2)}, u32[]{:S(2)}) collective-permute-start(bf16[32,8704]{1,0:T(8,128)(2,1)S(1)} %pad_maximum_fusion.refs_1_), channel_id=1, source_target_pairs={{0,1},{4,5},{8,9},{12,13},{16,17},{20,21},{24,25},{28,29},{32,33},... | collective-permute-start | bytes 1671176 | tf_op jit(solution)/shard_map/ppermute | solution.py:65
  45.1 19.2 %collective-permute-start.6 = (bf16[32,8704]{1,0:T(8,128)(2,1)S(1)}, bf16[32,8704]{1,0:T(8,128)(2,1)}, u32[]{:S(2)}, u32[]{:S(2)}) collective-permute-start(bf16[32,8704]{1,0:T(8,128)(2,1)S(1)} %collective-permute-done.2.refs_3_), channel_id=1, source_target_pairs={{0,1},{4,5},{8,9},{12,13},{16,17},{20,21},{24,25},{28,29},{32,33},... | collective-permute-start | bytes 1671176 | tf_op jit(solution)/shard_map/ppermute | solution.py:65
  51.5 12.7 %collective-permute-start.7 = (bf16[32,8704]{1,0:T(8,128)(2,1)}, bf16[32,8704]{1,0:T(8,128)(2,1)}, u32[]{:S(2)}, u32[]{:S(2)}) collective-permute-start(bf16[32,8704]{1,0:T(8,128)(2,1)} %collective-permute-done.5.refs_2_), channel_id=1, source_target_pairs={{0,3},{4,7},{8,11},{12,15},{16,19},{20,23},{24,27},{28,31},{32,35}... | collective-permute-start | bytes 1671176 | tf_op jit(solution)/shard_map/ppermute | solution.py:65
  55.5 8.7 %copy-start.1 = (s32[128,256]{1,0:T(8,128)S(1)}, s32[128,256]{1,0:T(8,128)}, u32[]{:S(2)}) copy-start(s32[128,256]{1,0:T(8,128)} %shard_map.64.refs_4_.word_ref) | copy-start | bytes 393220
  64.3 15.8 %copy-start.2 = (bf16[2,256,256]{2,1,0:T(8,128)(2,1)S(1)}, bf16[2,256,256]{2,1,0:T(8,128)(2,1)}, u32[]{:S(2)}) copy-start(bf16[2,256,256]{2,1,0:T(8,128)(2,1)} %constant.51.clone) | copy-start | bytes 786436
  68.3 5.0 %collective-permute-start.10 = (f32[72,256]{1,0:T(8,128)S(1)}, f32[72,256]{1,0:T(8,128)S(1)}, u32[]{:S(2)}, u32[]{:S(2)}) collective-permute-start(f32[72,256]{1,0:T(8,128)S(1)} %get-tuple-element.35), channel_id=1, source_target_pairs={{0,2},{4,6},{8,10},{12,14},{16,18},{20,22},{24,26},{28,30},{32,34}... | collective-permute-start | bytes 221192 | tf_op jit(solution)/shard_map/ppermute | solution.py:65
  68.6 4.7 %collective-permute-start.11 = (f32[72,256]{1,0:T(8,128)S(1)}, f32[72,256]{1,0:T(8,128)S(1)}, u32[]{:S(2)}, u32[]{:S(2)}) collective-permute-start(f32[72,256]{1,0:T(8,128)S(1)} %get-tuple-element.36), channel_id=1, source_target_pairs={{0,3},{4,7},{8,11},{12,15},{16,19},{20,23},{24,27},{28,31},{32,35}... | collective-permute-start | bytes 221192 | tf_op jit(solution)/shard_map/ppermute | solution.py:65
  69.4 4.7 %collective-permute-start.9 = (f32[72,256]{1,0:T(8,128)S(1)}, f32[72,256]{1,0:T(8,128)S(1)}, u32[]{:S(2)}, u32[]{:S(2)}) collective-permute-start(f32[72,256]{1,0:T(8,128)S(1)} %get-tuple-element.34), channel_id=1, source_target_pairs={{0,1},{4,5},{8,9},{12,13},{16,17},{20,21},{24,25},{28,29},{32,33},... | collective-permute-start | bytes 221192 | tf_op jit(solution)/shard_map/ppermute | solution.py:65
  75.2 16.3 %all-to-all-start.1 = ((f32[32,16,256]{2,1,0:T(8,128)}), f32[32,16,256]{2,1,0:T(8,128)S(1)}, u32[]{:S(2)}, u32[]{:S(2)}) async-start(f32[32,16,256]{2,1,0:T(8,128)} %shard_map.67), calls=%async_computation.1 | async-start | bytes 1048576 | tf_op jit(solution)/shard_map/all_to_all | solution.py:45
  96.7 9.7 %collective-permute-start.12 = (bf16[64,3584]{1,0:T(8,128)(2,1)S(1)}, bf16[64,3584]{1,0:T(8,128)(2,1)S(1)}, u32[]{:S(2)}, u32[]{:S(2)}) collective-permute-start(bf16[64,3584]{1,0:T(8,128)(2,1)S(1)} %get-tuple-element.38), channel_id=1, source_target_pairs={{0,2},{4,6},{8,10},{12,14},{16,18},{20,22},{24,26},{28,30},{32,34}... | collective-permute-start | bytes 1376264 | tf_op jit(solution)/shard_map/ppermute | solution.py:65
  97.5 13.8 %collective-permute-start.13 = (bf16[64,3584]{1,0:T(8,128)(2,1)S(1)}, bf16[64,3584]{1,0:T(8,128)(2,1)S(1)}, u32[]{:S(2)}, u32[]{:S(2)}) collective-permute-start(bf16[64,3584]{1,0:T(8,128)(2,1)S(1)} %get-tuple-element.39), channel_id=1, source_target_pairs={{0,1},{4,5},{8,9},{12,13},{16,17},{20,21},{24,25},{28,29},{32,33},... | collective-permute-start | bytes 1376264 | tf_op jit(solution)/shard_map/ppermute | solution.py:65
  98.4 12.9 %collective-permute-start.14 = (bf16[64,3584]{1,0:T(8,128)(2,1)S(1)}, bf16[64,3584]{1,0:T(8,128)(2,1)S(1)}, u32[]{:S(2)}, u32[]{:S(2)}) collective-permute-start(bf16[64,3584]{1,0:T(8,128)(2,1)S(1)} %get-tuple-element.40), channel_id=1, source_target_pairs={{0,3},{4,7},{8,11},{12,15},{16,19},{20,23},{24,27},{28,31},{32,35}... | collective-permute-start | bytes 1376264 | tf_op jit(solution)/shard_map/ppermute | solution.py:65
  127.9 18.5 %collective-permute-start.15 = (bf16[2,3584]{1,0:T(2,128)(2,1)S(1)}, bf16[2,3584]{1,0:T(2,128)(2,1)S(1)}, u32[]{:S(2)}, u32[]{:S(2)}) collective-permute-start(bf16[2,3584]{1,0:T(2,128)(2,1)S(1)} %reduce_sum.12), channel_id=1, source_target_pairs={{0,0},{4,4},{8,8},{12,12},{16,16},{20,20},{24,24},{28,28},{32,32},... | collective-permute-start | bytes 43016 | tf_op jit(solution)/shard_map/ppermute | solution.py:487

commit v8 on v6

--- a/solution.py
+++ b/solution.py
@@ -138,7 +138,7 @@
 
 DEPTH = 512
 EARLY_LIMIT = 40 * 1024 * 1024
-GRADIENT_LIMIT = 48 * 1024 * 1024
+NEAR_LIMIT = 48 * 1024 * 1024
 LATE_LIMIT = 16 * 1024 * 1024
 
 
@@ -357,15 +357,42 @@
     return jnp.dot(chosen, value, preferred_element_type=jnp.float32)
 
 
-def gradient(slots, words, logit, arrived, order, student_cols, per_shard):
+def bring_near(head, pieces):
+    def kernel(head_hbm, *refs):
+        near_refs, sem = refs[:pieces], refs[pieces]
+        copies = [
+            pltpu.make_async_copy(head_hbm.at[pl.ds(k * DEPTH, DEPTH)], near_refs[k], sem.at[k])
+            for k in range(pieces)
+        ]
+        for copy in copies:
+            copy.start()
+        for copy in copies:
+            copy.wait()
+
+    return pl.pallas_call(
+        kernel,
+        in_specs=[pl.BlockSpec(memory_space=pltpu.HBM)],
+        out_specs=[pl.BlockSpec(memory_space=pltpu.VMEM)] * pieces,
+        out_shape=[jax.ShapeDtypeStruct((DEPTH, head.shape[1]), head.dtype)] * pieces,
+        scratch_shapes=[pltpu.SemaphoreType.DMA((pieces,))],
+        cost_estimate=pl.CostEstimate(
+            flops=2 * head.size * 512, bytes_accessed=2 * head.size, transcendentals=0
+        ),
+        compiler_params=pltpu.CompilerParams(vmem_limit_bytes=NEAR_LIMIT),
+    )(head)
+
+
+def gradient(slots, words, logit, arrived, order, pieces, student_cols, per_shard):
     cols, rows = logit.shape
     ds = student_cols.shape[0]
-    width = 512
+    count, width = len(pieces), pieces[0].shape[0]
+    rest = ds - count * width
     block = rows // 4
 
-    def kernel(slot_ref, word_ref, logit_ref, msg_ref, order_ref, w_hbm, *refs):
-        out_refs, (kl_ref, near_ref, w_ref, w_sem) = refs[:4], refs[4:]
-        copies = fetch(w_hbm, width, w_ref, w_sem)
+    def kernel(slot_ref, word_ref, logit_ref, msg_ref, order_ref, *refs):
+        near_w, w_hbm, out_refs = refs[:count], refs[count], refs[count + 1 : count + 5]
+        kl_ref, near_ref, w_ref, w_sem = refs[count + 5 :]
+        copies = fetch(w_hbm.at[pl.ds(count * width, rest)], width, w_ref, w_sem)
 
         def sums(at):
             top_each = msg_ref[:, at, :]
@@ -398,10 +425,14 @@
             near_ref[n * block : (n + 1) * block, :] = kl_ref[pl.ds(at, block), :]
         for k in range(ds // width):
             span = slice(k * width, (k + 1) * width)
-            copies[k].wait()
+            if k < count:
+                piece = near_w[k][...]
+            else:
+                copies[k - count].wait()
+                piece = w_ref[(k - count) * width : (k - count + 1) * width, :]
             term = lax.dot_general(
                 near_ref[...],
-                w_ref[span, :],
+                piece,
                 (((1,), (1,)), ((), ())),
                 preferred_element_type=jnp.float32,
             ).astype(jnp.bfloat16)
@@ -412,18 +443,18 @@
     return pl.pallas_call(
         kernel,
         in_specs=[pl.BlockSpec(memory_space=pltpu.SMEM)]
-        + [whole] * 4
+        + [whole] * (4 + count)
         + [pl.BlockSpec(memory_space=pltpu.HBM)],
         out_specs=[whole] * 4,
         out_shape=[jax.ShapeDtypeStruct((block, ds), jnp.bfloat16)] * 4,
         scratch_shapes=[
             pltpu.VMEM((rows, cols), jnp.bfloat16),
             pltpu.VMEM((rows, cols), jnp.bfloat16),
-            pltpu.VMEM(student_cols.shape, jnp.bfloat16),
-            pltpu.SemaphoreType.DMA((ds // width,)),
+            pltpu.VMEM((rest, cols), jnp.bfloat16),
+            pltpu.SemaphoreType.DMA((rest // width,)),
         ],
-        compiler_params=pltpu.CompilerParams(vmem_limit_bytes=GRADIENT_LIMIT),
-    )(slots, words, logit, arrived, order, student_cols)
+        compiler_params=pltpu.CompilerParams(vmem_limit_bytes=NEAR_LIMIT),
+    )(slots, words, logit, arrived, order, *pieces, student_cols)
 
 
 def per_device(teacher_hidden, teacher_head, student_hidden, student_head, tiles):
@@ -469,13 +500,15 @@
     near = (
         message[0], along(message[1], 1), along(message[2], 2), along(message[3], -1),
     )
-    arrived = exchange(regroup(near), PLANES_YZ + PLANES_XZ)
+    joined, student_far = lax.optimization_barrier((regroup(near), student_cols))
+    arrived = exchange(joined, PLANES_YZ + PLANES_XZ)
+    student_near = bring_near(student_far, 2)
 
     order = lax.dynamic_index_in_dim(
         jnp.asarray(row_orders(), jnp.bfloat16), core, 0, keepdims=False
     )
     kept, after_chip, opposite_chip, last_chip = gradient(
-        slots, words, logit, arrived, order, student_cols, per_shard
+        slots, words, logit, arrived, order, student_near, student_cols, per_shard
     )
     terms = (kept, along(opposite_chip, 2), along(after_chip, 1), along(last_chip, -1))
     near = sum(term.astype(jnp.float32) for term in terms)

time: 134 us -> 133 us (level)
  waiting for transfers between devices: 45.8 us -> 43.1 us
  local copies, waits for them, and re-layouts: 3.31 us -> 5.58 us
    all_to_all x2, waiting for transfers between devices: 17.1 us -> 14.3 us  [exchange(): lax.all_to_all(value, WHOLE, 0, 0, tiled=True, axis_index_groups=groups)]
    unnamed x9 -> x11, local copies, waits for them, and re-layouts: 0.65 us -> 2.94 us
where the time goes in v8:
time: 133 us; the launch traced here: 132 us
  waiting for transfers between devices  43.1 us (32%)
  starting transfers between devices  40.3 us (30%)
  Pallas kernels  23.2 us (17%)
  blocking collectives  18.5 us (14%)
  local copies, waits for them, and re-layouts  5.58 us (4%)
  other arithmetic  1.61 us (1%)
    ppermute x15, waiting for transfers between devices, step(): return lax.ppermute(value, WHOLE, pairs)  27.4 us
    all_to_all x1, blocking collectives, exchange(): lax.all_to_all(value, WHOLE, 0, 0, tiled=True, axis_index_groups=groups)  18.5 us
    ppermute x15, starting transfers between devices, step(): return lax.ppermute(value, WHOLE, pairs)  18.1 us
    all_to_all x2, waiting for transfers between devices, exchange(): lax.all_to_all(value, WHOLE, 0, 0, tiled=True, axis_index_groups=groups)  14.3 us
    all_to_all x2, starting transfers between devices, exchange(): lax.all_to_all(value, WHOLE, 0, 0, tiled=True, axis_index_groups=groups)  14.1 us
    pallas_call x1, Pallas kernels, early_logits(): pl.pallas_call(kernel, in_specs=[whole] * count + [pl.BlockSpec(memory_sp...  8.69 us
    ppermute x1, starting transfers between devices, per_device(): return lax.ppermute(summed.astype(jnp.bfloat16), WHOLE, last_hop())  8.1 us
    pallas_call x1, Pallas kernels, tile_words(): pl.pallas_call(kernel, out_shape=jax.ShapeDtypeStruct((count, rows), jnp....  4.71 us
  transfers between devices with their start and end apart: 18, of which 12 were waited for; matrix products, arithmetic and copies ran while one was open for 1% of the time, Pallas kernels for 10%

profile of v8, /device:TPU:1, one launch (start us, length us, event | category | flops | bytes accessed | tf_op | source)
XLA Modules:
  0.0 132.5 jit_solution(8228354384943028265)
XLA Ops:
  1.7 9.0 %all-to-all-start = ((bf16[8,2,8704]{2,1,0:T(2,128)(2,1)}), bf16[8,2,8704]{2,1,0:T(2,128)(2,1)S(1)}, u32[]{:S(2)}, u32[]{:S(2)}) async-start(bf16[8,2,8704]{2,1,0:T(2,128)(2,1)} %broadcast_in_dim.2), calls=%async_computation | async-start | bytes 557056 | tf_op jit(solution)/shard_map/all_to_all | solution.py:45
  11.6 4.7 %shard_map.64.refs_4_.word_ref = s32[128,256]{1,0:T(8,128)} custom-call(s32[128,256]{1,0:T(8,128)} %copy.11.tiles_ref), custom_call_target="tpu_custom_call" | custom-call | flops 67108864 | bytes 262144 | tf_op jit(solution)/shard_map/pallas_call | solution.py:121
  16.3 5.3 %all-to-all-done = bf16[8,2,8704]{2,1,0:T(2,128)(2,1)S(1)} async-done(((bf16[8,2,8704]{2,1,0:T(2,128)(2,1)}), bf16[8,2,8704]{2,1,0:T(2,128)(2,1)S(1)}, u32[]{:S(2)}, u32[]{:S(2)}) %all-to-all-start) | async-done | bytes 278560 | tf_op jit(solution)/shard_map/all_to_all | solution.py:45
  21.6 2.8 %collective-permute-start = (bf16[16,8704]{1,0:T(8,128)(2,1)S(1)}, bf16[16,8704]{1,0:T(8,128)(2,1)S(1)}, u32[]{:S(2)}, u32[]{:S(2)}) collective-permute-start(bf16[16,8704]{1,0:T(8,128)(2,1)S(1)} %all_to_all.16), channel_id=1, source_target_pairs={{0,64},{4,68},{8,72},{12,76},{16,80},{20,84},{24,88},{28,92},{32,9... | collective-permute-start | bytes 835592 | tf_op jit(solution)/shard_map/ppermute | solution.py:65
  26.0 2.9 %collective-permute-done = bf16[16,8704]{1,0:T(8,128)(2,1)S(1)} collective-permute-done((bf16[16,8704]{1,0:T(8,128)(2,1)S(1)}, bf16[16,8704]{1,0:T(8,128)(2,1)S(1)}, u32[]{:S(2)}, u32[]{:S(2)}) %collective-permute-start) | collective-permute-done | bytes 278560 | tf_op jit(solution)/shard_map/ppermute | solution.py:65
  28.9 2.8 %collective-permute-done.2 = bf16[16,8704]{1,0:T(8,128)(2,1)S(1)} collective-permute-done((bf16[16,8704]{1,0:T(8,128)(2,1)S(1)}, bf16[16,8704]{1,0:T(8,128)(2,1)S(1)}, u32[]{:S(2)}, u32[]{:S(2)}) %collective-permute-start.2) | collective-permute-done | bytes 278560 | tf_op jit(solution)/shard_map/ppermute | solution.py:65
  31.8 3.1 %collective-permute-start.3 = (bf16[32,8704]{1,0:T(8,128)(2,1)S(1)}, bf16[32,8704]{1,0:T(8,128)(2,1)S(1)}, u32[]{:S(2)}, u32[]{:S(2)}) collective-permute-start(bf16[32,8704]{1,0:T(8,128)(2,1)S(1)} %constant_dynamic-update-slice_fusion.2.refs_1_), channel_id=1, source_target_pairs={{0,3},{4,7},{8,11},{12,15},{16,19},{20,23},{24,27},{28,31},{32,35}... | collective-permute-start | bytes 1671176 | tf_op jit(solution)/shard_map/ppermute | solution.py:65
  35.1 2.7 %collective-permute-start.5 = (bf16[32,8704]{1,0:T(8,128)(2,1)S(1)}, bf16[32,8704]{1,0:T(8,128)(2,1)S(1)}, u32[]{:S(2)}, u32[]{:S(2)}) collective-permute-start(bf16[32,8704]{1,0:T(8,128)(2,1)S(1)} %constant_dynamic-update-slice_fusion.refs_0_), channel_id=1, source_target_pairs={{0,3},{4,7},{8,11},{12,15},{16,19},{20,23},{24,27},{28,31},{32,35}... | collective-permute-start | bytes 1671176 | tf_op jit(solution)/shard_map/ppermute | solution.py:65
  37.8 3.6 %collective-permute-done.3.refs_2_ = bf16[32,8704]{1,0:T(8,128)(2,1)S(1)} collective-permute-done((bf16[32,8704]{1,0:T(8,128)(2,1)S(1)}, bf16[32,8704]{1,0:T(8,128)(2,1)S(1)}, u32[]{:S(2)}, u32[]{:S(2)}) %collective-permute-start.3) | collective-permute-done | bytes 557088 | tf_op jit(solution)/shard_map/ppermute | solution.py:65
  41.4 3.1 %collective-permute-start.7 = (bf16[32,8704]{1,0:T(8,128)(2,1)S(1)}, bf16[32,8704]{1,0:T(8,128)(2,1)}, u32[]{:S(2)}, u32[]{:S(2)}) collective-permute-start(bf16[32,8704]{1,0:T(8,128)(2,1)S(1)} %collective-permute-done.3.refs_2_), channel_id=1, source_target_pairs={{0,3},{4,7},{8,11},{12,15},{16,19},{20,23},{24,27},{28,31},{32,35}... | collective-permute-start | bytes 1671176 | tf_op jit(solution)/shard_map/ppermute | solution.py:65
  45.8 8.7 %shard_map.65 = (f32[128,1280]{1,0:T(8,128)S(1)}, bf16[2560,640]{1,0:T(8,128)(2,1)S(1)}, bf16[2560,640]{1,0:T(8,128)(2,1)S(1)}, bf16[3584,640]{1,0:T(8,128)(2,1)S(1)}) custom-call(bf16[32,8704]{1,0:T(8,128)(2,1)S(1)} %constant_dynamic-update-slice_fusion.refs_0_, bf16[32,8704]{1,0:T(8,128)(2,1)S(1)} %constant_dynamic-update-slice_fusion.2.refs_1_, ...), custom_call_target="tpu_custom_call" | custom-call | flops 1426063360 | bytes 11141120 | tf_op jit(solution)/shard_map/pallas_call | solution.py:189
  54.5 2.4 %collective-permute-done.6.refs_1_ = bf16[32,8704]{1,0:T(8,128)(2,1)} collective-permute-done((bf16[32,8704]{1,0:T(8,128)(2,1)}, bf16[32,8704]{1,0:T(8,128)(2,1)}, u32[]{:S(2)}, u32[]{:S(2)}) %collective-permute-start.6) | collective-permute-done | bytes 557088 | tf_op jit(solution)/shard_map/ppermute | solution.py:65
  57.0 4.0 %shard_map.66 = (f32[72,256]{1,0:T(8,128)S(1)}, f32[72,256]{1,0:T(8,128)S(1)}, f32[72,256]{1,0:T(8,128)S(1)}, f32[72,256]{1,0:T(8,128)S(1)}, f32[640,256]{1,0:T(8,128)S(1)}) custom-call(s32[3]{0:T(128)S(1)} %pad_add_fusion.slot_ref, f32[128,1280]{1,0:T(8,128)S(1)} %get-tuple-element.26.early_ref, bf16[32,8704]{1,0:T(8,128)(2,1)S(1)} %collective-permute-done.5.refs_0_, ...), custom_call_target="tpu_custom_call" | custom-call | flops 1426063360 | bytes 11141120 | tf_op jit(solution)/shard_map/pallas_call | solution.py:279
  62.8 3.1 %collective-permute-done.10.refs_2_ = f32[72,256]{1,0:T(8,128)S(1)} collective-permute-done((f32[72,256]{1,0:T(8,128)S(1)}, f32[72,256]{1,0:T(8,128)S(1)}, u32[]{:S(2)}, u32[]{:S(2)}) %collective-permute-start.10) | collective-permute-done | bytes 73760 | tf_op jit(solution)/shard_map/ppermute | solution.py:65
  67.9 5.1 %all-to-all-start.1 = ((f32[32,16,256]{2,1,0:T(8,128)}), f32[32,16,256]{2,1,0:T(8,128)S(1)}, u32[]{:S(2)}, u32[]{:S(2)}) async-start(f32[32,16,256]{2,1,0:T(8,128)} %shard_map.67), calls=%async_computation.1 | async-start | bytes 1048576 | tf_op jit(solution)/shard_map/all_to_all | solution.py:45
  73.1 2.3 %copy-done.1 = bf16[3584,640,1]{1,0,2:T(8,128)(2,1)S(1)} copy-done((bf16[3584,640,1]{1,0,2:T(8,128)(2,1)S(1)}, bf16[3584,640,1]{1,0,2:T(8,128)(2,1)}, u32[]{:S(2)}) %copy-start.1) | copy-done | bytes 4587544
  75.8 9.1 %all-to-all-done.1.msg_ref = f32[32,16,256]{2,1,0:T(8,128)S(1)} async-done(((f32[32,16,256]{2,1,0:T(8,128)}), f32[32,16,256]{2,1,0:T(8,128)S(1)}, u32[]{:S(2)}, u32[]{:S(2)}) %all-to-all-start.1) | async-done | bytes 524320 | tf_op jit(solution)/shard_map/all_to_all | solution.py:45
  84.9 4.3 %shard_map.69 = (bf16[64,3584]{1,0:T(8,128)(2,1)S(1)}, bf16[64,3584]{1,0:T(8,128)(2,1)S(1)}, bf16[64,3584]{1,0:T(8,128)(2,1)S(1)}, bf16[64,3584]{1,0:T(8,128)(2,1)S(1)}) custom-call(s32[3]{0:T(128)S(1)} %pad_add_fusion.slot_ref, s32[128,256]{1,0:T(8,128)S(1)} %copy-done.2, f32[640,256]{1,0:T(8,128)S(1)} %get-tuple-element.30.logit_ref, ...), custom_call_target="tpu_custom_call" | custom-call | tf_op jit(solution)/shard_map/pallas_call | solution.py:443
  90.2 1.8 %collective-permute-start.14 = (bf16[64,3584]{1,0:T(8,128)(2,1)S(1)}, bf16[64,3584]{1,0:T(8,128)(2,1)S(1)}, u32[]{:S(2)}, u32[]{:S(2)}) collective-permute-start(bf16[64,3584]{1,0:T(8,128)(2,1)S(1)} %get-tuple-element.42), channel_id=1, source_target_pairs={{0,3},{4,7},{8,11},{12,15},{16,19},{20,23},{24,27},{28,31},{32,35}... | collective-permute-start | bytes 1376264 | tf_op jit(solution)/shard_map/ppermute | solution.py:65
  92.1 6.1 %collective-permute-done.12 = bf16[64,3584]{1,0:T(8,128)(2,1)S(1)} collective-permute-done((bf16[64,3584]{1,0:T(8,128)(2,1)S(1)}, bf16[64,3584]{1,0:T(8,128)(2,1)S(1)}, u32[]{:S(2)}, u32[]{:S(2)}) %collective-permute-start.12) | collective-permute-done | bytes 458784 | tf_op jit(solution)/shard_map/ppermute | solution.py:65
  98.2 4.9 %collective-permute-done.13 = bf16[64,3584]{1,0:T(8,128)(2,1)S(1)} collective-permute-done((bf16[64,3584]{1,0:T(8,128)(2,1)S(1)}, bf16[64,3584]{1,0:T(8,128)(2,1)S(1)}, u32[]{:S(2)}, u32[]{:S(2)}) %collective-permute-start.13) | collective-permute-done | bytes 458784 | tf_op jit(solution)/shard_map/ppermute | solution.py:65
  103.5 18.5 %all_to_all.23 = bf16[32,2,3584]{2,1,0:T(2,128)(2,1)S(1)} all-to-all(bf16[32,2,3584]{2,1,0:T(2,128)(2,1)S(1)} %all_to_all.18), channel_id=1, replica_groups={{0,4,8,12,16,20,24,28,32,36,40,44,48,52,56,60,64,68,72,76,80,84,88,92,9..., dimensions={0} | all-to-all | bytes 917504 | tf_op jit(solution)/shard_map/all_to_all | solution.py:45
  122.4 8.1 %collective-permute-start.15 = (bf16[2,3584]{1,0:T(2,128)(2,1)S(1)}, bf16[2,3584]{1,0:T(2,128)(2,1)S(1)}, u32[]{:S(2)}, u32[]{:S(2)}) collective-permute-start(bf16[2,3584]{1,0:T(2,128)(2,1)S(1)} %reduce_sum.12), channel_id=1, source_target_pairs={{0,0},{4,4},{8,8},{12,12},{16,16},{20,20},{24,24},{28,28},{32,32},... | collective-permute-start | bytes 43016 | tf_op jit(solution)/shard_map/ppermute | solution.py:517
  130.5 1.4 %collective-permute-done.15 = bf16[2,3584]{1,0:T(2,128)(2,1)S(1)} collective-permute-done((bf16[2,3584]{1,0:T(2,128)(2,1)S(1)}, bf16[2,3584]{1,0:T(2,128)(2,1)S(1)}, u32[]{:S(2)}, u32[]{:S(2)}) %collective-permute-start.15) | collective-permute-done | bytes 14368 | tf_op jit(solution)/shard_map/ppermute | solution.py:517
  (43 shorter events, 12.4 us)
Async XLA Ops:
  0.0 10.7 %copy-start = (s32[512,128]{1,0:T(8,128)S(1)}, s32[512,128]{1,0:T(8,128)}, u32[]{:S(2)}) copy-start(s32[512,128]{1,0:T(8,128)} %param.10) | copy-start | bytes 786436
  1.7 19.8 %all-to-all-start = ((bf16[8,2,8704]{2,1,0:T(2,128)(2,1)}), bf16[8,2,8704]{2,1,0:T(2,128)(2,1)S(1)}, u32[]{:S(2)}, u32[]{:S(2)}) async-start(bf16[8,2,8704]{2,1,0:T(2,128)(2,1)} %broadcast_in_dim.2), calls=%async_computation | async-start | bytes 557056 | tf_op jit(solution)/shard_map/all_to_all | solution.py:45
  21.6 7.3 %collective-permute-start = (bf16[16,8704]{1,0:T(8,128)(2,1)S(1)}, bf16[16,8704]{1,0:T(8,128)(2,1)S(1)}, u32[]{:S(2)}, u32[]{:S(2)}) collective-permute-start(bf16[16,8704]{1,0:T(8,128)(2,1)S(1)} %all_to_all.16), channel_id=1, source_target_pairs={{0,64},{4,68},{8,72},{12,76},{16,80},{20,84},{24,88},{28,92},{32,9... | collective-permute-start | bytes 835592 | tf_op jit(solution)/shard_map/ppermute | solution.py:65
  24.5 7.3 %collective-permute-start.2 = (bf16[16,8704]{1,0:T(8,128)(2,1)S(1)}, bf16[16,8704]{1,0:T(8,128)(2,1)S(1)}, u32[]{:S(2)}, u32[]{:S(2)}) collective-permute-start(bf16[16,8704]{1,0:T(8,128)(2,1)S(1)} %all_to_all.16), channel_id=1, source_target_pairs={{0,96},{4,100},{8,104},{12,108},{16,112},{20,116},{24,120},{28,124... | collective-permute-start | bytes 835592 | tf_op jit(solution)/shard_map/ppermute | solution.py:65
  25.4 9.6 %collective-permute-start.1 = (bf16[16,8704]{1,0:T(8,128)(2,1)S(1)}, bf16[16,8704]{1,0:T(8,128)(2,1)S(1)}, u32[]{:S(2)}, u32[]{:S(2)}) collective-permute-start(bf16[16,8704]{1,0:T(8,128)(2,1)S(1)} %all_to_all.16), channel_id=1, source_target_pairs={{0,32},{4,36},{8,40},{12,44},{16,48},{20,52},{24,56},{28,60},{32,6... | collective-permute-start | bytes 835592 | tf_op jit(solution)/shard_map/ppermute | solution.py:65
  31.8 9.6 %collective-permute-start.3 = (bf16[32,8704]{1,0:T(8,128)(2,1)S(1)}, bf16[32,8704]{1,0:T(8,128)(2,1)S(1)}, u32[]{:S(2)}, u32[]{:S(2)}) collective-permute-start(bf16[32,8704]{1,0:T(8,128)(2,1)S(1)} %constant_dynamic-update-slice_fusion.2.refs_1_), channel_id=1, source_target_pairs={{0,3},{4,7},{8,11},{12,15},{16,19},{20,23},{24,27},{28,31},{32,35}... | collective-permute-start | bytes 1671176 | tf_op jit(solution)/shard_map/ppermute | solution.py:65
  34.9 10.1 %collective-permute-start.4 = (bf16[32,8704]{1,0:T(8,128)(2,1)S(1)}, bf16[32,8704]{1,0:T(8,128)(2,1)}, u32[]{:S(2)}, u32[]{:S(2)}) collective-permute-start(bf16[32,8704]{1,0:T(8,128)(2,1)S(1)} %constant_dynamic-update-slice_fusion.refs_0_), channel_id=1, source_target_pairs={{0,1},{4,5},{8,9},{12,13},{16,17},{20,21},{24,25},{28,29},{32,33},... | collective-permute-start | bytes 1671176 | tf_op jit(solution)/shard_map/ppermute | solution.py:65
  35.0 19.5 %collective-permute-start.8 = (bf16[32,8704]{1,0:T(8,128)(2,1)S(1)}, bf16[32,8704]{1,0:T(8,128)(2,1)S(1)}, u32[]{:S(2)}, u32[]{:S(2)}) collective-permute-start(bf16[32,8704]{1,0:T(8,128)(2,1)S(1)} %constant_dynamic-update-slice_fusion.2.refs_1_), channel_id=1, source_target_pairs={{0,1},{4,5},{8,9},{12,13},{16,17},{20,21},{24,25},{28,29},{32,33},... | collective-permute-start | bytes 1671176 | tf_op jit(solution)/shard_map/ppermute | solution.py:65
  35.1 19.4 %collective-permute-start.5 = (bf16[32,8704]{1,0:T(8,128)(2,1)S(1)}, bf16[32,8704]{1,0:T(8,128)(2,1)S(1)}, u32[]{:S(2)}, u32[]{:S(2)}) collective-permute-start(bf16[32,8704]{1,0:T(8,128)(2,1)S(1)} %constant_dynamic-update-slice_fusion.refs_0_), channel_id=1, source_target_pairs={{0,3},{4,7},{8,11},{12,15},{16,19},{20,23},{24,27},{28,31},{32,35}... | collective-permute-start | bytes 1671176 | tf_op jit(solution)/shard_map/ppermute | solution.py:65
  41.4 13.1 %collective-permute-start.7 = (bf16[32,8704]{1,0:T(8,128)(2,1)S(1)}, bf16[32,8704]{1,0:T(8,128)(2,1)}, u32[]{:S(2)}, u32[]{:S(2)}) collective-permute-start(bf16[32,8704]{1,0:T(8,128)(2,1)S(1)} %collective-permute-done.3.refs_2_), channel_id=1, source_target_pairs={{0,3},{4,7},{8,11},{12,15},{16,19},{20,23},{24,27},{28,31},{32,35}... | collective-permute-start | bytes 1671176 | tf_op jit(solution)/shard_map/ppermute | solution.py:65
  45.0 11.9 %collective-permute-start.6 = (bf16[32,8704]{1,0:T(8,128)(2,1)}, bf16[32,8704]{1,0:T(8,128)(2,1)}, u32[]{:S(2)}, u32[]{:S(2)}) collective-permute-start(bf16[32,8704]{1,0:T(8,128)(2,1)} %collective-permute-done.4.refs_3_), channel_id=1, source_target_pairs={{0,1},{4,5},{8,9},{12,13},{16,17},{20,21},{24,25},{28,29},{32,33},... | collective-permute-start | bytes 1671176 | tf_op jit(solution)/shard_map/ppermute | solution.py:65
  45.8 11.2 %copy-start.2 = (s32[128,256]{1,0:T(8,128)S(1)}, s32[128,256]{1,0:T(8,128)}, u32[]{:S(2)}) copy-start(s32[128,256]{1,0:T(8,128)} %shard_map.64.refs_4_.word_ref) | copy-start | bytes 393220
  56.9 16.1 %copy-start.3 = (bf16[2,256,256]{2,1,0:T(8,128)(2,1)S(1)}, bf16[2,256,256]{2,1,0:T(8,128)(2,1)}, u32[]{:S(2)}) copy-start(bf16[2,256,256]{2,1,0:T(8,128)(2,1)} %constant.51.clone) | copy-start | bytes 786436
  61.0 5.0 %collective-permute-start.10 = (f32[72,256]{1,0:T(8,128)S(1)}, f32[72,256]{1,0:T(8,128)S(1)}, u32[]{:S(2)}, u32[]{:S(2)}) collective-permute-start(f32[72,256]{1,0:T(8,128)S(1)} %get-tuple-element.33), channel_id=1, source_target_pairs={{0,2},{4,6},{8,10},{12,14},{16,18},{20,22},{24,26},{28,30},{32,34}... | collective-permute-start | bytes 221192 | tf_op jit(solution)/shard_map/ppermute | solution.py:65
  61.3 4.7 %collective-permute-start.11 = (f32[72,256]{1,0:T(8,128)S(1)}, f32[72,256]{1,0:T(8,128)S(1)}, u32[]{:S(2)}, u32[]{:S(2)}) collective-permute-start(f32[72,256]{1,0:T(8,128)S(1)} %get-tuple-element.34), channel_id=1, source_target_pairs={{0,3},{4,7},{8,11},{12,15},{16,19},{20,23},{24,27},{28,31},{32,35}... | collective-permute-start | bytes 221192 | tf_op jit(solution)/shard_map/ppermute | solution.py:65
  62.5 4.4 %collective-permute-start.9 = (f32[72,256]{1,0:T(8,128)S(1)}, f32[72,256]{1,0:T(8,128)S(1)}, u32[]{:S(2)}, u32[]{:S(2)}) collective-permute-start(f32[72,256]{1,0:T(8,128)S(1)} %get-tuple-element.32), channel_id=1, source_target_pairs={{0,1},{4,5},{8,9},{12,13},{16,17},{20,21},{24,25},{28,29},{32,33},... | collective-permute-start | bytes 221192 | tf_op jit(solution)/shard_map/ppermute | solution.py:65
  67.9 17.0 %all-to-all-start.1 = ((f32[32,16,256]{2,1,0:T(8,128)}), f32[32,16,256]{2,1,0:T(8,128)S(1)}, u32[]{:S(2)}, u32[]{:S(2)}) async-start(f32[32,16,256]{2,1,0:T(8,128)} %shard_map.67), calls=%async_computation.1 | async-start | bytes 1048576 | tf_op jit(solution)/shard_map/all_to_all | solution.py:45
  73.1 2.3 %copy-start.1 = (bf16[3584,640,1]{1,0,2:T(8,128)(2,1)S(1)}, bf16[3584,640,1]{1,0,2:T(8,128)(2,1)}, u32[]{:S(2)}) copy-start(bf16[3584,640,1]{1,0,2:T(8,128)(2,1)} %param.9) | copy-start | bytes 13762564
  89.2 9.0 %collective-permute-start.12 = (bf16[64,3584]{1,0:T(8,128)(2,1)S(1)}, bf16[64,3584]{1,0:T(8,128)(2,1)S(1)}, u32[]{:S(2)}, u32[]{:S(2)}) collective-permute-start(bf16[64,3584]{1,0:T(8,128)(2,1)S(1)} %get-tuple-element.40), channel_id=1, source_target_pairs={{0,2},{4,6},{8,10},{12,14},{16,18},{20,22},{24,26},{28,30},{32,34}... | collective-permute-start | bytes 1376264 | tf_op jit(solution)/shard_map/ppermute | solution.py:65
  89.4 13.8 %collective-permute-start.13 = (bf16[64,3584]{1,0:T(8,128)(2,1)S(1)}, bf16[64,3584]{1,0:T(8,128)(2,1)S(1)}, u32[]{:S(2)}, u32[]{:S(2)}) collective-permute-start(bf16[64,3584]{1,0:T(8,128)(2,1)S(1)} %get-tuple-element.41), channel_id=1, source_target_pairs={{0,1},{4,5},{8,9},{12,13},{16,17},{20,21},{24,25},{28,29},{32,33},... | collective-permute-start | bytes 1376264 | tf_op jit(solution)/shard_map/ppermute | solution.py:65
  90.2 12.9 %collective-permute-start.14 = (bf16[64,3584]{1,0:T(8,128)(2,1)S(1)}, bf16[64,3584]{1,0:T(8,128)(2,1)S(1)}, u32[]{:S(2)}, u32[]{:S(2)}) collective-permute-start(bf16[64,3584]{1,0:T(8,128)(2,1)S(1)} %get-tuple-element.42), channel_id=1, source_target_pairs={{0,3},{4,7},{8,11},{12,15},{16,19},{20,23},{24,27},{28,31},{32,35}... | collective-permute-start | bytes 1376264 | tf_op jit(solution)/shard_map/ppermute | solution.py:65
  122.4 9.5 %collective-permute-start.15 = (bf16[2,3584]{1,0:T(2,128)(2,1)S(1)}, bf16[2,3584]{1,0:T(2,128)(2,1)S(1)}, u32[]{:S(2)}, u32[]{:S(2)}) collective-permute-start(bf16[2,3584]{1,0:T(2,128)(2,1)S(1)} %reduce_sum.12), channel_id=1, source_target_pairs={{0,0},{4,4},{8,8},{12,12},{16,16},{20,20},{24,24},{28,28},{32,32},... | collective-permute-start | bytes 43016 | tf_op jit(solution)/shard_map/ppermute | solution.py:517

commit v9 on v8

--- a/solution.py
+++ b/solution.py
@@ -45,11 +45,23 @@
     return lax.all_to_all(value, WHOLE, 0, 0, tiled=True, axis_index_groups=groups)
 
 
-def spread(value, groups):
-    count = len(groups[0])
-    rows, width = value.shape
-    copies = jnp.broadcast_to(value[None], (count, rows, width)).reshape(count * rows, width)
-    return exchange(copies, groups)
+def row_copies(core, teacher_hidden, student_hidden):
+    dt, ds = teacher_hidden.shape[1], student_hidden.shape[1]
+
+    def kernel(core_ref, t_ref, s_ref, out_ref):
+        for ref, span in ((t_ref, slice(0, dt)), (s_ref, slice(dt, dt + ds))):
+            rows = ref[...].astype(jnp.float32)
+            rows = jnp.where(core_ref[0] == 0, rows[:2], rows[2:]).astype(jnp.bfloat16)
+            for k in range(NZ):
+                out_ref[k, :, span] = rows
+
+    whole = pl.BlockSpec(memory_space=pltpu.VMEM)
+    return pl.pallas_call(
+        kernel,
+        in_specs=[pl.BlockSpec(memory_space=pltpu.SMEM), whole, whole],
+        out_specs=whole,
+        out_shape=jax.ShapeDtypeStruct((NZ, 2, dt + ds), jnp.bfloat16),
+    )(core, teacher_hidden, student_hidden)
 
 
 def step(value, axes, by):
@@ -466,9 +478,9 @@
     per_shard = tiles_all // shards
     picks = tiles.shape[1]
 
-    both = jnp.concatenate((teacher_hidden, student_hidden), axis=1)
-    mine = lax.dynamic_slice_in_dim(both, 2 * core, 2, 0)
-    gathered = spread(mine, LINES_Z)
+    copies = row_copies(core.reshape(1), teacher_hidden, student_hidden)
+    gathered = exchange(copies.reshape(2 * NZ, copies.shape[2]), LINES_Z)
+
     by_chip = tiles.reshape(NY, NZ, NX, 2, 2, picks)
     by_chip = lax.dynamic_index_in_dim(by_chip, core, 3, keepdims=False)
     tiles_t = jnp.where(

time: 133 us -> 133 us (level)
  Pallas kernels: 23.2 us -> 24.8 us
    pallas_call x0 -> x1, Pallas kernels: none -> 1.57 us  [row_copies(): pl.pallas_call(kernel, in_specs=[pl.BlockSpec(memory_space=pltpu.SMEM), w...]
where the time goes in v9:
time: 133 us; the launch traced here: 132 us
  waiting for transfers between devices  43.1 us (32%)
  starting transfers between devices  40.3 us (30%)
  Pallas kernels  24.8 us (19%)
  blocking collectives  18.5 us (14%)
  local copies, waits for them, and re-layouts  4.73 us (4%)
    ppermute x15, waiting for transfers between devices, step(): return lax.ppermute(value, WHOLE, pairs)  27.4 us
    all_to_all x1, blocking collectives, exchange(): lax.all_to_all(value, WHOLE, 0, 0, tiled=True, axis_index_groups=groups)  18.5 us
    ppermute x15, starting transfers between devices, step(): return lax.ppermute(value, WHOLE, pairs)  18.1 us
    all_to_all x2, waiting for transfers between devices, exchange(): lax.all_to_all(value, WHOLE, 0, 0, tiled=True, axis_index_groups=groups)  14.3 us
    all_to_all x2, starting transfers between devices, exchange(): lax.all_to_all(value, WHOLE, 0, 0, tiled=True, axis_index_groups=groups)  14.1 us
    pallas_call x1, Pallas kernels, early_logits(): pl.pallas_call(kernel, in_specs=[whole] * count + [pl.BlockSpec(memory_sp...  8.69 us
    ppermute x1, starting transfers between devices, per_device(): return lax.ppermute(summed.astype(jnp.bfloat16), WHOLE, last_hop())  8.1 us
    pallas_call x1, Pallas kernels, tile_words(): pl.pallas_call(kernel, out_shape=jax.ShapeDtypeStruct((count, rows), jnp....  4.71 us
  transfers between devices with their start and end apart: 18, of which 12 were waited for; matrix products, arithmetic and copies ran while one was open for 1% of the time, Pallas kernels for 10%

profile of v9, /device:TPU:1, one launch (start us, length us, event | category | flops | bytes accessed | tf_op | source)
XLA Modules:
  0.0 132.3 jit_solution(15956871574909560354)
XLA Ops:
  0.0 1.6 %shard_map.64 = bf16[8,2,8704]{2,1,0:T(2,128)(2,1)} custom-call(s32[1]{0:T(128)} %bitcast.2.core_ref, bf16[4,5120]{1,0:T(4,128)(2,1)} %t_ref.1, bf16[4,3584]{1,0:T(4,128)(2,1)} %s_ref.1), custom_call_target="tpu_custom_call" | custom-call | tf_op jit(solution)/shard_map/pallas_call | solution.py:59
  1.6 9.0 %all-to-all-start = ((bf16[8,2,8704]{2,1,0:T(2,128)(2,1)}), bf16[8,2,8704]{2,1,0:T(2,128)(2,1)S(1)}, u32[]{:S(2)}, u32[]{:S(2)}) async-start(bf16[8,2,8704]{2,1,0:T(2,128)(2,1)} %shard_map.64), calls=%async_computation | async-start | bytes 557056 | tf_op jit(solution)/shard_map/all_to_all | solution.py:45
  11.4 4.7 %shard_map.65.refs_4_.word_ref = s32[128,256]{1,0:T(8,128)} custom-call(s32[128,256]{1,0:T(8,128)} %copy.11.tiles_ref), custom_call_target="tpu_custom_call" | custom-call | flops 67108864 | bytes 262144 | tf_op jit(solution)/shard_map/pallas_call | solution.py:133
  16.1 5.3 %all-to-all-done = bf16[8,2,8704]{2,1,0:T(2,128)(2,1)S(1)} async-done(((bf16[8,2,8704]{2,1,0:T(2,128)(2,1)}), bf16[8,2,8704]{2,1,0:T(2,128)(2,1)S(1)}, u32[]{:S(2)}, u32[]{:S(2)}) %all-to-all-start) | async-done | bytes 278560 | tf_op jit(solution)/shard_map/all_to_all | solution.py:45
  21.5 2.8 %collective-permute-start = (bf16[16,8704]{1,0:T(8,128)(2,1)S(1)}, bf16[16,8704]{1,0:T(8,128)(2,1)S(1)}, u32[]{:S(2)}, u32[]{:S(2)}) collective-permute-start(bf16[16,8704]{1,0:T(8,128)(2,1)S(1)} %all_to_all.16), channel_id=1, source_target_pairs={{0,64},{4,68},{8,72},{12,76},{16,80},{20,84},{24,88},{28,92},{32,9... | collective-permute-start | bytes 835592 | tf_op jit(solution)/shard_map/ppermute | solution.py:77
  25.9 2.9 %collective-permute-done = bf16[16,8704]{1,0:T(8,128)(2,1)S(1)} collective-permute-done((bf16[16,8704]{1,0:T(8,128)(2,1)S(1)}, bf16[16,8704]{1,0:T(8,128)(2,1)S(1)}, u32[]{:S(2)}, u32[]{:S(2)}) %collective-permute-start) | collective-permute-done | bytes 278560 | tf_op jit(solution)/shard_map/ppermute | solution.py:77
  28.8 2.8 %collective-permute-done.2 = bf16[16,8704]{1,0:T(8,128)(2,1)S(1)} collective-permute-done((bf16[16,8704]{1,0:T(8,128)(2,1)S(1)}, bf16[16,8704]{1,0:T(8,128)(2,1)S(1)}, u32[]{:S(2)}, u32[]{:S(2)}) %collective-permute-start.2) | collective-permute-done | bytes 278560 | tf_op jit(solution)/shard_map/ppermute | solution.py:77
  31.7 3.1 %collective-permute-start.3 = (bf16[32,8704]{1,0:T(8,128)(2,1)S(1)}, bf16[32,8704]{1,0:T(8,128)(2,1)S(1)}, u32[]{:S(2)}, u32[]{:S(2)}) collective-permute-start(bf16[32,8704]{1,0:T(8,128)(2,1)S(1)} %constant_dynamic-update-slice_fusion.2.refs_1_), channel_id=1, source_target_pairs={{0,3},{4,7},{8,11},{12,15},{16,19},{20,23},{24,27},{28,31},{32,35}... | collective-permute-start | bytes 1671176 | tf_op jit(solution)/shard_map/ppermute | solution.py:77
  35.0 2.7 %collective-permute-start.5 = (bf16[32,8704]{1,0:T(8,128)(2,1)S(1)}, bf16[32,8704]{1,0:T(8,128)(2,1)S(1)}, u32[]{:S(2)}, u32[]{:S(2)}) collective-permute-start(bf16[32,8704]{1,0:T(8,128)(2,1)S(1)} %constant_dynamic-update-slice_fusion.refs_0_), channel_id=1, source_target_pairs={{0,3},{4,7},{8,11},{12,15},{16,19},{20,23},{24,27},{28,31},{32,35}... | collective-permute-start | bytes 1671176 | tf_op jit(solution)/shard_map/ppermute | solution.py:77
  37.6 3.6 %collective-permute-done.3.refs_2_ = bf16[32,8704]{1,0:T(8,128)(2,1)S(1)} collective-permute-done((bf16[32,8704]{1,0:T(8,128)(2,1)S(1)}, bf16[32,8704]{1,0:T(8,128)(2,1)S(1)}, u32[]{:S(2)}, u32[]{:S(2)}) %collective-permute-start.3) | collective-permute-done | bytes 557088 | tf_op jit(solution)/shard_map/ppermute | solution.py:77
  41.2 3.1 %collective-permute-start.7 = (bf16[32,8704]{1,0:T(8,128)(2,1)S(1)}, bf16[32,8704]{1,0:T(8,128)(2,1)}, u32[]{:S(2)}, u32[]{:S(2)}) collective-permute-start(bf16[32,8704]{1,0:T(8,128)(2,1)S(1)} %collective-permute-done.3.refs_2_), channel_id=1, source_target_pairs={{0,3},{4,7},{8,11},{12,15},{16,19},{20,23},{24,27},{28,31},{32,35}... | collective-permute-start | bytes 1671176 | tf_op jit(solution)/shard_map/ppermute | solution.py:77
  45.6 8.7 %shard_map.66 = (f32[128,1280]{1,0:T(8,128)S(1)}, bf16[2560,640]{1,0:T(8,128)(2,1)S(1)}, bf16[2560,640]{1,0:T(8,128)(2,1)S(1)}, bf16[3584,640]{1,0:T(8,128)(2,1)S(1)}) custom-call(bf16[32,8704]{1,0:T(8,128)(2,1)S(1)} %constant_dynamic-update-slice_fusion.refs_0_, bf16[32,8704]{1,0:T(8,128)(2,1)S(1)} %constant_dynamic-update-slice_fusion.2.refs_1_, ...), custom_call_target="tpu_custom_call" | custom-call | flops 1426063360 | bytes 11141120 | tf_op jit(solution)/shard_map/pallas_call | solution.py:201
  54.4 2.4 %collective-permute-done.6.refs_1_ = bf16[32,8704]{1,0:T(8,128)(2,1)} collective-permute-done((bf16[32,8704]{1,0:T(8,128)(2,1)}, bf16[32,8704]{1,0:T(8,128)(2,1)}, u32[]{:S(2)}, u32[]{:S(2)}) %collective-permute-start.6) | collective-permute-done | bytes 557088 | tf_op jit(solution)/shard_map/ppermute | solution.py:77
  56.8 4.0 %shard_map.67 = (f32[72,256]{1,0:T(8,128)S(1)}, f32[72,256]{1,0:T(8,128)S(1)}, f32[72,256]{1,0:T(8,128)S(1)}, f32[72,256]{1,0:T(8,128)S(1)}, f32[640,256]{1,0:T(8,128)S(1)}) custom-call(s32[3]{0:T(128)S(1)} %pad_add_fusion.slot_ref, f32[128,1280]{1,0:T(8,128)S(1)} %get-tuple-element.26.early_ref, bf16[32,8704]{1,0:T(8,128)(2,1)S(1)} %collective-permute-done.5.refs_0_, ...), custom_call_target="tpu_custom_call" | custom-call | flops 1426063360 | bytes 11141120 | tf_op jit(solution)/shard_map/pallas_call | solution.py:291
  62.7 3.1 %collective-permute-done.10.refs_2_ = f32[72,256]{1,0:T(8,128)S(1)} collective-permute-done((f32[72,256]{1,0:T(8,128)S(1)}, f32[72,256]{1,0:T(8,128)S(1)}, u32[]{:S(2)}, u32[]{:S(2)}) %collective-permute-start.10) | collective-permute-done | bytes 73760 | tf_op jit(solution)/shard_map/ppermute | solution.py:77
  67.8 5.1 %all-to-all-start.1 = ((f32[32,16,256]{2,1,0:T(8,128)}), f32[32,16,256]{2,1,0:T(8,128)S(1)}, u32[]{:S(2)}, u32[]{:S(2)}) async-start(f32[32,16,256]{2,1,0:T(8,128)} %shard_map.68), calls=%async_computation.1 | async-start | bytes 1048576 | tf_op jit(solution)/shard_map/all_to_all | solution.py:45
  72.9 2.3 %copy-done.1 = bf16[3584,640,1]{1,0,2:T(8,128)(2,1)S(1)} copy-done((bf16[3584,640,1]{1,0,2:T(8,128)(2,1)S(1)}, bf16[3584,640,1]{1,0,2:T(8,128)(2,1)}, u32[]{:S(2)}) %copy-start.1) | copy-done | bytes 4587544
  75.7 9.1 %all-to-all-done.1.msg_ref = f32[32,16,256]{2,1,0:T(8,128)S(1)} async-done(((f32[32,16,256]{2,1,0:T(8,128)}), f32[32,16,256]{2,1,0:T(8,128)S(1)}, u32[]{:S(2)}, u32[]{:S(2)}) %all-to-all-start.1) | async-done | bytes 524320 | tf_op jit(solution)/shard_map/all_to_all | solution.py:45
  84.7 4.3 %shard_map.70 = (bf16[64,3584]{1,0:T(8,128)(2,1)S(1)}, bf16[64,3584]{1,0:T(8,128)(2,1)S(1)}, bf16[64,3584]{1,0:T(8,128)(2,1)S(1)}, bf16[64,3584]{1,0:T(8,128)(2,1)S(1)}) custom-call(s32[3]{0:T(128)S(1)} %pad_add_fusion.slot_ref, s32[128,256]{1,0:T(8,128)S(1)} %copy-done.2, f32[640,256]{1,0:T(8,128)S(1)} %get-tuple-element.30.logit_ref, ...), custom_call_target="tpu_custom_call" | custom-call | tf_op jit(solution)/shard_map/pallas_call | solution.py:455
  90.1 1.8 %collective-permute-start.14 = (bf16[64,3584]{1,0:T(8,128)(2,1)S(1)}, bf16[64,3584]{1,0:T(8,128)(2,1)S(1)}, u32[]{:S(2)}, u32[]{:S(2)}) collective-permute-start(bf16[64,3584]{1,0:T(8,128)(2,1)S(1)} %get-tuple-element.42), channel_id=1, source_target_pairs={{0,3},{4,7},{8,11},{12,15},{16,19},{20,23},{24,27},{28,31},{32,35}... | collective-permute-start | bytes 1376264 | tf_op jit(solution)/shard_map/ppermute | solution.py:77
  91.9 6.1 %collective-permute-done.12 = bf16[64,3584]{1,0:T(8,128)(2,1)S(1)} collective-permute-done((bf16[64,3584]{1,0:T(8,128)(2,1)S(1)}, bf16[64,3584]{1,0:T(8,128)(2,1)S(1)}, u32[]{:S(2)}, u32[]{:S(2)}) %collective-permute-start.12) | collective-permute-done | bytes 458784 | tf_op jit(solution)/shard_map/ppermute | solution.py:77
  98.0 4.9 %collective-permute-done.13 = bf16[64,3584]{1,0:T(8,128)(2,1)S(1)} collective-permute-done((bf16[64,3584]{1,0:T(8,128)(2,1)S(1)}, bf16[64,3584]{1,0:T(8,128)(2,1)S(1)}, u32[]{:S(2)}, u32[]{:S(2)}) %collective-permute-start.13) | collective-permute-done | bytes 458784 | tf_op jit(solution)/shard_map/ppermute | solution.py:77
  103.4 18.5 %all_to_all.23 = bf16[32,2,3584]{2,1,0:T(2,128)(2,1)S(1)} all-to-all(bf16[32,2,3584]{2,1,0:T(2,128)(2,1)S(1)} %all_to_all.18), channel_id=1, replica_groups={{0,4,8,12,16,20,24,28,32,36,40,44,48,52,56,60,64,68,72,76,80,84,88,92,9..., dimensions={0} | all-to-all | bytes 917504 | tf_op jit(solution)/shard_map/all_to_all | solution.py:45
  122.2 8.1 %collective-permute-start.15 = (bf16[2,3584]{1,0:T(2,128)(2,1)S(1)}, bf16[2,3584]{1,0:T(2,128)(2,1)S(1)}, u32[]{:S(2)}, u32[]{:S(2)}) collective-permute-start(bf16[2,3584]{1,0:T(2,128)(2,1)S(1)} %reduce_sum.12), channel_id=1, source_target_pairs={{0,0},{4,4},{8,8},{12,12},{16,16},{20,20},{24,24},{28,28},{32,32},... | collective-permute-start | bytes 43016 | tf_op jit(solution)/shard_map/ppermute | solution.py:529
  (42 shorter events, 12.0 us)
Async XLA Ops:
  0.0 10.6 %copy-start = (s32[512,128]{1,0:T(8,128)S(1)}, s32[512,128]{1,0:T(8,128)}, u32[]{:S(2)}) copy-start(s32[512,128]{1,0:T(8,128)} %param.10) | copy-start | bytes 786436
  1.6 19.8 %all-to-all-start = ((bf16[8,2,8704]{2,1,0:T(2,128)(2,1)}), bf16[8,2,8704]{2,1,0:T(2,128)(2,1)S(1)}, u32[]{:S(2)}, u32[]{:S(2)}) async-start(bf16[8,2,8704]{2,1,0:T(2,128)(2,1)} %shard_map.64), calls=%async_computation | async-start | bytes 557056 | tf_op jit(solution)/shard_map/all_to_all | solution.py:45
  21.5 7.3 %collective-permute-start = (bf16[16,8704]{1,0:T(8,128)(2,1)S(1)}, bf16[16,8704]{1,0:T(8,128)(2,1)S(1)}, u32[]{:S(2)}, u32[]{:S(2)}) collective-permute-start(bf16[16,8704]{1,0:T(8,128)(2,1)S(1)} %all_to_all.16), channel_id=1, source_target_pairs={{0,64},{4,68},{8,72},{12,76},{16,80},{20,84},{24,88},{28,92},{32,9... | collective-permute-start | bytes 835592 | tf_op jit(solution)/shard_map/ppermute | solution.py:77
  24.3 7.3 %collective-permute-start.2 = (bf16[16,8704]{1,0:T(8,128)(2,1)S(1)}, bf16[16,8704]{1,0:T(8,128)(2,1)S(1)}, u32[]{:S(2)}, u32[]{:S(2)}) collective-permute-start(bf16[16,8704]{1,0:T(8,128)(2,1)S(1)} %all_to_all.16), channel_id=1, source_target_pairs={{0,96},{4,100},{8,104},{12,108},{16,112},{20,116},{24,120},{28,124... | collective-permute-start | bytes 835592 | tf_op jit(solution)/shard_map/ppermute | solution.py:77
  25.2 9.6 %collective-permute-start.1 = (bf16[16,8704]{1,0:T(8,128)(2,1)S(1)}, bf16[16,8704]{1,0:T(8,128)(2,1)S(1)}, u32[]{:S(2)}, u32[]{:S(2)}) collective-permute-start(bf16[16,8704]{1,0:T(8,128)(2,1)S(1)} %all_to_all.16), channel_id=1, source_target_pairs={{0,32},{4,36},{8,40},{12,44},{16,48},{20,52},{24,56},{28,60},{32,6... | collective-permute-start | bytes 835592 | tf_op jit(solution)/shard_map/ppermute | solution.py:77
  31.7 9.6 %collective-permute-start.3 = (bf16[32,8704]{1,0:T(8,128)(2,1)S(1)}, bf16[32,8704]{1,0:T(8,128)(2,1)S(1)}, u32[]{:S(2)}, u32[]{:S(2)}) collective-permute-start(bf16[32,8704]{1,0:T(8,128)(2,1)S(1)} %constant_dynamic-update-slice_fusion.2.refs_1_), channel_id=1, source_target_pairs={{0,3},{4,7},{8,11},{12,15},{16,19},{20,23},{24,27},{28,31},{32,35}... | collective-permute-start | bytes 1671176 | tf_op jit(solution)/shard_map/ppermute | solution.py:77
  34.8 10.1 %collective-permute-start.4 = (bf16[32,8704]{1,0:T(8,128)(2,1)S(1)}, bf16[32,8704]{1,0:T(8,128)(2,1)}, u32[]{:S(2)}, u32[]{:S(2)}) collective-permute-start(bf16[32,8704]{1,0:T(8,128)(2,1)S(1)} %constant_dynamic-update-slice_fusion.refs_0_), channel_id=1, source_target_pairs={{0,1},{4,5},{8,9},{12,13},{16,17},{20,21},{24,25},{28,29},{32,33},... | collective-permute-start | bytes 1671176 | tf_op jit(solution)/shard_map/ppermute | solution.py:77
  34.9 19.5 %collective-permute-start.8 = (bf16[32,8704]{1,0:T(8,128)(2,1)S(1)}, bf16[32,8704]{1,0:T(8,128)(2,1)S(1)}, u32[]{:S(2)}, u32[]{:S(2)}) collective-permute-start(bf16[32,8704]{1,0:T(8,128)(2,1)S(1)} %constant_dynamic-update-slice_fusion.2.refs_1_), channel_id=1, source_target_pairs={{0,1},{4,5},{8,9},{12,13},{16,17},{20,21},{24,25},{28,29},{32,33},... | collective-permute-start | bytes 1671176 | tf_op jit(solution)/shard_map/ppermute | solution.py:77
  35.0 19.4 %collective-permute-start.5 = (bf16[32,8704]{1,0:T(8,128)(2,1)S(1)}, bf16[32,8704]{1,0:T(8,128)(2,1)S(1)}, u32[]{:S(2)}, u32[]{:S(2)}) collective-permute-start(bf16[32,8704]{1,0:T(8,128)(2,1)S(1)} %constant_dynamic-update-slice_fusion.refs_0_), channel_id=1, source_target_pairs={{0,3},{4,7},{8,11},{12,15},{16,19},{20,23},{24,27},{28,31},{32,35}... | collective-permute-start | bytes 1671176 | tf_op jit(solution)/shard_map/ppermute | solution.py:77
  41.2 13.1 %collective-permute-start.7 = (bf16[32,8704]{1,0:T(8,128)(2,1)S(1)}, bf16[32,8704]{1,0:T(8,128)(2,1)}, u32[]{:S(2)}, u32[]{:S(2)}) collective-permute-start(bf16[32,8704]{1,0:T(8,128)(2,1)S(1)} %collective-permute-done.3.refs_2_), channel_id=1, source_target_pairs={{0,3},{4,7},{8,11},{12,15},{16,19},{20,23},{24,27},{28,31},{32,35}... | collective-permute-start | bytes 1671176 | tf_op jit(solution)/shard_map/ppermute | solution.py:77
  44.9 11.9 %collective-permute-start.6 = (bf16[32,8704]{1,0:T(8,128)(2,1)}, bf16[32,8704]{1,0:T(8,128)(2,1)}, u32[]{:S(2)}, u32[]{:S(2)}) collective-permute-start(bf16[32,8704]{1,0:T(8,128)(2,1)} %collective-permute-done.4.refs_3_), channel_id=1, source_target_pairs={{0,1},{4,5},{8,9},{12,13},{16,17},{20,21},{24,25},{28,29},{32,33},... | collective-permute-start | bytes 1671176 | tf_op jit(solution)/shard_map/ppermute | solution.py:77
  45.6 11.2 %copy-start.2 = (s32[128,256]{1,0:T(8,128)S(1)}, s32[128,256]{1,0:T(8,128)}, u32[]{:S(2)}) copy-start(s32[128,256]{1,0:T(8,128)} %shard_map.65.refs_4_.word_ref) | copy-start | bytes 393220
  56.8 16.1 %copy-start.3 = (bf16[2,256,256]{2,1,0:T(8,128)(2,1)S(1)}, bf16[2,256,256]{2,1,0:T(8,128)(2,1)}, u32[]{:S(2)}) copy-start(bf16[2,256,256]{2,1,0:T(8,128)(2,1)} %constant.50.clone) | copy-start | bytes 786436
  60.8 5.0 %collective-permute-start.10 = (f32[72,256]{1,0:T(8,128)S(1)}, f32[72,256]{1,0:T(8,128)S(1)}, u32[]{:S(2)}, u32[]{:S(2)}) collective-permute-start(f32[72,256]{1,0:T(8,128)S(1)} %get-tuple-element.33), channel_id=1, source_target_pairs={{0,2},{4,6},{8,10},{12,14},{16,18},{20,22},{24,26},{28,30},{32,34}... | collective-permute-start | bytes 221192 | tf_op jit(solution)/shard_map/ppermute | solution.py:77
  61.1 4.7 %collective-permute-start.11 = (f32[72,256]{1,0:T(8,128)S(1)}, f32[72,256]{1,0:T(8,128)S(1)}, u32[]{:S(2)}, u32[]{:S(2)}) collective-permute-start(f32[72,256]{1,0:T(8,128)S(1)} %get-tuple-element.34), channel_id=1, source_target_pairs={{0,3},{4,7},{8,11},{12,15},{16,19},{20,23},{24,27},{28,31},{32,35}... | collective-permute-start | bytes 221192 | tf_op jit(solution)/shard_map/ppermute | solution.py:77
  62.3 4.4 %collective-permute-start.9 = (f32[72,256]{1,0:T(8,128)S(1)}, f32[72,256]{1,0:T(8,128)S(1)}, u32[]{:S(2)}, u32[]{:S(2)}) collective-permute-start(f32[72,256]{1,0:T(8,128)S(1)} %get-tuple-element.32), channel_id=1, source_target_pairs={{0,1},{4,5},{8,9},{12,13},{16,17},{20,21},{24,25},{28,29},{32,33},... | collective-permute-start | bytes 221192 | tf_op jit(solution)/shard_map/ppermute | solution.py:77
  67.8 17.0 %all-to-all-start.1 = ((f32[32,16,256]{2,1,0:T(8,128)}), f32[32,16,256]{2,1,0:T(8,128)S(1)}, u32[]{:S(2)}, u32[]{:S(2)}) async-start(f32[32,16,256]{2,1,0:T(8,128)} %shard_map.68), calls=%async_computation.1 | async-start | bytes 1048576 | tf_op jit(solution)/shard_map/all_to_all | solution.py:45
  72.9 2.3 %copy-start.1 = (bf16[3584,640,1]{1,0,2:T(8,128)(2,1)S(1)}, bf16[3584,640,1]{1,0,2:T(8,128)(2,1)}, u32[]{:S(2)}) copy-start(bf16[3584,640,1]{1,0,2:T(8,128)(2,1)} %param.9) | copy-start | bytes 13762564
  89.0 9.0 %collective-permute-start.12 = (bf16[64,3584]{1,0:T(8,128)(2,1)S(1)}, bf16[64,3584]{1,0:T(8,128)(2,1)S(1)}, u32[]{:S(2)}, u32[]{:S(2)}) collective-permute-start(bf16[64,3584]{1,0:T(8,128)(2,1)S(1)} %get-tuple-element.40), channel_id=1, source_target_pairs={{0,2},{4,6},{8,10},{12,14},{16,18},{20,22},{24,26},{28,30},{32,34}... | collective-permute-start | bytes 1376264 | tf_op jit(solution)/shard_map/ppermute | solution.py:77
  89.2 13.8 %collective-permute-start.13 = (bf16[64,3584]{1,0:T(8,128)(2,1)S(1)}, bf16[64,3584]{1,0:T(8,128)(2,1)S(1)}, u32[]{:S(2)}, u32[]{:S(2)}) collective-permute-start(bf16[64,3584]{1,0:T(8,128)(2,1)S(1)} %get-tuple-element.41), channel_id=1, source_target_pairs={{0,1},{4,5},{8,9},{12,13},{16,17},{20,21},{24,25},{28,29},{32,33},... | collective-permute-start | bytes 1376264 | tf_op jit(solution)/shard_map/ppermute | solution.py:77
  90.1 12.9 %collective-permute-start.14 = (bf16[64,3584]{1,0:T(8,128)(2,1)S(1)}, bf16[64,3584]{1,0:T(8,128)(2,1)S(1)}, u32[]{:S(2)}, u32[]{:S(2)}) collective-permute-start(bf16[64,3584]{1,0:T(8,128)(2,1)S(1)} %get-tuple-element.42), channel_id=1, source_target_pairs={{0,3},{4,7},{8,11},{12,15},{16,19},{20,23},{24,27},{28,31},{32,35}... | collective-permute-start | bytes 1376264 | tf_op jit(solution)/shard_map/ppermute | solution.py:77
  122.2 9.5 %collective-permute-start.15 = (bf16[2,3584]{1,0:T(2,128)(2,1)S(1)}, bf16[2,3584]{1,0:T(2,128)(2,1)S(1)}, u32[]{:S(2)}, u32[]{:S(2)}) collective-permute-start(bf16[2,3584]{1,0:T(2,128)(2,1)S(1)} %reduce_sum.12), channel_id=1, source_target_pairs={{0,0},{4,4},{8,8},{12,12},{16,16},{20,20},{24,24},{28,28},{32,32},... | collective-permute-start | bytes 43016 | tf_op jit(solution)/shard_map/ppermute | solution.py:529

commit v10 on v9

--- a/solution.py
+++ b/solution.py
@@ -488,7 +488,7 @@
     ).reshape(picks, 2 * shards)
     words = tile_words(tiles_t)
     last, after, opposite = across(gathered, 1), across(gathered, -1), across(gathered, 2)
-    opposite, words = lax.optimization_barrier((opposite, words))
+    gathered, words = lax.optimization_barrier((gathered, words))
     own = (
         jnp.concatenate((gathered, last), axis=0),
         jnp.concatenate((after, opposite), axis=0),

time: 133 us -> 135 us (1.015)
  starting transfers between devices: 40.3 us -> 48.2 us
  waiting for transfers between devices: 43.1 us -> 39.9 us
  blocking collectives: 18.5 us -> 15.9 us
    ppermute x1, starting transfers between devices: 8.1 us -> 14.1 us  [per_device(): return lax.ppermute(summed.astype(jnp.bfloat16), WHOLE, last_hop())]
    ppermute x15, waiting for transfers between devices: 27.4 us -> 24.6 us  [step(): return lax.ppermute(value, WHOLE, pairs)]
    all_to_all x1, blocking collectives: 18.5 us -> 15.9 us  [exchange(): lax.all_to_all(value, WHOLE, 0, 0, tiled=True, axis_index_groups=groups)]
    ppermute x15, starting transfers between devices: 18.1 us -> 20.5 us  [step(): return lax.ppermute(value, WHOLE, pairs)]
where the time goes in v10:
time: 135 us; the launch traced here: 134 us
  starting transfers between devices  48.2 us (36%)
  waiting for transfers between devices  39.9 us (30%)
  Pallas kernels  24.8 us (18%)
  blocking collectives  15.9 us (12%)
  local copies, waits for them, and re-layouts  4.73 us (4%)
    ppermute x15, waiting for transfers between devices, step(): return lax.ppermute(value, WHOLE, pairs)  24.6 us
    ppermute x15, starting transfers between devices, step(): return lax.ppermute(value, WHOLE, pairs)  20.5 us
    all_to_all x1, blocking collectives, exchange(): lax.all_to_all(value, WHOLE, 0, 0, tiled=True, axis_index_groups=groups)  15.9 us
    ppermute x1, starting transfers between devices, per_device(): return lax.ppermute(summed.astype(jnp.bfloat16), WHOLE, last_hop())  14.1 us
    all_to_all x2, waiting for transfers between devices, exchange(): lax.all_to_all(value, WHOLE, 0, 0, tiled=True, axis_index_groups=groups)  13.9 us
    all_to_all x2, starting transfers between devices, exchange(): lax.all_to_all(value, WHOLE, 0, 0, tiled=True, axis_index_groups=groups)  13.5 us
    pallas_call x1, Pallas kernels, early_logits(): pl.pallas_call(kernel, in_specs=[whole] * count + [pl.BlockSpec(memory_sp...  8.69 us
    pallas_call x1, Pallas kernels, tile_words(): pl.pallas_call(kernel, out_shape=jax.ShapeDtypeStruct((count, rows), jnp....  4.71 us
  transfers between devices with their start and end apart: 18, of which 12 were waited for; matrix products, arithmetic and copies ran while one was open for 1% of the time, Pallas kernels for 10%

profile of v10, /device:TPU:1, one launch (start us, length us, event | category | flops | bytes accessed | tf_op | source)
XLA Modules:
  0.0 134.4 jit_solution(17366294181838645361)
XLA Ops:
  0.0 1.6 %shard_map.64 = bf16[8,2,8704]{2,1,0:T(2,128)(2,1)} custom-call(s32[1]{0:T(128)} %bitcast.2.core_ref, bf16[4,5120]{1,0:T(4,128)(2,1)} %t_ref.1, bf16[4,3584]{1,0:T(4,128)(2,1)} %s_ref.1), custom_call_target="tpu_custom_call" | custom-call | tf_op jit(solution)/shard_map/pallas_call | solution.py:59
  1.6 9.0 %all-to-all-start = ((bf16[8,2,8704]{2,1,0:T(2,128)(2,1)}), bf16[8,2,8704]{2,1,0:T(2,128)(2,1)S(1)}, u32[]{:S(2)}, u32[]{:S(2)}) async-start(bf16[8,2,8704]{2,1,0:T(2,128)(2,1)} %shard_map.64), calls=%async_computation | async-start | bytes 557056 | tf_op jit(solution)/shard_map/all_to_all | solution.py:45
  11.4 4.7 %shard_map.65.refs_4_.word_ref = s32[128,256]{1,0:T(8,128)} custom-call(s32[128,256]{1,0:T(8,128)} %copy.11.tiles_ref), custom_call_target="tpu_custom_call" | custom-call | flops 67108864 | bytes 262144 | tf_op jit(solution)/shard_map/pallas_call | solution.py:133
  16.1 5.3 %all-to-all-done = bf16[8,2,8704]{2,1,0:T(2,128)(2,1)S(1)} async-done(((bf16[8,2,8704]{2,1,0:T(2,128)(2,1)}), bf16[8,2,8704]{2,1,0:T(2,128)(2,1)S(1)}, u32[]{:S(2)}, u32[]{:S(2)}) %all-to-all-start) | async-done | bytes 278560 | tf_op jit(solution)/shard_map/all_to_all | solution.py:45
  22.8 1.5 %collective-permute-start.1 = (bf16[16,8704]{1,0:T(8,128)(2,1)S(1)}, bf16[16,8704]{1,0:T(8,128)(2,1)S(1)}, u32[]{:S(2)}, u32[]{:S(2)}) collective-permute-start(bf16[16,8704]{1,0:T(8,128)(2,1)S(1)} %all_to_all.16), channel_id=1, source_target_pairs={{0,96},{4,100},{8,104},{12,108},{16,112},{20,116},{24,120},{28,124... | collective-permute-start | bytes 835592 | tf_op jit(solution)/shard_map/ppermute | solution.py:77
  24.2 1.5 %collective-permute-start.2 = (bf16[16,8704]{1,0:T(8,128)(2,1)S(1)}, bf16[16,8704]{1,0:T(8,128)(2,1)S(1)}, u32[]{:S(2)}, u32[]{:S(2)}) collective-permute-start(bf16[16,8704]{1,0:T(8,128)(2,1)S(1)} %all_to_all.16), channel_id=1, source_target_pairs={{0,64},{4,68},{8,72},{12,76},{16,80},{20,84},{24,88},{28,92},{32,9... | collective-permute-start | bytes 835592 | tf_op jit(solution)/shard_map/ppermute | solution.py:77
  25.8 2.7 %collective-permute-done = bf16[16,8704]{1,0:T(8,128)(2,1)S(1)} collective-permute-done((bf16[16,8704]{1,0:T(8,128)(2,1)S(1)}, bf16[16,8704]{1,0:T(8,128)(2,1)S(1)}, u32[]{:S(2)}, u32[]{:S(2)}) %collective-permute-start) | collective-permute-done | bytes 278560 | tf_op jit(solution)/shard_map/ppermute | solution.py:77
  29.6 2.5 %collective-permute-done.2 = bf16[16,8704]{1,0:T(8,128)(2,1)S(1)} collective-permute-done((bf16[16,8704]{1,0:T(8,128)(2,1)S(1)}, bf16[16,8704]{1,0:T(8,128)(2,1)S(1)}, u32[]{:S(2)}, u32[]{:S(2)}) %collective-permute-start.2) | collective-permute-done | bytes 278560 | tf_op jit(solution)/shard_map/ppermute | solution.py:77
  32.2 3.1 %collective-permute-start.3 = (bf16[32,8704]{1,0:T(8,128)(2,1)S(1)}, bf16[32,8704]{1,0:T(8,128)(2,1)}, u32[]{:S(2)}, u32[]{:S(2)}) collective-permute-start(bf16[32,8704]{1,0:T(8,128)(2,1)S(1)} %constant_dynamic-update-slice_fusion.2.refs_1_), channel_id=1, source_target_pairs={{0,3},{4,7},{8,11},{12,15},{16,19},{20,23},{24,27},{28,31},{32,35}... | collective-permute-start | bytes 1671176 | tf_op jit(solution)/shard_map/ppermute | solution.py:77
  36.7 4.7 %collective-permute-done.4.refs_3_ = bf16[32,8704]{1,0:T(8,128)(2,1)S(1)} collective-permute-done((bf16[32,8704]{1,0:T(8,128)(2,1)S(1)}, bf16[32,8704]{1,0:T(8,128)(2,1)S(1)}, u32[]{:S(2)}, u32[]{:S(2)}) %collective-permute-start.4) | collective-permute-done | bytes 557088 | tf_op jit(solution)/shard_map/ppermute | solution.py:77
  41.8 3.2 %collective-permute-start.7 = (bf16[32,8704]{1,0:T(8,128)(2,1)}, bf16[32,8704]{1,0:T(8,128)(2,1)}, u32[]{:S(2)}, u32[]{:S(2)}) collective-permute-start(bf16[32,8704]{1,0:T(8,128)(2,1)} %collective-permute-done.3.refs_2_), channel_id=1, source_target_pairs={{0,3},{4,7},{8,11},{12,15},{16,19},{20,23},{24,27},{28,31},{32,35}... | collective-permute-start | bytes 1671176 | tf_op jit(solution)/shard_map/ppermute | solution.py:77
  45.8 8.7 %shard_map.66 = (f32[128,1280]{1,0:T(8,128)S(1)}, bf16[2560,640]{1,0:T(8,128)(2,1)S(1)}, bf16[2560,640]{1,0:T(8,128)(2,1)S(1)}, bf16[3584,640]{1,0:T(8,128)(2,1)S(1)}) custom-call(bf16[32,8704]{1,0:T(8,128)(2,1)S(1)} %constant_dynamic-update-slice_fusion.refs_0_, bf16[32,8704]{1,0:T(8,128)(2,1)S(1)} %constant_dynamic-update-slice_fusion.2.refs_1_, ...), custom_call_target="tpu_custom_call" | custom-call | flops 1426063360 | bytes 11141120 | tf_op jit(solution)/shard_map/pallas_call | solution.py:201
  54.5 4.0 %shard_map.67 = (f32[72,256]{1,0:T(8,128)S(1)}, f32[72,256]{1,0:T(8,128)S(1)}, f32[72,256]{1,0:T(8,128)S(1)}, f32[72,256]{1,0:T(8,128)S(1)}, f32[640,256]{1,0:T(8,128)S(1)}) custom-call(s32[3]{0:T(128)S(1)} %pad_add_fusion.slot_ref, f32[128,1280]{1,0:T(8,128)S(1)} %get-tuple-element.26.early_ref, bf16[32,8704]{1,0:T(8,128)(2,1)S(1)} %collective-permute-done.5.refs_0_, ...), custom_call_target="tpu_custom_call" | custom-call | flops 1426063360 | bytes 11141120 | tf_op jit(solution)/shard_map/pallas_call | solution.py:291
  58.6 1.6 %collective-permute-start.10 = (f32[72,256]{1,0:T(8,128)S(1)}, f32[72,256]{1,0:T(8,128)S(1)}, u32[]{:S(2)}, u32[]{:S(2)}) collective-permute-start(f32[72,256]{1,0:T(8,128)S(1)} %get-tuple-element.33), channel_id=1, source_target_pairs={{0,2},{4,6},{8,10},{12,14},{16,18},{20,22},{24,26},{28,30},{32,34}... | collective-permute-start | bytes 221192 | tf_op jit(solution)/shard_map/ppermute | solution.py:77
  62.1 1.4 %collective-permute-done.10.refs_2_ = f32[72,256]{1,0:T(8,128)S(1)} collective-permute-done((f32[72,256]{1,0:T(8,128)S(1)}, f32[72,256]{1,0:T(8,128)S(1)}, u32[]{:S(2)}, u32[]{:S(2)}) %collective-permute-start.10) | collective-permute-done | bytes 73760 | tf_op jit(solution)/shard_map/ppermute | solution.py:77
  67.1 4.5 %all-to-all-start.1 = ((f32[32,16,256]{2,1,0:T(8,128)}), f32[32,16,256]{2,1,0:T(8,128)S(1)}, u32[]{:S(2)}, u32[]{:S(2)}) async-start(f32[32,16,256]{2,1,0:T(8,128)} %shard_map.68), calls=%async_computation.1 | async-start | bytes 1048576 | tf_op jit(solution)/shard_map/all_to_all | solution.py:45
  71.6 2.3 %copy-done.1 = bf16[3584,640,1]{1,0,2:T(8,128)(2,1)S(1)} copy-done((bf16[3584,640,1]{1,0,2:T(8,128)(2,1)S(1)}, bf16[3584,640,1]{1,0,2:T(8,128)(2,1)}, u32[]{:S(2)}) %copy-start.1) | copy-done | bytes 4587544
  74.4 8.6 %all-to-all-done.1.msg_ref = f32[32,16,256]{2,1,0:T(8,128)S(1)} async-done(((f32[32,16,256]{2,1,0:T(8,128)}), f32[32,16,256]{2,1,0:T(8,128)S(1)}, u32[]{:S(2)}, u32[]{:S(2)}) %all-to-all-start.1) | async-done | bytes 524320 | tf_op jit(solution)/shard_map/all_to_all | solution.py:45
  83.0 4.3 %shard_map.70 = (bf16[64,3584]{1,0:T(8,128)(2,1)S(1)}, bf16[64,3584]{1,0:T(8,128)(2,1)S(1)}, bf16[64,3584]{1,0:T(8,128)(2,1)S(1)}, bf16[64,3584]{1,0:T(8,128)(2,1)S(1)}) custom-call(s32[3]{0:T(128)S(1)} %pad_add_fusion.slot_ref, s32[128,256]{1,0:T(8,128)S(1)} %copy-done.2, f32[640,256]{1,0:T(8,128)S(1)} %get-tuple-element.30.logit_ref, ...), custom_call_target="tpu_custom_call" | custom-call | tf_op jit(solution)/shard_map/pallas_call | solution.py:455
  88.7 2.4 %collective-permute-start.14 = (bf16[64,3584]{1,0:T(8,128)(2,1)S(1)}, bf16[64,3584]{1,0:T(8,128)(2,1)S(1)}, u32[]{:S(2)}, u32[]{:S(2)}) collective-permute-start(bf16[64,3584]{1,0:T(8,128)(2,1)S(1)} %get-tuple-element.42), channel_id=1, source_target_pairs={{0,3},{4,7},{8,11},{12,15},{16,19},{20,23},{24,27},{28,31},{32,35}... | collective-permute-start | bytes 1376264 | tf_op jit(solution)/shard_map/ppermute | solution.py:77
  91.1 5.3 %collective-permute-done.12 = bf16[64,3584]{1,0:T(8,128)(2,1)S(1)} collective-permute-done((bf16[64,3584]{1,0:T(8,128)(2,1)S(1)}, bf16[64,3584]{1,0:T(8,128)(2,1)S(1)}, u32[]{:S(2)}, u32[]{:S(2)}) %collective-permute-start.12) | collective-permute-done | bytes 458784 | tf_op jit(solution)/shard_map/ppermute | solution.py:77
  96.4 5.1 %collective-permute-done.13 = bf16[64,3584]{1,0:T(8,128)(2,1)S(1)} collective-permute-done((bf16[64,3584]{1,0:T(8,128)(2,1)S(1)}, bf16[64,3584]{1,0:T(8,128)(2,1)S(1)}, u32[]{:S(2)}, u32[]{:S(2)}) %collective-permute-start.13) | collective-permute-done | bytes 458784 | tf_op jit(solution)/shard_map/ppermute | solution.py:77
  102.0 15.9 %all_to_all.23 = bf16[32,2,3584]{2,1,0:T(2,128)(2,1)S(1)} all-to-all(bf16[32,2,3584]{2,1,0:T(2,128)(2,1)S(1)} %all_to_all.18), channel_id=1, replica_groups={{0,4,8,12,16,20,24,28,32,36,40,44,48,52,56,60,64,68,72,76,80,84,88,92,9..., dimensions={0} | all-to-all | bytes 917504 | tf_op jit(solution)/shard_map/all_to_all | solution.py:45
  118.3 14.1 %collective-permute-start.15 = (bf16[2,3584]{1,0:T(2,128)(2,1)S(1)}, bf16[2,3584]{1,0:T(2,128)(2,1)S(1)}, u32[]{:S(2)}, u32[]{:S(2)}) collective-permute-start(bf16[2,3584]{1,0:T(2,128)(2,1)S(1)} %reduce_sum.12), channel_id=1, source_target_pairs={{0,0},{4,4},{8,8},{12,12},{16,16},{20,20},{24,24},{28,28},{32,32},... | collective-permute-start | bytes 43016 | tf_op jit(solution)/shard_map/ppermute | solution.py:529
  (42 shorter events, 16.0 us)
Async XLA Ops:
  0.0 10.6 %copy-start = (s32[512,128]{1,0:T(8,128)S(1)}, s32[512,128]{1,0:T(8,128)}, u32[]{:S(2)}) copy-start(s32[512,128]{1,0:T(8,128)} %param.10) | copy-start | bytes 786436
  1.6 19.8 %all-to-all-start = ((bf16[8,2,8704]{2,1,0:T(2,128)(2,1)}), bf16[8,2,8704]{2,1,0:T(2,128)(2,1)S(1)}, u32[]{:S(2)}, u32[]{:S(2)}) async-start(bf16[8,2,8704]{2,1,0:T(2,128)(2,1)} %shard_map.64), calls=%async_computation | async-start | bytes 557056 | tf_op jit(solution)/shard_map/all_to_all | solution.py:45
  21.5 7.0 %collective-permute-start = (bf16[16,8704]{1,0:T(8,128)(2,1)S(1)}, bf16[16,8704]{1,0:T(8,128)(2,1)S(1)}, u32[]{:S(2)}, u32[]{:S(2)}) collective-permute-start(bf16[16,8704]{1,0:T(8,128)(2,1)S(1)} %all_to_all.16), channel_id=1, source_target_pairs={{0,32},{4,36},{8,40},{12,44},{16,48},{20,52},{24,56},{28,60},{32,6... | collective-permute-start | bytes 835592 | tf_op jit(solution)/shard_map/ppermute | solution.py:77
  22.8 6.8 %collective-permute-start.1 = (bf16[16,8704]{1,0:T(8,128)(2,1)S(1)}, bf16[16,8704]{1,0:T(8,128)(2,1)S(1)}, u32[]{:S(2)}, u32[]{:S(2)}) collective-permute-start(bf16[16,8704]{1,0:T(8,128)(2,1)S(1)} %all_to_all.16), channel_id=1, source_target_pairs={{0,96},{4,100},{8,104},{12,108},{16,112},{20,116},{24,120},{28,124... | collective-permute-start | bytes 835592 | tf_op jit(solution)/shard_map/ppermute | solution.py:77
  24.2 7.9 %collective-permute-start.2 = (bf16[16,8704]{1,0:T(8,128)(2,1)S(1)}, bf16[16,8704]{1,0:T(8,128)(2,1)S(1)}, u32[]{:S(2)}, u32[]{:S(2)}) collective-permute-start(bf16[16,8704]{1,0:T(8,128)(2,1)S(1)} %all_to_all.16), channel_id=1, source_target_pairs={{0,64},{4,68},{8,72},{12,76},{16,80},{20,84},{24,88},{28,92},{32,9... | collective-permute-start | bytes 835592 | tf_op jit(solution)/shard_map/ppermute | solution.py:77
  28.5 12.9 %collective-permute-start.4 = (bf16[32,8704]{1,0:T(8,128)(2,1)S(1)}, bf16[32,8704]{1,0:T(8,128)(2,1)S(1)}, u32[]{:S(2)}, u32[]{:S(2)}) collective-permute-start(bf16[32,8704]{1,0:T(8,128)(2,1)S(1)} %constant_dynamic-update-slice_fusion.refs_0_), channel_id=1, source_target_pairs={{0,1},{4,5},{8,9},{12,13},{16,17},{20,21},{24,25},{28,29},{32,33},... | collective-permute-start | bytes 1671176 | tf_op jit(solution)/shard_map/ppermute | solution.py:77
  32.2 9.6 %collective-permute-start.3 = (bf16[32,8704]{1,0:T(8,128)(2,1)S(1)}, bf16[32,8704]{1,0:T(8,128)(2,1)}, u32[]{:S(2)}, u32[]{:S(2)}) collective-permute-start(bf16[32,8704]{1,0:T(8,128)(2,1)S(1)} %constant_dynamic-update-slice_fusion.2.refs_1_), channel_id=1, source_target_pairs={{0,3},{4,7},{8,11},{12,15},{16,19},{20,23},{24,27},{28,31},{32,35}... | collective-permute-start | bytes 1671176 | tf_op jit(solution)/shard_map/ppermute | solution.py:77
  35.3 19.2 %collective-permute-start.5 = (bf16[32,8704]{1,0:T(8,128)(2,1)S(1)}, bf16[32,8704]{1,0:T(8,128)(2,1)S(1)}, u32[]{:S(2)}, u32[]{:S(2)}) collective-permute-start(bf16[32,8704]{1,0:T(8,128)(2,1)S(1)} %constant_dynamic-update-slice_fusion.refs_0_), channel_id=1, source_target_pairs={{0,3},{4,7},{8,11},{12,15},{16,19},{20,23},{24,27},{28,31},{32,35}... | collective-permute-start | bytes 1671176 | tf_op jit(solution)/shard_map/ppermute | solution.py:77
  35.4 19.0 %collective-permute-start.8 = (bf16[32,8704]{1,0:T(8,128)(2,1)S(1)}, bf16[32,8704]{1,0:T(8,128)(2,1)S(1)}, u32[]{:S(2)}, u32[]{:S(2)}) collective-permute-start(bf16[32,8704]{1,0:T(8,128)(2,1)S(1)} %constant_dynamic-update-slice_fusion.2.refs_1_), channel_id=1, source_target_pairs={{0,1},{4,5},{8,9},{12,13},{16,17},{20,21},{24,25},{28,29},{32,33},... | collective-permute-start | bytes 1671176 | tf_op jit(solution)/shard_map/ppermute | solution.py:77
  41.4 13.0 %collective-permute-start.6 = (bf16[32,8704]{1,0:T(8,128)(2,1)S(1)}, bf16[32,8704]{1,0:T(8,128)(2,1)}, u32[]{:S(2)}, u32[]{:S(2)}) collective-permute-start(bf16[32,8704]{1,0:T(8,128)(2,1)S(1)} %collective-permute-done.4.refs_3_), channel_id=1, source_target_pairs={{0,1},{4,5},{8,9},{12,13},{16,17},{20,21},{24,25},{28,29},{32,33},... | collective-permute-start | bytes 1671176 | tf_op jit(solution)/shard_map/ppermute | solution.py:77
  41.8 12.7 %collective-permute-start.7 = (bf16[32,8704]{1,0:T(8,128)(2,1)}, bf16[32,8704]{1,0:T(8,128)(2,1)}, u32[]{:S(2)}, u32[]{:S(2)}) collective-permute-start(bf16[32,8704]{1,0:T(8,128)(2,1)} %collective-permute-done.3.refs_2_), channel_id=1, source_target_pairs={{0,3},{4,7},{8,11},{12,15},{16,19},{20,23},{24,27},{28,31},{32,35}... | collective-permute-start | bytes 1671176 | tf_op jit(solution)/shard_map/ppermute | solution.py:77
  45.8 8.7 %copy-start.2 = (s32[128,256]{1,0:T(8,128)S(1)}, s32[128,256]{1,0:T(8,128)}, u32[]{:S(2)}) copy-start(s32[128,256]{1,0:T(8,128)} %shard_map.65.refs_4_.word_ref) | copy-start | bytes 393220
  54.5 17.1 %copy-start.3 = (bf16[2,256,256]{2,1,0:T(8,128)(2,1)S(1)}, bf16[2,256,256]{2,1,0:T(8,128)(2,1)}, u32[]{:S(2)}) copy-start(bf16[2,256,256]{2,1,0:T(8,128)(2,1)} %constant.50.clone) | copy-start | bytes 786436
  58.6 5.0 %collective-permute-start.10 = (f32[72,256]{1,0:T(8,128)S(1)}, f32[72,256]{1,0:T(8,128)S(1)}, u32[]{:S(2)}, u32[]{:S(2)}) collective-permute-start(f32[72,256]{1,0:T(8,128)S(1)} %get-tuple-element.33), channel_id=1, source_target_pairs={{0,2},{4,6},{8,10},{12,14},{16,18},{20,22},{24,26},{28,30},{32,34}... | collective-permute-start | bytes 221192 | tf_op jit(solution)/shard_map/ppermute | solution.py:77
  60.2 4.4 %collective-permute-start.11 = (f32[72,256]{1,0:T(8,128)S(1)}, f32[72,256]{1,0:T(8,128)S(1)}, u32[]{:S(2)}, u32[]{:S(2)}) collective-permute-start(f32[72,256]{1,0:T(8,128)S(1)} %get-tuple-element.34), channel_id=1, source_target_pairs={{0,3},{4,7},{8,11},{12,15},{16,19},{20,23},{24,27},{28,31},{32,35}... | collective-permute-start | bytes 221192 | tf_op jit(solution)/shard_map/ppermute | solution.py:77
  61.6 4.4 %collective-permute-start.9 = (f32[72,256]{1,0:T(8,128)S(1)}, f32[72,256]{1,0:T(8,128)S(1)}, u32[]{:S(2)}, u32[]{:S(2)}) collective-permute-start(f32[72,256]{1,0:T(8,128)S(1)} %get-tuple-element.32), channel_id=1, source_target_pairs={{0,1},{4,5},{8,9},{12,13},{16,17},{20,21},{24,25},{28,29},{32,33},... | collective-permute-start | bytes 221192 | tf_op jit(solution)/shard_map/ppermute | solution.py:77
  67.1 15.9 %all-to-all-start.1 = ((f32[32,16,256]{2,1,0:T(8,128)}), f32[32,16,256]{2,1,0:T(8,128)S(1)}, u32[]{:S(2)}, u32[]{:S(2)}) async-start(f32[32,16,256]{2,1,0:T(8,128)} %shard_map.68), calls=%async_computation.1 | async-start | bytes 1048576 | tf_op jit(solution)/shard_map/all_to_all | solution.py:45
  71.6 2.3 %copy-start.1 = (bf16[3584,640,1]{1,0,2:T(8,128)(2,1)S(1)}, bf16[3584,640,1]{1,0,2:T(8,128)(2,1)}, u32[]{:S(2)}) copy-start(bf16[3584,640,1]{1,0,2:T(8,128)(2,1)} %param.9) | copy-start | bytes 13762564
  87.3 9.2 %collective-permute-start.12 = (bf16[64,3584]{1,0:T(8,128)(2,1)S(1)}, bf16[64,3584]{1,0:T(8,128)(2,1)S(1)}, u32[]{:S(2)}, u32[]{:S(2)}) collective-permute-start(bf16[64,3584]{1,0:T(8,128)(2,1)S(1)} %get-tuple-element.40), channel_id=1, source_target_pairs={{0,2},{4,6},{8,10},{12,14},{16,18},{20,22},{24,26},{28,30},{32,34}... | collective-permute-start | bytes 1376264 | tf_op jit(solution)/shard_map/ppermute | solution.py:77
  88.4 13.1 %collective-permute-start.13 = (bf16[64,3584]{1,0:T(8,128)(2,1)S(1)}, bf16[64,3584]{1,0:T(8,128)(2,1)S(1)}, u32[]{:S(2)}, u32[]{:S(2)}) collective-permute-start(bf16[64,3584]{1,0:T(8,128)(2,1)S(1)} %get-tuple-element.41), channel_id=1, source_target_pairs={{0,1},{4,5},{8,9},{12,13},{16,17},{20,21},{24,25},{28,29},{32,33},... | collective-permute-start | bytes 1376264 | tf_op jit(solution)/shard_map/ppermute | solution.py:77
  88.7 12.8 %collective-permute-start.14 = (bf16[64,3584]{1,0:T(8,128)(2,1)S(1)}, bf16[64,3584]{1,0:T(8,128)(2,1)S(1)}, u32[]{:S(2)}, u32[]{:S(2)}) collective-permute-start(bf16[64,3584]{1,0:T(8,128)(2,1)S(1)} %get-tuple-element.42), channel_id=1, source_target_pairs={{0,3},{4,7},{8,11},{12,15},{16,19},{20,23},{24,27},{28,31},{32,35}... | collective-permute-start | bytes 1376264 | tf_op jit(solution)/shard_map/ppermute | solution.py:77
  118.3 15.5 %collective-permute-start.15 = (bf16[2,3584]{1,0:T(2,128)(2,1)S(1)}, bf16[2,3584]{1,0:T(2,128)(2,1)S(1)}, u32[]{:S(2)}, u32[]{:S(2)}) collective-permute-start(bf16[2,3584]{1,0:T(2,128)(2,1)S(1)} %reduce_sum.12), channel_id=1, source_target_pairs={{0,0},{4,4},{8,8},{12,12},{16,16},{20,20},{24,24},{28,28},{32,32},... | collective-permute-start | bytes 43016 | tf_op jit(solution)/shard_map/ppermute | solution.py:529
